TPU v7x, 512 devices: a whole 4x4x16 slice. The times are simulated.
512 devices in a mesh: head: 16 (over x, y), seq: 32 (over z, core).
Axes of the slice: x: 4, y: 4, z: 16, core: 2. Of those that a mesh axis runs over, the one named last changes fastest.
Arguments:
- q_latent: bfloat16 [4096, 128, 512], P('seq', 'head'), may hold values from -14 to 14
- q_rope: bfloat16 [4096, 128, 64], P('seq', 'head'), may hold values from -4 to 4
- latent_cache: bfloat16 [16384, 512], P('seq'), may hold values from -4 to 4
- rope_keys: bfloat16 [16384, 64], P('seq'), may hold values from -4 to 4
- index_queries: bfloat16 [4096, 64, 128], P('seq', 'head'), may hold values from -6 to 6
- index_weights: float32 [4096, 64], P('seq', 'head'), may hold values from 0.05 to 0.4
- index_keys: bfloat16 [16384, 128], P('seq'), may hold values from -4 to 4
- sel_blocks: int32 [32, 16], replicated, may hold values from -1 to 127, as said below
Outputs:
- grad_index_queries: float32 [4096, 64, 128], P('seq', 'head')
- grad_index_weights: float32 [4096, 64], P('seq', 'head')
- grad_index_keys: float32 [16384, 128], P('seq')
Inputs may be any that keep to these rules, and one draw needn't show every extreme that they name: `sel_blocks`: entry 0 of row d is 4 * d + 3. The other entries are distinct blocks no later than entry 0, never entry 0 itself, at most one of them from the key blocks 4 * e to 4 * e + 3 of any one e, followed by -1 entries; row d has exactly min(16, d + 2) entries that are not -1.
All inputs are finite; a program needn't handle non-finite values.
Results may differ from a plain program's by a relative error of at most 0.008.
Values may be sent and summed in bfloat16 or wider, within the bound.
No kernel may reach another device: no remote copies, remote signals or barrier semaphores. Data moves between devices by JAX's collectives and lax.ppermute only.
A program may use at most 64 MiB of HBM per device.

v0:
```python
import math

import jax
import jax.numpy as jnp
from jax import lax
from jax.sharding import PartitionSpec as P

score_scale = 192.0 ** (-0.5)
gelu_coef = math.sqrt(2.0 / math.pi)
cubic_coef = 0.044715


def gelu_pair(values):
    inner = gelu_coef * (values + cubic_coef * values * values * values)
    tangent = jnp.tanh(inner)
    active = 0.5 * values * (1.0 + tangent)
    slope = 0.5 * (1.0 + tangent) + 0.5 * values * (1.0 - tangent * tangent) * gelu_coef * (
        1.0 + 3.0 * cubic_coef * values * values
    )
    return (active, slope)


def head_probs(scores, key_mask):
    full_mask = key_mask[:, None]
    highest = jnp.max(jnp.where(full_mask, scores, -jnp.inf), axis=(2, 3), keepdims=True)
    weights = jnp.where(full_mask, jnp.exp(scores - highest), 0.0)
    return jnp.sum(weights / jnp.sum(weights, axis=(2, 3), keepdims=True), axis=1)


def logit_grad(target, logits, key_mask, loss_weight):
    highest = jnp.max(jnp.where(key_mask, logits, -jnp.inf), axis=(1, 2), keepdims=True)
    weights = jnp.where(key_mask, jnp.exp(logits - highest), 0.0)
    predicted = weights / jnp.sum(weights, axis=(1, 2), keepdims=True)
    return jnp.where(key_mask, loss_weight * (predicted - target), 0.0).astype(jnp.bfloat16)


def body(
    q_latent, q_rope, latent_cache, rope_keys, index_queries, index_weights, index_keys, sel_blocks
):
    seq_count = lax.axis_size("seq")
    head_count = lax.axis_size("head")
    seq_index = lax.axis_index("seq")
    block = q_latent.shape[0]
    slot_count = sel_blocks.shape[1]
    local_blocks = latent_cache.shape[0] // block
    index_width = index_keys.shape[1]
    index_scale = index_width ** (-0.5)
    total_heads = q_latent.shape[1] * head_count
    loss_weight = float(slot_count * block)
    latent_tables = latent_cache.reshape(local_blocks, block, -1)
    rope_tables = rope_keys.reshape(local_blocks, block, -1)
    index_tables = index_keys.reshape(local_blocks, block, -1)
    first_block = seq_index * local_blocks
    later_slots = sel_blocks[:, 1:]
    offsets = later_slots - first_block
    inside = (later_slots >= 0) & (offsets >= 0) & (offsets < local_blocks)
    wanted = jnp.any(
        inside[:, :, None] & (offsets[:, :, None] == jnp.arange(local_blocks)[None, None, :]),
        axis=1,
    )
    pick_table = wanted.astype(jnp.bfloat16)
    owner_table = wanted.astype(jnp.float32)

    def pack(table):
        return jnp.einsum(
            "ek,krc->erc", pick_table, table, preferred_element_type=jnp.float32
        ).astype(jnp.bfloat16)

    fetched = (
        lax.all_to_all(pack(latent_tables), "seq", split_axis=0, concat_axis=0, tiled=True),
        lax.all_to_all(pack(rope_tables), "seq", split_axis=0, concat_axis=0, tiled=True),
        lax.all_to_all(pack(index_tables), "seq", split_axis=0, concat_axis=0, tiled=True),
    )
    sel_row = lax.dynamic_index_in_dim(sel_blocks, seq_index, 0, keepdims=False)
    slot_valid = sel_row >= 0
    source = jnp.where(slot_valid, sel_row // local_blocks, 0)

    def chosen(table, remote):
        picked = jnp.take(remote, source[1:], axis=0)
        return jnp.concatenate([table[local_blocks - 1][None], picked], axis=0)

    sel_latent = chosen(latent_tables, fetched[0])
    sel_rope = chosen(rope_tables, fetched[1])
    sel_index = chosen(index_tables, fetched[2])
    positions = jnp.arange(block)
    slots = jnp.arange(slot_count)
    key_mask = slot_valid[None, :, None] & (
        (slots[None, :, None] > 0) | (positions[None, None, :] <= positions[:, None, None])
    )
    scores = (
        jnp.einsum("thc,jkc->thjk", q_latent, sel_latent, preferred_element_type=jnp.float32)
        + jnp.einsum("thc,jkc->thjk", q_rope, sel_rope, preferred_element_type=jnp.float32)
    ) * score_scale
    part_target = head_probs(scores, key_mask) / total_heads
    pre = (
        jnp.einsum("tid,jkd->tijk", index_queries, sel_index, preferred_element_type=jnp.float32)
        * index_scale
    )
    active, slope = gelu_pair(pre)
    part_logits = jnp.sum(index_weights[:, :, None, None] * active, axis=1)
    target, logits = lax.psum((part_target, part_logits), "head")
    grad_logits = logit_grad(target, logits, key_mask, loss_weight)
    grad_float = grad_logits.astype(jnp.float32)
    grad_weights = jnp.sum(grad_float[:, None] * active, axis=(2, 3))
    grad_pre = (grad_float[:, None] * index_weights[:, :, None, None] * slope * index_scale).astype(
        jnp.bfloat16
    )
    grad_queries = jnp.einsum(
        "tijk,jkd->tid", grad_pre, sel_index, preferred_element_type=jnp.float32
    )
    key_part = jnp.einsum(
        "tijk,tid->jkd", grad_pre, index_queries, preferred_element_type=jnp.float32
    )
    route = (
        (source[1:][None, :] == jnp.arange(seq_count)[:, None]) & slot_valid[1:][None, :]
    ).astype(jnp.float32)
    outgoing = jnp.einsum("ej,jkd->ekd", route, key_part[1:], precision=lax.Precision.HIGHEST)
    returned = lax.all_to_all(outgoing, "seq", split_axis=0, concat_axis=0, tiled=True)
    owned = jnp.einsum("ek,erd->krd", owner_table, returned, precision=lax.Precision.HIGHEST)
    owned = owned.at[local_blocks - 1].add(key_part[0])
    summed = lax.psum(owned, "head")
    grad_keys = summed.reshape(-1, index_width)
    return (grad_queries, grad_weights, grad_keys)


def solution(mesh):
    placed = (
        P("seq", "head", None),
        P("seq", "head", None),
        P("seq", None),
        P("seq", None),
        P("seq", "head", None),
        P("seq", "head"),
        P("seq", None),
        P(),
    )
    return jax.shard_map(
        body,
        mesh=mesh,
        in_specs=placed,
        out_specs=(P("seq", "head", None), P("seq", "head"), P("seq", None)),
        check_vma=False,
    )
```

profile of v0, /device:TPU:6, one launch (start us, length us, event | category | flops | bytes accessed | tf_op | source)
XLA Modules:
  0.0 685.7 jit_solution(3124595847814261056)
XLA Ops:
  7.2 0.0 copy-start
  7.2 0.0 copy-start.2
  7.2 0.9 reshape.94
  8.1 0.7 compare_and_fusion
  8.9 0.4 convolution_convert_fusion.2
  9.2 1.0 copy.95
  10.3 15.5 %all-to-all-start.2 = ((bf16[32,128,64]{1,2,0:T(8,128)(2,1)}), bf16[32,128,64]{1,2,0:T(8,128)(2,1)S(1)}, u32[]{:S(2)}, u32[]{:S(2)}) async-start(bf16[32,128,64]{1,2,0:T(8,128)(2,1)} %copy.95), calls=%async_computation.2 | async-start | bytes 1048576 | tf_op jit(solution)/shard_map/all_to_all | solution.py:71
  25.8 1.4 convolution_convert_fusion.1
  27.2 1.4 copy.90
  28.6 30.9 %all-to-all-done.2 = bf16[32,128,64]{1,2,0:T(8,128)(2,1)S(1)} async-done(((bf16[32,128,64]{1,2,0:T(8,128)(2,1)}), bf16[32,128,64]{1,2,0:T(8,128)(2,1)S(1)}, u32[]{:S(2)}, u32[]{:S(2)}) %all-to-all-start.2) | async-done | bytes 524320 | tf_op jit(solution)/shard_map/all_to_all | solution.py:71
  59.5 3.9 all-to-all-start
  63.5 0.0 copy-done.2
  63.5 1.3 convolution_convert_fusion
  64.8 4.4 copy.93
  69.2 0.0 copy-start.4
  69.2 50.8 %all-to-all-done = bf16[32,128,128]{2,1,0:T(8,128)(2,1)S(1)} async-done(((bf16[32,128,128]{2,1,0:T(8,128)(2,1)}), bf16[32,128,128]{2,1,0:T(8,128)(2,1)S(1)}, u32[]{:S(2)}, u32[]{:S(2)}) %all-to-all-start) | async-done | bytes 1048608 | tf_op jit(solution)/shard_map/all_to_all | solution.py:72
  120.0 4.9 all-to-all-start.1
  124.8 0.2 all-reduce.6.cloned.1.call-start
  125.1 0.0 copy-done.4
  125.1 0.2 dynamic-slice_reduce_fusion
  125.3 0.1 compare_and_fusion.1
  125.4 0.7 slice_bitcast_fusion.2
  126.1 0.8 slice_bitcast_fusion.1
  126.9 0.2 or_and_fusion
  127.1 0.6 gather_fusion.2
  127.7 0.1 broadcast_select_fusion.2
  127.8 0.6 gather_fusion
  128.5 0.1 broadcast_select_fusion.1
  128.6 0.0 copy-done.3
  128.6 0.0 copy-done.5
  128.6 4.8 multiply_reduce_fusion.1
  133.4 182.8 %all-to-all-done.1 = bf16[32,128,512]{2,1,0:T(8,128)(2,1)} async-done(((bf16[32,128,512]{2,1,0:T(8,128)(2,1)}), bf16[32,128,512]{2,1,0:T(8,128)(2,1)}, u32[]{:S(2)}, u32[]{:S(2)}) %all-to-all-start.1) | async-done | bytes 4194336 | tf_op jit(solution)/shard_map/all_to_all | solution.py:70
  316.1 2.9 gather_fusion.1
  319.0 0.3 broadcast_select_fusion
  319.3 3.8 fusion.14
  323.0 0.0 copy-done
  323.0 1.7 fusion
  324.8 1.5 fusion.3
  326.2 1.9 divide_reduce_fusion
  328.2 1.1 broadcast_multiply_fusion
  329.2 0.0 all-reduce.6.cloned.1.call-update
  329.3 0.3 all-reduce.4.cloned.1.call-start
  329.5 0.1 slice.66
  329.6 0.1 slice.60
  329.7 111.8 %all-reduce.6.cloned.1.call-done = (f32[128,16,128]{0,2,1:T(8,128)}, f32[128,16,128]{0,2,1:T(8,128)}) async-done(((f32[128,16,128]{0,2,1:T(8,128)}, f32[128,16,128]{0,2,1:T(8,128)}), (f32[128,16,128]{0,2,1:T(8,128)}, f32[128,16,128]{0,2,1:T(8,128)})) %all-reduce.6.cloned.1.call-update) | async-done | bytes 2097168 | tf_op jit(solution)/shard_map/psum | solution.py:101
  441.5 1.7 select_reduce_fusion
  443.3 1.7 fusion.23
  444.9 2.0 fusion.25
  446.9 0.0 copy-done.1
  446.9 4.2 multiply_reduce_fusion
  451.1 0.7 convolution_bitcast_fusion
  451.8 0.1 slice.76
  451.9 1.5 fusion.20
  453.4 1.2 copy.99
  454.6 113.3 %all_to_all.20 = f32[32,128,128]{2,1,0:T(8,128)S(1)} all-to-all(f32[32,128,128]{2,1,0:T(8,128)S(1)} %copy.99), channel_id=1, replica_groups=mesh['head'=16,'seq'=32] {'seq'}, dimensions={0} | all-to-all | bytes 4194304 | tf_op jit(solution)/shard_map/all_to_all | solution.py:118
  567.9 2.0 fusion.17
  569.9 0.1 slice.77
  570.0 1.5 scatter-add.4
  571.5 0.7 copy.103
  572.2 0.0 all-reduce.4.cloned.1.call-update
  572.2 0.7 convolution_bitcast_fusion.1
  573.0 0.9 copy.104
  573.8 103.3 %all-reduce.4.cloned.1.call-done = f32[512,128]{1,0:T(8,128)} async-done(((f32[512,128]{1,0:T(8,128)}), f32[512,128]{1,0:T(8,128)}) %all-reduce.4.cloned.1.call-update) | async-done | bytes 262160 | tf_op jit(solution)/shard_map/psum | solution.py:121
  677.1 1.7 copy.137
  (10 shorter events, 0.1 us)
Async XLA Ops:
  7.2 315.9 %copy-start = (bf16[128,8,64]{0,2,1:T(8,128)(2,1)S(1)}, bf16[128,8,64]{0,2,1:T(8,128)(2,1)}, u32[]{:S(2)}) copy-start(bf16[128,8,64]{0,2,1:T(8,128)(2,1)} %param.11) | copy-start | bytes 393220
  7.2 56.3 %copy-start.2 = (bf16[512,512]{1,0:T(8,128)(2,1)S(1)}, bf16[512,512]{1,0:T(8,128)(2,1)}, u32[]{:S(2)}) copy-start(bf16[512,512]{1,0:T(8,128)(2,1)} %param.12) | copy-start | bytes 1572868
  10.3 49.3 %all-to-all-start.2 = ((bf16[32,128,64]{1,2,0:T(8,128)(2,1)}), bf16[32,128,64]{1,2,0:T(8,128)(2,1)S(1)}, u32[]{:S(2)}, u32[]{:S(2)}) async-start(bf16[32,128,64]{1,2,0:T(8,128)(2,1)} %copy.95), calls=%async_computation.2 | async-start | bytes 1048576 | tf_op jit(solution)/shard_map/all_to_all | solution.py:71
  59.5 60.4 %all-to-all-start = ((bf16[32,128,128]{2,1,0:T(8,128)(2,1)}), bf16[32,128,128]{2,1,0:T(8,128)(2,1)S(1)}, u32[]{:S(2)}, u32[]{:S(2)}) async-start(bf16[32,128,128]{2,1,0:T(8,128)(2,1)} %copy.90), calls=%async_computation | async-start | bytes 2097152 | tf_op jit(solution)/shard_map/all_to_all | solution.py:72
  69.2 55.9 %copy-start.4 = (s32[32,16]{0,1:T(8,128)S(1)}, s32[32,16]{0,1:T(8,128)}, u32[]{:S(2)}) copy-start(s32[32,16]{0,1:T(8,128)} %param.17) | copy-start | bytes 6148
  69.2 59.5 %copy-start.3 = (bf16[128,4,128]{2,1,0:T(4,128)(2,1)S(1)}, bf16[128,4,128]{2,1,0:T(4,128)(2,1)}, u32[]{:S(2)}) copy-start(bf16[128,4,128]{2,1,0:T(4,128)(2,1)} %param.14) | copy-start | bytes 393220
  69.2 59.5 %copy-start.5 = (f32[128,4]{0,1:T(4,128)S(1)}, f32[128,4]{0,1:T(4,128)}, u32[]{:S(2)}) copy-start(f32[128,4]{0,1:T(4,128)} %param.15) | copy-start | bytes 6148
  120.0 196.2 %all-to-all-start.1 = ((bf16[32,128,512]{2,1,0:T(8,128)(2,1)}), bf16[32,128,512]{2,1,0:T(8,128)(2,1)}, u32[]{:S(2)}, u32[]{:S(2)}) async-start(bf16[32,128,512]{2,1,0:T(8,128)(2,1)} %copy.93), calls=%async_computation.1 | async-start | bytes 8388608 | tf_op jit(solution)/shard_map/all_to_all | solution.py:70
  124.8 316.7 %all-reduce.6.cloned.1.call-start = ((), (), s32[]{:S(2)}) async-start(), calls=%async_computation.5 | async-start | bytes 4194304 | tf_op jit(solution)/shard_map/psum | solution.py:101
  329.3 347.9 %all-reduce.4.cloned.1.call-start = ((), (), s32[]{:S(2)}) async-start(), calls=%async_computation.4 | async-start | bytes 524288 | tf_op jit(solution)/shard_map/psum | solution.py:121
  441.5 5.4 copy-start.1
Sparse Core Ops, SparseCore 0:
  329.4 112.1 all-reduce.5
  572.3 104.7 all-reduce.3
where the time goes:
time: 686 us
  waiting for transfers between devices  480 us (70%)
  blocking collectives  113 us (16%)
  starting transfers between devices  24.8 us (4%)
  local copies, waits for them, and re-layouts  19.8 us (3%)
  matrix products  18.3 us (3%)
  other arithmetic  15.5 us (2%)
  between operations  14.3 us (2%)
    all_to_all x1, waiting for transfers between devices, body(): lax.all_to_all(pack(latent_tables), 'seq', split_axis=0, concat_axis=0, t...  183 us
    all_to_all x1, blocking collectives, body(): lax.all_to_all(outgoing, 'seq', split_axis=0, concat_axis=0, tiled=True)  113 us
    psum x1, waiting for transfers between devices, body(): target, logits = lax.psum((part_target, part_logits), 'head')  112 us
    psum x1, waiting for transfers between devices, body(): summed = lax.psum(owned, 'head')  103 us
    all_to_all x1, waiting for transfers between devices, body(): lax.all_to_all(pack(index_tables), 'seq', split_axis=0, concat_axis=0, ti...  50.8 us
    all_to_all x1, waiting for transfers between devices, body(): lax.all_to_all(pack(rope_tables), 'seq', split_axis=0, concat_axis=0, til...  30.9 us
    all_to_all x1, starting transfers between devices, body(): lax.all_to_all(pack(rope_tables), 'seq', split_axis=0, concat_axis=0, til...  15.5 us
  transfers between devices with their start and end apart: 5, of which 5 were waited for; matrix products, arithmetic and copies ran while one was open for 3% of the time, Pallas kernels for 0%

commit v1 on v0

v1 whole, which is shorter than its diff:
```python
import math

import jax
import jax.numpy as jnp
from jax import lax
from jax.sharding import PartitionSpec as P

score_scale = 192.0 ** (-0.5)
gelu_coef = math.sqrt(2.0 / math.pi)
cubic_coef = 0.044715
bf16 = jnp.bfloat16
f32 = jnp.float32


def gelu_pair(values):
    inner = gelu_coef * (values + cubic_coef * values * values * values)
    tangent = jnp.tanh(inner)
    active = 0.5 * values * (1.0 + tangent)
    slope = 0.5 * (1.0 + tangent) + 0.5 * values * (1.0 - tangent * tangent) * gelu_coef * (
        1.0 + 3.0 * cubic_coef * values * values
    )
    return (active, slope)


def exchange(array, axis):
    return lax.all_to_all(array, axis, split_axis=0, concat_axis=0, tiled=True)


def pad_lanes(array, width):
    return jnp.pad(array, [(0, 0)] * (array.ndim - 1) + [(0, width - array.shape[-1])])


def body(
    q_latent, q_rope, latent_cache, rope_keys, index_queries, index_weights, index_keys, sel_blocks
):
    head_count = lax.axis_size("head")
    seq_count = lax.axis_size("seq")
    head_index = lax.axis_index("head")
    seq_index = lax.axis_index("seq")
    block, heads, latent_width = q_latent.shape
    rope_width = q_rope.shape[2]
    index_heads, index_width = index_queries.shape[1:]
    slot_count = sel_blocks.shape[1]
    local_blocks = latent_cache.shape[0] // block
    index_scale = index_width ** (-0.5)
    loss_weight = float(slot_count * block)
    groups = head_count // 2
    rows = block // groups
    small = rows // 2
    tokens = block // head_count
    half_width = latent_width // 2
    lanes = half_width + index_width
    remote_slots = slot_count - 1
    group = head_index % groups
    half = head_index // groups

    later = sel_blocks[:, 1:]
    offsets = later - seq_index * local_blocks
    inside = (later >= 0) & (offsets >= 0) & (offsets < local_blocks)
    wanted = jnp.any(inside, axis=1)
    which = jnp.sum(jnp.where(inside, offsets, 0), axis=1)
    sel_row = lax.dynamic_index_in_dim(sel_blocks, seq_index, 0, keepdims=False)
    slot_valid = sel_row >= 0
    source = jnp.where(slot_valid, sel_row // local_blocks, 0)

    latent_tables = latent_cache.reshape(local_blocks, block, latent_width)
    rope_tables = rope_keys.reshape(local_blocks, block, rope_width)
    index_tables = index_keys.reshape(local_blocks, block, index_width)
    first_row = group * rows
    latent_share = lax.dynamic_slice(
        latent_tables, (0, first_row, half * half_width), (local_blocks, rows, half_width)
    )
    index_share = lax.dynamic_slice(
        index_tables, (0, first_row, 0), (local_blocks, rows, index_width)
    )
    rope_share = lax.dynamic_slice(rope_tables, (0, first_row, 0), (local_blocks, rows, rope_width))
    share = jnp.concatenate(
        [latent_share, jnp.where(half == 0, index_share, pad_lanes(rope_share, index_width))],
        axis=-1,
    )
    packed = jnp.broadcast_to(share[0], (seq_count, rows, lanes))
    for k in range(1, local_blocks):
        packed = jnp.where((which == k)[:, None, None], share[k], packed)
    fetched = exchange(packed, "seq")
    chosen = jnp.take(fetched, source[1:], axis=0).reshape(remote_slots * rows, lanes)

    share_rows = remote_slots * rows
    query_rows = tokens * heads
    index_rows = tokens * index_heads
    latent_parts = q_latent.reshape(head_count, query_rows, latent_width)
    rope_parts = q_rope.reshape(head_count, query_rows, rope_width)
    index_parts = index_queries.reshape(head_count, index_rows, index_width)
    weight_parts = index_weights.reshape(head_count, index_rows, 1)
    high = lax.reduce_precision(weight_parts, 8, 7)
    middle = lax.reduce_precision(weight_parts - high, 8, 7)
    low = weight_parts - high - middle
    weight_pieces = pad_lanes(
        jnp.concatenate([high, middle, low], axis=-1).astype(bf16), index_width
    )
    second = jnp.concatenate(
        [
            latent_parts[:, :, lanes:],
            pad_lanes(rope_parts, 128),
            jnp.concatenate([index_parts, weight_pieces], axis=1),
        ],
        axis=-1,
    )
    outgoing = jnp.concatenate(
        [
            jnp.broadcast_to(chosen, (head_count, share_rows, lanes)),
            latent_parts[:, :, :lanes],
            second,
        ],
        axis=1,
    )
    arrived = exchange(outgoing, "head")

    key_low = arrived[:groups, :share_rows].reshape(groups * share_rows, lanes)
    key_high = arrived[groups:, :share_rows].reshape(groups * share_rows, lanes)
    query_first = arrived[:, share_rows : share_rows + query_rows]
    query_second = arrived[:, share_rows + query_rows :]
    queries = jnp.concatenate(
        [query_first, query_second[:, :, : 128 + rope_width]], axis=-1
    )
    index_q = query_second[:, :index_rows, 256:]
    weights = jnp.sum(query_second[:, index_rows:, 256:259].astype(f32), axis=-1)
    own = slice((local_blocks - 1) * block, local_blocks * block)
    own_index = index_keys[own]
    remote_keys = jnp.concatenate(
        [
            key_low[:, :half_width],
            key_high[:, :half_width],
            key_high[:, half_width : half_width + rope_width],
        ],
        axis=-1,
    )
    own_keys = jnp.concatenate([latent_cache[own], rope_keys[own]], axis=-1)
    keys = jnp.concatenate([remote_keys, own_keys], axis=0)
    index_k = jnp.concatenate([key_low[:, half_width:], own_index], axis=0)
    total = keys.shape[0]

    token_at = head_index * tokens + jnp.arange(tokens)
    remote_mask = jnp.broadcast_to(
        slot_valid[None, 1:, None], (groups, remote_slots, rows)
    ).reshape(-1)
    key_mask = jnp.concatenate(
        [
            jnp.broadcast_to(remote_mask, (tokens, remote_mask.shape[0])),
            jnp.arange(block)[None, :] <= token_at[:, None],
        ],
        axis=1,
    )

    scores = (
        jnp.einsum("sqc,kc->sqk", queries, keys, preferred_element_type=f32) * score_scale
    ).reshape(head_count, tokens, heads, total)
    mask = key_mask[None, :, None, :]
    highest = jnp.max(jnp.where(mask, scores, -jnp.inf), axis=-1, keepdims=True)
    powers = jnp.where(mask, jnp.exp(scores - highest), 0.0)
    target = jnp.sum(powers / jnp.sum(powers, axis=-1, keepdims=True), axis=(0, 2)) / (
        heads * head_count
    )

    pre = (
        jnp.einsum("sqc,kc->sqk", index_q, index_k, preferred_element_type=f32) * index_scale
    ).reshape(head_count, tokens, index_heads, total)
    active, slope = gelu_pair(pre)
    weights = weights.reshape(head_count, tokens, index_heads, 1)
    logits = jnp.sum(weights * active, axis=(0, 2))
    top = jnp.max(jnp.where(key_mask, logits, -jnp.inf), axis=-1, keepdims=True)
    likely = jnp.where(key_mask, jnp.exp(logits - top), 0.0)
    predicted = likely / jnp.sum(likely, axis=-1, keepdims=True)
    grad_logits = jnp.where(key_mask, loss_weight * (predicted - target), 0.0).astype(bf16)
    grad_float = grad_logits.astype(f32)[None, :, None, :]
    grad_weights = jnp.sum(grad_float * active, axis=-1)
    grad_pre = (
        (grad_float * weights * slope * index_scale)
        .astype(bf16)
        .reshape(head_count, index_rows, total)
    )
    grad_queries = jnp.einsum("sqk,kc->sqc", grad_pre, index_k, preferred_element_type=f32)
    key_part = jnp.einsum("sqk,sqc->kc", grad_pre, index_q, preferred_element_type=f32)

    remote_part = key_part[: groups * share_rows].reshape(
        groups, remote_slots, 2, small, index_width
    )
    own_part = key_part[groups * share_rows :].reshape(groups, 1, 2, small, index_width)
    shares = (
        jnp.concatenate([own_part, remote_part], axis=1)
        .transpose(2, 0, 1, 3, 4)
        .reshape(head_count, slot_count * small, index_width)
        .astype(bf16)
    )
    summed = jnp.sum(exchange(shares, "head").astype(f32), axis=0).reshape(
        slot_count, small, index_width
    )
    found = (source[1:][None, :] == jnp.arange(seq_count)[:, None]) & slot_valid[1:][None, :]
    slot_of = jnp.sum(jnp.where(found, jnp.arange(1, slot_count)[None, :], 0), axis=1)
    returned = exchange(jnp.take(summed, slot_of, axis=0), "seq")
    owner = wanted[:, None] & (which[:, None] == jnp.arange(local_blocks)[None, :])
    owned = jnp.sum(
        jnp.where(owner[:, :, None, None], returned[:, None], 0.0), axis=0
    )
    owned = owned.at[local_blocks - 1].add(summed[0])

    own_rows = local_blocks * small
    last = jnp.concatenate(
        [
            jnp.broadcast_to(
                owned.reshape(own_rows, index_width), (head_count, own_rows, index_width)
            ),
            grad_queries,
            pad_lanes(grad_weights.reshape(head_count, 1, index_rows), index_width),
            jnp.zeros((head_count, 7, index_width), f32),
        ],
        axis=1,
    )
    final = exchange(last, "head")
    grad_keys = (
        final[:, :own_rows]
        .reshape(2, groups, local_blocks, small, index_width)
        .transpose(2, 1, 0, 3, 4)
        .reshape(local_blocks * block, index_width)
    )
    out_queries = final[:, own_rows : own_rows + index_rows].reshape(
        block, index_heads, index_width
    )
    out_weights = final[:, own_rows + index_rows, :index_rows].reshape(block, index_heads)
    return (out_queries, out_weights, grad_keys)


def solution(mesh):
    placed = (
        P("seq", "head", None),
        P("seq", "head", None),
        P("seq", None),
        P("seq", None),
        P("seq", "head", None),
        P("seq", "head"),
        P("seq", None),
        P(),
    )
    return jax.shard_map(
        body,
        mesh=mesh,
        in_specs=placed,
        out_specs=(P("seq", "head", None), P("seq", "head"), P("seq", None)),
        check_vma=False,
    )
```

time: 686 us -> 247 us (0.36)
  waiting for transfers between devices: 480 us -> 116 us
  blocking collectives: 113 us -> 14.8 us
  other arithmetic: 15.5 us -> 42.2 us
  between operations: 14.3 us -> 1.06 us
  starting transfers between devices: 24.8 us -> 35.4 us
    psum x2 -> x0, waiting for transfers between devices: 215 us -> none  [the longest x1 112 us: body(): target, logits = lax.psum((part_target, part_logits), 'head')]
    all_to_all x3 -> x4, waiting for transfers between devices: 265 us -> 116 us  [exchange(): return lax.all_to_all(array, axis, split_axis=0, concat_axis=0, tiled=True)]
    all_to_all x1, blocking collectives: 113 us -> 14.8 us  [exchange(): return lax.all_to_all(array, axis, split_axis=0, concat_axis=0, tiled=True)]
    sub x0 -> x1, other arithmetic: none -> 12.2 us  [body(): powers = jnp.where(mask, jnp.exp(scores - highest), 0.0)]
    div x1, other arithmetic: 1.09 us -> 12.3 us  [body(): powers / jnp.sum(powers, axis=-1, keepdims=True)]
    all_to_all x3 -> x4, starting transfers between devices: 24.3 us -> 35.4 us  [exchange(): return lax.all_to_all(array, axis, split_axis=0, concat_axis=0, tiled=True)]
    slice x5 -> x17, local copies, waits for them, and re-layouts: 1.63 us -> 10.7 us  [the longest x1 2.11 us: body(): key_low = arrived[:groups, :share_rows].reshape(groups * share_rows, lanes)]
    dot_general x10 -> x4, matrix products: 18.3 us -> 14.9 us  [the longest x1 7.84 us: body(): jnp.einsum('sqc,kc->sqk', queries, keys, preferred_element_type=f32)]
  transfers between devices with their start and end apart: 5 -> 4, of which waited for: 5 -> 4; matrix products, arithmetic and copies ran while one was open for 3% -> 3% of each run, Pallas kernels for 0% -> 0%
where the time goes in v1:
time: 247 us; the launch traced here: 245 us
  waiting for transfers between devices  116 us (47%)
  other arithmetic  42.2 us (17%)
  starting transfers between devices  35.4 us (14%)
  local copies, waits for them, and re-layouts  20 us (8%)
  matrix products  14.9 us (6%)
  blocking collectives  14.8 us (6%)
    all_to_all x4, waiting for transfers between devices, exchange(): return lax.all_to_all(array, axis, split_axis=0, concat_axis=0, tiled=True)  116 us
    all_to_all x4, starting transfers between devices, exchange(): return lax.all_to_all(array, axis, split_axis=0, concat_axis=0, tiled=True)  35.4 us
    all_to_all x1, blocking collectives, exchange(): return lax.all_to_all(array, axis, split_axis=0, concat_axis=0, tiled=True)  14.8 us
    div x1, other arithmetic, body(): powers / jnp.sum(powers, axis=-1, keepdims=True)  12.3 us
    sub x1, other arithmetic, body(): powers = jnp.where(mask, jnp.exp(scores - highest), 0.0)  12.2 us
    dot_general x1, matrix products, body(): jnp.einsum('sqc,kc->sqk', queries, keys, preferred_element_type=f32)  7.84 us
    convert_element_type x1, other arithmetic, body(): grad_pre = (grad_float * weights * slope * index_scale).astype(bf16).resh...  7.25 us
  transfers between devices with their start and end apart: 4, of which 4 were waited for; matrix products, arithmetic and copies ran while one was open for 3% of the time, Pallas kernels for 0%

profile of v1, /device:TPU:6, one launch (start us, length us, event | category | flops | bytes accessed | tf_op | source)
XLA Modules:
  0.0 244.8 jit_solution(10291566875361558758)
XLA Ops:
  0.7 1.0 copy.66
  1.7 0.8 fusion.69
  2.5 0.7 select_reduce_fusion.4
  3.2 0.8 constant_dynamic-slice_fusion.1
  4.0 0.7 pad_select_fusion
  4.7 0.9 select_select_fusion
  5.6 15.5 %all-to-all-start = ((bf16[32,16,384]{2,1,0:T(8,128)(2,1)}), bf16[32,16,384]{2,1,0:T(8,128)(2,1)S(1)}, u32[]{:S(2)}, u32[]{:S(2)}) async-start(bf16[32,16,384]{2,1,0:T(8,128)(2,1)} %select_select_fusion), calls=%async_computation | async-start | bytes 786432 | tf_op jit(solution)/shard_map/all_to_all | solution.py:26
  21.1 1.2 slice.152
  22.3 1.0 slice.153
  23.3 0.9 dynamic-slice_reduce_fusion
  24.2 0.1 compare_and_fusion.1
  24.3 0.1 broadcast_in_dim.167
  24.4 0.1 broadcast_in_dim.168
  24.5 0.8 copy.56
  25.3 0.1 reshape.341
  25.4 0.2 copy.57
  25.6 0.2 copy.55
  25.8 23.6 %all-to-all-done = bf16[32,16,384]{2,1,0:T(8,128)(2,1)S(1)} async-done(((bf16[32,16,384]{2,1,0:T(8,128)(2,1)}), bf16[32,16,384]{2,1,0:T(8,128)(2,1)S(1)}, u32[]{:S(2)}, u32[]{:S(2)}) %all-to-all-start) | async-done | bytes 393248 | tf_op jit(solution)/shard_map/all_to_all | solution.py:26
  49.4 0.6 gather_fusion
  50.0 0.1 bitcast_select_fusion
  50.1 0.3 broadcast_in_dim.179
  50.3 2.7 %fusion.15 = bf16[16,368,384]{2,1,0:T(8,128)(2,1)} fusion(bf16[16,32,3]{2,1,0:T(8,128)(2,1)S(1)} %copy.57, bf16[16,64,64]{2,1,0:T(8,128)(2,1)S(1)} %bitcast.65, bf16[16,32,128]{2,1,0:T(8,128)(2,1)S(1)} %bitcast.73, bf16[16,64,128]{2,1,0:T(8,128)(2,1)S(1)} %slice.153, bf16[16,64,384]{2,1,0:T(8,128)(2,1)S(1)} %slice.152, ...), kind=kLoop, calls=%fused_computation.24 | loop fusion | flops 54263808 | bytes 8784896 | tf_op jit(solution)/shard_map/concatenate | solution.py:108
  53.0 7.4 %all-to-all-start.1 = ((bf16[16,368,384]{2,1,0:T(8,128)(2,1)}), bf16[16,368,384]{2,1,0:T(8,128)(2,1)}, u32[]{:S(2)}, u32[]{:S(2)}) async-start(bf16[16,368,384]{2,1,0:T(8,128)(2,1)} %fusion.15), calls=%async_computation.1 | async-start | bytes 9043968 | tf_op jit(solution)/shard_map/all_to_all | solution.py:26
  60.4 0.9 slice.133
  61.4 0.8 slice.127
  62.2 0.1 copy.69
  62.4 0.1 broadcast_in_dim.164
  62.5 0.1 reshape.380
  62.7 0.1 select_reduce_fusion.3
  63.0 68.1 %all-to-all-done.1 = bf16[16,368,384]{2,1,0:T(8,128)(2,1)} async-done(((bf16[16,368,384]{2,1,0:T(8,128)(2,1)}), bf16[16,368,384]{2,1,0:T(8,128)(2,1)}, u32[]{:S(2)}, u32[]{:S(2)}) %all-to-all-start.1) | async-done | bytes 4522016 | tf_op jit(solution)/shard_map/all_to_all | solution.py:26
  131.1 2.1 fusion.70
  133.3 1.5 copy.60
  134.8 1.6 copy.68
  136.3 1.2 slice.158
  137.6 1.1 slice.159
  138.7 7.8 %fusion.25 = f32[16,64,2048]{2,1,0:T(8,128)} fusion(bf16[128,64]{0,1:T(8,128)(2,1)S(1)} %slice-done, bf16[128,512]{0,1:T(8,128)(2,1)S(1)} %copy.69, bf16[1920,320]{0,1:T(8,128)(2,1)S(1)} %copy.68, bf16[1920,256]{0,1:T(8,128)(2,1)} %copy.60, bf16[16,64,192]{2,1,0:T(8,128)(2,1)S(1)} %slice.159, bf16[16,64,384]{2,1,0:T(8,128)(2,1)S(1)} %slice.158), kind=kOutput, calls=%fused_computation.39 | convolution fusion | flops 2427715584 | bytes 11927552 | tf_op jit(solution)/shard_map/sqc,kc->sqk/dot_general | solution.py:155
  146.5 12.3 %fusion = f32[16,64,2048]{2,1,0:T(8,128)} fusion(f32[16,64,2048]{2,1,0:T(8,128)} %fusion.25, pred[64,2048]{1,0:T(8,128)(4,1)S(1)} %broadcast_bitcast_fusion), kind=kOutput, calls=%fused_computation.2 | output fusion | flops 10491902 | bytes 16908288 | tf_op jit(solution)/shard_map/div | solution.py:160
  158.9 12.2 %divide_reduce_fusion = f32[64,2048]{1,0:T(8,128)S(1)} fusion(f32[16,64,2048]{2,1,0:T(8,128)} %fusion, f32[16,64,2048]{2,1,0:T(8,128)} %fusion.25, pred[64,2048]{1,0:T(8,128)(4,1)S(1)} %broadcast_bitcast_fusion), kind=kOutput, calls=%fused_computation.19 | output fusion | flops 14552063 | bytes 17432576 | tf_op jit(solution)/shard_map/sub | solution.py:159
  171.0 0.1 bitcast_reduce_fusion
  171.2 1.1 convert_reduce_fusion.1
  172.2 4.6 %multiply_reduce_fusion.1 = (f32[32,2048]{1,0:T(8,128)S(1)}, f32[16,32,2048]{2,1,0:T(8,128)}) fusion(f32[16,32]{1,0:T(8,128)S(1)} %convert_reduce_fusion.1, bf16[128,128]{1,0:T(8,128)(2,1)S(1)} %slice.127, bf16[1920,128]{1,0:T(8,128)(2,1)S(1)} %slice.157, bf16[16,368,384]{2,1,0:T(8,128)(2,1)} %all-to-all-done.1), kind=kOutput, calls=%fused_computation.32 | convolution fusion | flops 280952832 | bytes 5113856 | tf_op jit(solution)/shard_map/sqc,kc->sqk/dot_general | solution.py:165
  176.9 0.4 reduce_sum.111
  177.3 0.1 select_reduce_fusion.2
  177.4 0.2 fusion.43
  177.7 0.1 fusion.44
  177.8 0.1 mul.168
  177.9 7.3 %multiply_convert_fusion = (bf16[16,32,2048]{2,1,0:T(8,128)(2,1)S(1)}, f32[16,32]{1,0:T(8,128)S(1)}) fusion(f32[16,32,2048]{2,1,0:T(8,128)} %get-tuple-element.51, f32[32,2048]{1,0:T(8,128)S(1)} %mul.168, f32[16,32]{1,0:T(8,128)S(1)} %convert_reduce_fusion.1), kind=kLoop, calls=%fused_computation.29 | loop fusion | flops 26213888 | bytes 6557696 | tf_op jit(solution)/shard_map/convert_element_type | solution.py:178
  185.2 1.7 fusion.24
  186.9 0.9 pad_maximum_fusion
  187.8 8.6 %all-to-all-start.2 = ((bf16[16,128,128]{2,1,0:T(8,128)(2,1)}), bf16[16,128,128]{2,1,0:T(8,128)(2,1)S(1)}, u32[]{:S(2)}, u32[]{:S(2)}) async-start(bf16[16,128,128]{2,1,0:T(8,128)(2,1)} %bitcast.21), calls=%async_computation.2 | async-start | bytes 1048576 | tf_op jit(solution)/shard_map/all_to_all | solution.py:26
  196.5 8.4 %all-to-all-done.2 = bf16[16,128,128]{2,1,0:T(8,128)(2,1)S(1)} async-done(((bf16[16,128,128]{2,1,0:T(8,128)(2,1)}), bf16[16,128,128]{2,1,0:T(8,128)(2,1)S(1)}, u32[]{:S(2)}, u32[]{:S(2)}) %all-to-all-start.2) | async-done | bytes 524320 | tf_op jit(solution)/shard_map/all_to_all | solution.py:26
  205.0 0.6 gather_fusion.1
  205.6 0.8 broadcast_select_fusion
  206.3 3.9 %all-to-all-start.3 = ((f32[32,8,128]{2,1,0:T(8,128)}), f32[32,8,128]{2,1,0:T(8,128)S(1)}, u32[]{:S(2)}, u32[]{:S(2)}) async-start(f32[32,8,128]{2,1,0:T(8,128)} %broadcast_select_fusion), calls=%async_computation.3 | async-start | bytes 262144 | tf_op jit(solution)/shard_map/all_to_all | solution.py:26
  210.2 0.1 fusion.45
  210.3 0.7 fusion.39
  211.0 16.4 %all-to-all-done.3 = f32[32,8,128]{2,1,0:T(8,128)S(1)} async-done(((f32[32,8,128]{2,1,0:T(8,128)}), f32[32,8,128]{2,1,0:T(8,128)S(1)}, u32[]{:S(2)}, u32[]{:S(2)}) %all-to-all-start.3) | async-done | bytes 131104 | tf_op jit(solution)/shard_map/all_to_all | solution.py:26
  227.4 0.2 select_reduce_fusion.1
  227.6 0.1 fusion.37
  227.7 14.8 %all_to_all.25 = f32[16,72,128]{2,1,0:T(8,128)S(1)} all-to-all(f32[16,72,128]{2,1,0:T(8,128)S(1)} %fusion.37), channel_id=1, replica_groups=mesh['head'=16,'seq'=32] {'head'}, dimensions={0} | all-to-all | bytes 1179648 | tf_op jit(solution)/shard_map/all_to_all | solution.py:26
  242.6 0.7 fusion.71
  243.3 0.7 copy.64
  244.1 0.1 reshape_squeeze.3
  244.1 0.7 copy.65
  (37 shorter events, 0.9 us)
Async XLA Ops:
  0.6 24.9 %copy-start.1 = (bf16[128,8,64]{0,2,1:T(8,128)(2,1)S(1)}, bf16[128,8,64]{0,2,1:T(8,128)(2,1)}, u32[]{:S(2)}) copy-start(bf16[128,8,64]{0,2,1:T(8,128)(2,1)} %param.11) | copy-start | bytes 393220
  1.7 48.7 %copy-start = (bf16[128,4,128]{2,1,0:T(4,128)(2,1)S(1)}, bf16[128,4,128]{2,1,0:T(4,128)(2,1)}, u32[]{:S(2)}) copy-start(bf16[128,4,128]{2,1,0:T(4,128)(2,1)} %param.14) | copy-start | bytes 393220
  5.6 43.7 %all-to-all-start = ((bf16[32,16,384]{2,1,0:T(8,128)(2,1)}), bf16[32,16,384]{2,1,0:T(8,128)(2,1)S(1)}, u32[]{:S(2)}, u32[]{:S(2)}) async-start(bf16[32,16,384]{2,1,0:T(8,128)(2,1)} %select_select_fusion), calls=%async_computation | async-start | bytes 786432 | tf_op jit(solution)/shard_map/all_to_all | solution.py:26
  53.0 78.0 %all-to-all-start.1 = ((bf16[16,368,384]{2,1,0:T(8,128)(2,1)}), bf16[16,368,384]{2,1,0:T(8,128)(2,1)}, u32[]{:S(2)}, u32[]{:S(2)}) async-start(bf16[16,368,384]{2,1,0:T(8,128)(2,1)} %fusion.15), calls=%async_computation.1 | async-start | bytes 9043968 | tf_op jit(solution)/shard_map/all_to_all | solution.py:26
  133.2 5.4 %slice-start = ((bf16[512,64]{0,1:T(8,128)(2,1)}), bf16[128,64]{0,1:T(8,128)(2,1)S(1)}, s32[]{:S(2)}) async-start(bf16[512,64]{0,1:T(8,128)(2,1)} %param.13), calls=%async_computation.5 | async-start | bytes 32768 | tf_op jit(solution)/shard_map/slice | solution.py:137
  187.8 17.1 %all-to-all-start.2 = ((bf16[16,128,128]{2,1,0:T(8,128)(2,1)}), bf16[16,128,128]{2,1,0:T(8,128)(2,1)S(1)}, u32[]{:S(2)}, u32[]{:S(2)}) async-start(bf16[16,128,128]{2,1,0:T(8,128)(2,1)} %bitcast.21), calls=%async_computation.2 | async-start | bytes 1048576 | tf_op jit(solution)/shard_map/all_to_all | solution.py:26
  206.3 21.0 %all-to-all-start.3 = ((f32[32,8,128]{2,1,0:T(8,128)}), f32[32,8,128]{2,1,0:T(8,128)S(1)}, u32[]{:S(2)}, u32[]{:S(2)}) async-start(f32[32,8,128]{2,1,0:T(8,128)} %broadcast_select_fusion), calls=%async_computation.3 | async-start | bytes 262144 | tf_op jit(solution)/shard_map/all_to_all | solution.py:26

commit v2 on v0

v2 whole, which is shorter than its diff:
```python
import functools
import math

import jax
import jax.numpy as jnp
from jax import lax
from jax.experimental import pallas as pl
from jax.experimental.pallas import tpu as pltpu
from jax.sharding import PartitionSpec as P

score_scale = 192.0 ** (-0.5)
gelu_coef = math.sqrt(2.0 / math.pi)
cubic_coef = 0.044715
bf16 = jnp.bfloat16
f32 = jnp.float32


def dot_last(a, b):
    return lax.dot_general(a, b, (((1,), (1,)), ((), ())), preferred_element_type=f32)


def dot(a, b, precision=None):
    return jnp.dot(a, b, preferred_element_type=f32, precision=precision)


def gelu_pair(values):
    square = values * values
    tangent = jnp.tanh(values * (gelu_coef + (gelu_coef * cubic_coef) * square))
    upper = 0.5 + 0.5 * tangent
    active = values * upper
    slope = upper + active * (1.0 - upper) * (
        2.0 * gelu_coef + (6.0 * gelu_coef * cubic_coef) * square
    )
    return (active, slope)


def first_kernel(
    groups, sel_turned, latent, rope_turned, index, packed, wide, narrow, turned, rope, sems
):
    slots, destinations = sel_turned.shape
    local_blocks, rows, latent_width = wide.shape
    block = latent.shape[0] // local_blocks
    half_width = latent_width // 2
    head = lax.axis_index("head")
    group = lax.rem(head, groups)
    is_low = head < groups
    copies = [pltpu.make_async_copy(rope_turned, turned, sems.at[0])]
    spots = []
    for k in range(local_blocks):
        at = pl.ds(pl.multiple_of(k * block + group * rows, rows), rows)
        spots.append(at)
        copies.append(pltpu.make_async_copy(latent.at[at], wide.at[k], sems.at[1 + 2 * k]))
        copies.append(pltpu.make_async_copy(index.at[at], narrow.at[k], sems.at[2 + 2 * k]))
    for copy in copies:
        copy.start()

    total = packed.shape[0]
    repeat = lax.broadcasted_iota(jnp.int32, (total, destinations), 0) // rows
    repeat = (repeat == lax.broadcasted_iota(jnp.int32, (total, destinations), 1)).astype(f32)
    chosen = dot_last(repeat, sel_turned[...].astype(f32))
    offset = chosen - (lax.axis_index("seq") * local_blocks).astype(f32)
    slot = lax.broadcasted_iota(jnp.int32, (total, slots), 1)
    inside = (chosen >= 0) & (offset >= 0) & (offset < local_blocks) & (slot > 0)
    which = jnp.sum(jnp.where(inside, offset, 0.0), axis=1, keepdims=True)
    width = local_blocks * rows
    row = lax.broadcasted_iota(jnp.int32, (total, width), 0) % rows
    column = lax.broadcasted_iota(jnp.int32, (total, width), 1)
    pick = (column.astype(f32) == which * rows + row.astype(f32)).astype(bf16)

    for copy in copies:
        copy.wait()
    rope_rows = turned[...].astype(f32)
    rope[...] = jnp.concatenate([rope_rows, rope_rows], axis=0).T.astype(bf16)
    parts = []
    for k in range(local_blocks):
        parts.append(
            jnp.concatenate(
                [
                    jnp.where(is_low, wide[k, :, 0:half_width], wide[k, :, half_width:]),
                    jnp.where(is_low, narrow[k], rope[spots[k], :]),
                ],
                axis=1,
            )
        )
    share = jnp.concatenate(parts, axis=0)
    packed[...] = dot(pick, share).astype(bf16)


def second_kernel(local_blocks, sel, fetched, latent, rope, index, weight, outgoing):
    destinations = outgoing.shape[0]
    slots = sel.shape[0]
    rows, lanes = fetched.shape[1:]
    here = lax.axis_index("seq")
    query_rows = latent.shape[0] // destinations
    index_rows = index.shape[0] // destinations
    rope_rows = rope.shape[0] // destinations
    weight_rows = weight.shape[0] // destinations
    first = (slots - 1) * rows
    second = first + query_rows
    tall = index_rows + weight_rows
    rest = query_rows - tall
    for j in range(1, slots):
        source = lax.div(jnp.maximum(sel[j, here], 0), local_blocks)
        piece = fetched[source]
        for k in range(destinations):
            outgoing[k, (j - 1) * rows : j * rows, :] = piece
    for k in range(destinations):
        at = k * query_rows
        outgoing[k, first:second, :] = latent[at : at + query_rows, 0:lanes]
        outgoing[k, second : second + tall, 0:128] = latent[at : at + tall, lanes:]
        outgoing[k, second : second + rest, 128:256] = latent[
            at + tall : at + query_rows, lanes:
        ]
        outgoing[k, second + rest : second + tall, 128:256] = rope[
            k * rope_rows : (k + 1) * rope_rows, :
        ]
        outgoing[k, second : second + index_rows, 256:384] = index[
            k * index_rows : (k + 1) * index_rows, :
        ]
        outgoing[k, second + index_rows : second + tall, 256:384] = weight[
            k * weight_rows : (k + 1) * weight_rows, :
        ]


def compute_kernel(
    share_rows,
    loss_weight,
    index_scale,
    arrived,
    bias,
    key_bias,
    own_latent,
    own_rope,
    own_index,
    grad_queries,
    grad_weights,
    shares,
    keys,
    index_k,
    scores,
    highest,
    active,
    slope,
    grad_pre,
    logit_rows,
    target_rows,
    grad_keys,
):
    sources, _, lanes = arrived.shape
    groups = sources // 2
    tokens, total = bias.shape
    block, latent_width = own_latent.shape
    half_width = latent_width // 2
    index_width = own_index.shape[1]
    query_rows = target_rows.shape[0]
    heads = query_rows // tokens
    index_rows = logit_rows.shape[0]
    index_heads = index_rows // tokens
    remote = groups * share_rows
    tile = 2 * 128
    tiles = total // tile
    step = 4
    score_rows = step * query_rows
    index_step = step
    chunk = index_step * index_rows
    first = share_rows
    second = share_rows + query_rows

    low = arrived[0:groups, 0:share_rows, :]
    high = arrived[groups:sources, 0:share_rows, :]
    keys[0:remote, 0:half_width] = low[:, :, 0:half_width].reshape(remote, half_width)
    index_k[0:remote, :] = low[:, :, half_width:lanes].reshape(remote, index_width)
    keys[0:remote, half_width : latent_width + 128] = high.reshape(remote, lanes)
    keys[remote:total, 0:latent_width] = own_latent[...]
    keys[remote:total, latent_width : latent_width + 128] = own_rope[...]
    index_k[remote:total, :] = own_index[...]
    keys[:, latent_width + 128 :] = key_bias[...]
    target_rows[...] = jnp.zeros_like(target_rows)
    logit_rows[...] = jnp.zeros_like(logit_rows)

    lane_low = lax.broadcasted_iota(jnp.int32, (query_rows // 2, 128), 1) < 64
    lane_low = lane_low.astype(f32)
    keep_low = lane_low.astype(bf16)[None]
    keep_high = (1.0 - lane_low).astype(bf16)[None]
    tall = arrived.shape[1] - second
    rest = query_rows - tall

    on_token = (
        lax.broadcasted_iota(jnp.int32, (query_rows, 128), 0) // heads
        == lax.broadcasted_iota(jnp.int32, (query_rows, 128), 1)
    ).astype(bf16)
    on_token = jnp.broadcast_to(on_token[None], (step, query_rows, 128))

    def weight_of(c):
        pieces = arrived[
            pl.ds(c * index_step, index_step), second + index_rows : second + tall, 256:384
        ].astype(f32)
        early = lax.broadcasted_iota(jnp.int32, pieces.shape, 2) < 3
        return jnp.concatenate(
            [
                jnp.sum(jnp.where(early, pieces, 0.0), axis=-1, keepdims=True),
                jnp.sum(jnp.where(early, 0.0, pieces), axis=-1, keepdims=True),
            ],
            axis=1,
        )

    @pl.loop(0, sources // step)
    def _(c):
        here = pl.ds(c * step, step)
        score_at = pl.ds(pl.multiple_of(c * score_rows, score_rows), score_rows)
        rows = pl.ds(pl.multiple_of(c * chunk, chunk), chunk)
        rope = arrived[here, second + rest : second + tall, 128:256]
        queries = jnp.concatenate(
            [
                arrived[here, first:second, :],
                jnp.concatenate(
                    [
                        arrived[here, second : second + tall, 0:128],
                        arrived[here, second : second + rest, 128:256],
                    ],
                    axis=1,
                ),
                jnp.concatenate([rope * keep_low, rope * keep_high], axis=1),
                on_token,
            ],
            axis=-1,
        ).reshape(score_rows, latent_width + 256)
        index_q = arrived[here, second : second + index_rows, 256:384].reshape(chunk, index_width)
        weights = weight_of(c)
        best = jnp.full((score_rows, 128), -3e38, f32)
        for k in range(tiles):
            at = slice(k * tile, (k + 1) * tile)
            part = dot_last(queries, keys[at, :])
            scores[score_at, at] = part
            best = jnp.maximum(best, jnp.maximum(part[:, 0:128], part[:, 128:256]))
            act, rate = gelu_pair(dot_last(index_q, index_k[at, :]) * index_scale)
            active[rows, at] = act
            slope[rows, at] = rate
            logit_rows[:, at] += jnp.sum(
                act.reshape(index_step, index_rows, tile) * weights, axis=0
            )
        highest[score_at, :] = best

    @pl.loop(0, sources // step)
    def _(c):
        score_at = pl.ds(pl.multiple_of(c * score_rows, score_rows), score_rows)
        top = jnp.max(highest[score_at, :], axis=1, keepdims=True)
        sums = jnp.zeros((score_rows, 128), f32)
        for k in range(tiles):
            at = slice(k * tile, (k + 1) * tile)
            power = jnp.exp((scores[score_at, at] - top) * score_scale)
            scores[score_at, at] = power
            sums = sums + (power[:, 0:128] + power[:, 128:256])
        weight = 1.0 / ((heads * sources) * jnp.sum(sums, axis=1, keepdims=True))
        weight = weight.reshape(step, query_rows, 1)
        for k in range(tiles):
            at = slice(k * tile, (k + 1) * tile)
            power = scores[score_at, at].reshape(step, query_rows, tile)
            target_rows[:, at] += jnp.sum(power * weight, axis=0)

    def gather(count):
        return (
            lax.broadcasted_iota(jnp.int32, (tokens, tokens * count), 1) // count
            == lax.broadcasted_iota(jnp.int32, (tokens, tokens * count), 0)
        ).astype(f32)

    spread = (
        lax.broadcasted_iota(jnp.int32, (index_rows, tokens), 0) // index_heads
        == lax.broadcasted_iota(jnp.int32, (index_rows, tokens), 1)
    ).astype(bf16)
    logits = dot(gather(index_heads), logit_rows[...], lax.Precision.HIGHEST) + bias[...]
    target = dot(gather(heads), target_rows[...], lax.Precision.HIGHEST)
    likely = jnp.exp(logits - jnp.max(logits, axis=1, keepdims=True))
    predicted = likely / jnp.sum(likely, axis=1, keepdims=True)
    grad_logits = jnp.where(
        bias[...] == 0.0, loss_weight * (predicted - target), 0.0
    ).astype(bf16)
    logit_rows[...] = dot(spread, grad_logits)

    @pl.loop(0, sources // index_step)
    def _(c):
        rows = pl.ds(pl.multiple_of(c * chunk, chunk), chunk)
        weights = weight_of(c) * index_scale
        sums = jnp.zeros((chunk, 128), f32)
        for k in range(tiles):
            at = slice(k * tile, (k + 1) * tile)
            grad = logit_rows[:, at][None]
            product = (
                active[rows, at].reshape(index_step, index_rows, tile) * grad
            ).reshape(chunk, tile)
            sums = sums + (product[:, 0:128] + product[:, 128:256])
            grad_pre[rows, at] = (
                (slope[rows, at].reshape(index_step, index_rows, tile) * (grad * weights))
                .reshape(chunk, tile)
                .astype(bf16)
            )
        turned = jnp.broadcast_to(jnp.sum(sums, axis=1, keepdims=True), (chunk, 128)).T
        turned = turned[0:8]
        turned_high = turned.astype(bf16)
        turned_low = (turned - turned_high.astype(f32)).astype(bf16)
        for i in range(index_step):
            grad_weights[c * index_step + i] = jnp.concatenate([turned_high, turned_low], axis=0)

    grad_queries[...] = dot(grad_pre[...], index_k[...]).astype(bf16)
    turned = (
        arrived[:, second : second + index_rows, 256:384]
        .reshape(sources * index_rows, index_width)
        .astype(f32)
        .T.astype(bf16)
    )
    for k in range(tiles):
        at = slice(k * tile, (k + 1) * tile)
        grad_keys[at, :] = dot(turned, grad_pre[:, at]).T
    small = block // sources
    slots = total // block
    for g in range(groups):
        own = grad_keys[remote + g * 2 * small : remote + (g + 1) * 2 * small, :]
        own = own.reshape(1, 2, small, index_width)
        rest_keys = grad_keys[g * share_rows : (g + 1) * share_rows, :]
        rest_keys = rest_keys.reshape(slots - 1, 2, small, index_width)
        both_keys = jnp.concatenate([own, rest_keys], axis=0)
        for i in range(2):
            shares[i * groups + g] = both_keys[:, i].reshape(block, index_width).astype(bf16)


def last_kernel(groups, index_heads, final, grad_queries, grad_weights, grad_keys):
    sources, _, width = final.shape
    block = grad_weights.shape[1]
    tokens = block // sources
    index_rows = tokens * index_heads
    local_blocks = grad_keys.shape[0] // block
    small = block // sources
    own_rows = local_blocks * small
    second = own_rows + index_rows
    for k in range(sources):
        part = final[k, 0:own_rows, :].astype(f32)
        half, group = k // groups, k % groups
        for j in range(local_blocks):
            at = j * block + group * 2 * small + half * small
            grad_keys[at : at + small, :] = part[j * small : (j + 1) * small]
        grad_queries[k * index_rows : (k + 1) * index_rows, :] = final[
            k, own_rows:second, :
        ].astype(f32)
    together = 128 // index_rows
    first_lane = lax.rem(lax.axis_index("head"), together) * index_rows
    row = lax.broadcasted_iota(jnp.int32, (block, width), 0)
    lane = lax.broadcasted_iota(jnp.int32, (block, width), 1)
    spot = lane - first_lane
    keep = (spot >= 0) & (spot < index_rows) & (lax.div(spot, index_heads) == row % tokens)
    which = lax.broadcasted_iota(jnp.int32, (8, width), 0)
    head = lax.rem(lax.broadcasted_iota(jnp.int32, (8, width), 1), index_heads)
    fold = (which == head).astype(bf16)
    result = jnp.zeros((8, block), f32)
    for i in range(2):
        lines = []
        for k in range(sources):
            whole = final[k, second : second + 16, :].astype(f32)
            lines.append(jnp.broadcast_to(whole[8 * i : 8 * i + 1], (tokens, width)))
        lines = jnp.concatenate(lines, axis=0)
        result = result + dot_last(fold, jnp.where(keep, lines, 0.0).astype(bf16))
    grad_weights[...] = result[0:index_heads]


def exchange(array, axis):
    return lax.all_to_all(array, axis, split_axis=0, concat_axis=0, tiled=True)


def exchange_alone(array, axis, others):
    array, others = lax.optimization_barrier((array, others))
    return lax.optimization_barrier((exchange(array, axis), others))


def pad_lanes(array, width):
    return jnp.pad(array, [(0, 0)] * (array.ndim - 1) + [(0, width - array.shape[-1])])


def body(
    q_latent, q_rope, latent_cache, rope_keys, index_queries, index_weights, index_keys, sel_blocks
):
    head_count = lax.axis_size("head")
    seq_count = lax.axis_size("seq")
    head_index = lax.axis_index("head")
    seq_index = lax.axis_index("seq")
    block, heads, latent_width = q_latent.shape
    rope_width = q_rope.shape[2]
    index_heads, index_width = index_queries.shape[1:]
    slot_count = sel_blocks.shape[1]
    local_blocks = latent_cache.shape[0] // block
    index_scale = index_width ** (-0.5)
    loss_weight = float(slot_count * block)
    groups = head_count // 2
    rows = block // groups
    small = rows // 2
    tokens = block // head_count
    half_width = latent_width // 2
    lanes = half_width + index_width
    remote_slots = slot_count - 1

    later = sel_blocks[:, 1:]
    offsets = later - seq_index * local_blocks
    inside = (later >= 0) & (offsets >= 0) & (offsets < local_blocks)
    wanted = jnp.any(inside, axis=1)
    which = jnp.sum(jnp.where(inside, offsets, 0), axis=1)
    sel_row = lax.dynamic_index_in_dim(sel_blocks, seq_index, 0, keepdims=False)
    slot_valid = sel_row >= 0
    source = jnp.where(slot_valid, sel_row // local_blocks, 0)
    in_vmem = pl.BlockSpec(memory_space=pltpu.VMEM)
    in_smem = pl.BlockSpec(memory_space=pltpu.SMEM)
    in_place = pl.BlockSpec(memory_space=pl.ANY)

    packed = pl.pallas_call(
        functools.partial(first_kernel, groups),
        out_shape=jax.ShapeDtypeStruct((seq_count * rows, lanes), bf16),
        in_specs=[in_vmem] + [in_place] * 3,
        out_specs=in_vmem,
        scratch_shapes=[
            pltpu.VMEM((local_blocks, rows, latent_width), bf16),
            pltpu.VMEM((local_blocks, rows, index_width), bf16),
            pltpu.VMEM((rope_width, local_blocks * block), bf16),
            pltpu.VMEM((local_blocks * block, 2 * rope_width), bf16),
            pltpu.SemaphoreType.DMA((1 + 2 * local_blocks,)),
        ],
        compiler_params=pltpu.CompilerParams(vmem_limit_bytes=60 * 1024 * 1024),
    )(sel_blocks.T, latent_cache, rope_keys.T, index_keys)
    fetched = exchange(packed.reshape(seq_count, rows, lanes), "seq")

    share_rows = remote_slots * rows
    query_rows = tokens * heads
    index_rows = tokens * index_heads
    latent_parts = q_latent.reshape(block * heads, latent_width)
    rope_parts = q_rope.reshape(head_count, 2, query_rows // 2, rope_width)
    rope_parts = jnp.concatenate([rope_parts[:, 0], rope_parts[:, 1]], axis=-1)
    rope_parts = rope_parts.reshape(head_count * query_rows // 2, 2 * rope_width)
    index_parts = index_queries.reshape(head_count * index_rows, index_width)
    weight_parts = index_weights.reshape(head_count, 2, index_rows // 2, 1)
    high = lax.reduce_precision(weight_parts, 8, 7)
    middle = lax.reduce_precision(weight_parts - high, 8, 7)
    low = weight_parts - high - middle
    pieces = jnp.concatenate([high, middle, low], axis=-1).astype(bf16)
    pieces = pad_lanes(jnp.concatenate([pieces[:, 0], pieces[:, 1]], axis=-1), 128)
    pieces = pieces.reshape(head_count * index_rows // 2, 128)
    packed_rows = share_rows + query_rows + index_rows + index_rows // 2
    own = slice((local_blocks - 1) * block, local_blocks * block)
    own_rope = jnp.concatenate([rope_keys[own], rope_keys[own]], axis=-1)
    total = slot_count * block
    token_at = head_index * tokens + jnp.arange(tokens)
    remote_mask = jnp.broadcast_to(
        slot_valid[None, 1:, None], (groups, remote_slots, rows)
    ).reshape(-1)
    key_mask = jnp.concatenate(
        [
            jnp.broadcast_to(remote_mask, (tokens, remote_mask.shape[0])),
            jnp.arange(block)[None, :] <= token_at[:, None],
        ],
        axis=1,
    )
    bias = jnp.where(key_mask, 0.0, -1e30).astype(f32)
    key_bias = pad_lanes(bias.T.astype(bf16), 128)
    outgoing = pl.pallas_call(
        functools.partial(second_kernel, local_blocks),
        out_shape=jax.ShapeDtypeStruct((head_count, packed_rows, lanes), bf16),
        in_specs=[in_smem] + [in_vmem] * 5,
        out_specs=in_vmem,
        compiler_params=pltpu.CompilerParams(vmem_limit_bytes=24 * 1024 * 1024),
    )(sel_blocks.T, fetched, latent_parts, rope_parts, index_parts, pieces)
    found = (source[1:][None, :] == jnp.arange(seq_count)[:, None]) & slot_valid[1:][None, :]
    slot_of = jnp.sum(jnp.where(found, jnp.arange(1, slot_count)[None, :], 0), axis=1)
    owner = wanted[:, None] & (which[:, None] == jnp.arange(local_blocks)[None, :])
    owner = owner.astype(f32)
    arrived, (bias, key_bias, own_latent, own_rope, own_index, slot_of, owner) = exchange_alone(
        outgoing,
        "head",
        (bias, key_bias, latent_cache[own], own_rope, index_keys[own], slot_of, owner),
    )

    all_rows = head_count * index_rows
    grad_queries, grad_weights, shares = pl.pallas_call(
        functools.partial(compute_kernel, share_rows, loss_weight, index_scale),
        out_shape=(
            jax.ShapeDtypeStruct((all_rows, index_width), bf16),
            jax.ShapeDtypeStruct((head_count, 16, 128), bf16),
            jax.ShapeDtypeStruct((head_count, slot_count * small, index_width), bf16),
        ),
        in_specs=[in_vmem] * 6,
        out_specs=(in_vmem, in_vmem, in_vmem),
        scratch_shapes=[
            pltpu.VMEM((total, latent_width + 256), bf16),
            pltpu.VMEM((total, index_width), bf16),
            pltpu.VMEM((head_count * query_rows, total), f32),
            pltpu.VMEM((head_count * query_rows, 128), f32),
            pltpu.VMEM((all_rows, total), f32),
            pltpu.VMEM((all_rows, total), f32),
            pltpu.VMEM((all_rows, total), bf16),
            pltpu.VMEM((index_rows, total), f32),
            pltpu.VMEM((query_rows, total), f32),
            pltpu.VMEM((total, index_width), f32),
        ],
        compiler_params=pltpu.CompilerParams(vmem_limit_bytes=36 * 1024 * 1024),
    )(arrived, bias, key_bias, own_latent, own_rope, own_index)

    collected, (grad_queries, grad_weights, slot_of, owner) = exchange_alone(
        shares, "head", (grad_queries, grad_weights, slot_of, owner)
    )
    summed = jnp.sum(collected.astype(f32), axis=0).reshape(slot_count, small, index_width)
    own_sum = summed[0]
    returned, (own_sum, grad_queries, grad_weights, owner) = exchange_alone(
        jnp.take(summed, slot_of, axis=0).astype(bf16),
        "seq",
        (own_sum, grad_queries, grad_weights, owner),
    )
    owned = jnp.sum(owner[:, :, None, None] * returned.astype(f32)[:, None], axis=0)
    owned = owned.at[local_blocks - 1].add(own_sum)

    own_rows = local_blocks * small
    last = jnp.concatenate(
        [
            jnp.broadcast_to(
                owned.reshape(own_rows, index_width).astype(bf16), (head_count, own_rows, index_width)
            ),
            grad_queries.reshape(head_count, index_rows, index_width),
            grad_weights,
        ],
        axis=1,
    )
    final, _ = exchange_alone(last, "head", ())
    out_queries, out_weights, grad_keys = pl.pallas_call(
        functools.partial(last_kernel, groups, index_heads),
        out_shape=(
            jax.ShapeDtypeStruct((block * index_heads, index_width), f32),
            jax.ShapeDtypeStruct((index_heads, block), f32),
            jax.ShapeDtypeStruct((local_blocks * block, index_width), f32),
        ),
        in_specs=[in_vmem],
        out_specs=(in_vmem, in_vmem, in_vmem),
        compiler_params=pltpu.CompilerParams(vmem_limit_bytes=16 * 1024 * 1024),
    )(final)
    return (out_queries.reshape(block, index_heads, index_width), out_weights.T, grad_keys)


def solution(mesh):
    placed = (
        P("seq", "head", None),
        P("seq", "head", None),
        P("seq", None),
        P("seq", None),
        P("seq", "head", None),
        P("seq", "head"),
        P("seq", None),
        P(),
    )
    return jax.shard_map(
        body,
        mesh=mesh,
        in_specs=placed,
        out_specs=(P("seq", "head", None), P("seq", "head"), P("seq", None)),
        check_vma=False,
    )
```

time: 686 us -> 168 us (0.24)
  waiting for transfers between devices: 480 us -> 18.2 us
  matrix products: 18.3 us -> 0 us
  Pallas kernels: 0 us -> 16.8 us
  between operations: 14.3 us -> 0.9 us
  other arithmetic: 15.5 us -> 2.25 us
  blocking collectives: 113 us -> 102 us
  starting transfers between devices: 24.8 us -> 15.5 us
  local copies, waits for them, and re-layouts: 19.8 us -> 11.3 us
    all_to_all x3 -> x1, waiting for transfers between devices: 265 us -> 18.2 us  [exchange(): return lax.all_to_all(array, axis, split_axis=0, concat_axis=0, tiled=True)]
    psum x2 -> x0, waiting for transfers between devices: 215 us -> none  [the longest x1 112 us: body(): target, logits = lax.psum((part_target, part_logits), 'head')]
    dot_general x10 -> x0, matrix products: 18.3 us -> none  [the longest x1 4.76 us: body(): jnp.einsum('tid,jkd->tijk', index_queries, sel_index, preferred_element_t...]
    pallas_call x0 -> x4, Pallas kernels: none -> 16.8 us  [the longest x1 12.1 us: body(): pl.pallas_call(functools.partial(compute_kernel, share_rows, loss_weight,...]
    all_to_all x1 -> x4, blocking collectives: 113 us -> 102 us  [exchange(): return lax.all_to_all(array, axis, split_axis=0, concat_axis=0, tiled=True)]
    all_to_all x3 -> x1, starting transfers between devices: 24.3 us -> 15.5 us  [exchange(): return lax.all_to_all(array, axis, split_axis=0, concat_axis=0, tiled=True)]
    reduce_sum x4, other arithmetic: 9.18 us -> 0.9 us  [the longest x1 0.6 us: body(): jnp.sum(jnp.where(found, jnp.arange(1, slot_count)[None, :], 0), axis=1)]
  transfers between devices with their start and end apart: 5 -> 1, of which waited for: 5 -> 1; matrix products, arithmetic and copies ran while one was open for 3% -> 6% of each run, Pallas kernels for 0% -> 0%
where the time goes in v2:
time: 168 us; the launch traced here: 167 us
  blocking collectives  102 us (61%)
  waiting for transfers between devices  18.2 us (11%)
  Pallas kernels  16.8 us (10%)
  starting transfers between devices  15.5 us (9%)
  local copies, waits for them, and re-layouts  11.3 us (7%)
  other arithmetic  2.25 us (1%)
    all_to_all x4, blocking collectives, exchange(): return lax.all_to_all(array, axis, split_axis=0, concat_axis=0, tiled=True)  102 us
    all_to_all x1, waiting for transfers between devices, exchange(): return lax.all_to_all(array, axis, split_axis=0, concat_axis=0, tiled=True)  18.2 us
    all_to_all x1, starting transfers between devices, exchange(): return lax.all_to_all(array, axis, split_axis=0, concat_axis=0, tiled=True)  15.5 us
    pallas_call x1, Pallas kernels, body(): pl.pallas_call(functools.partial(compute_kernel, share_rows, loss_weight,...  12.1 us
    unnamed x16, local copies, waits for them, and re-layouts  5.14 us
  transfers between devices with their start and end apart: 1, of which 1 were waited for; matrix products, arithmetic and copies ran while one was open for 6% of the time, Pallas kernels for 0%

profile of v2, /device:TPU:6, one launch (start us, length us, event | category | flops | bytes accessed | tf_op | source)
XLA Modules:
  0.0 166.8 jit_solution(14413429545343440061)
XLA Ops:
  0.6 0.0 copy-start.2
  0.6 0.0 copy-start.3
  0.7 0.0 copy-start.1
  0.7 2.8 %shard_map.103 = bf16[512,384]{1,0:T(8,128)(2,1)} custom-call(s32[16,32]{1,0:T(8,128)} %bitcast.25, bf16[512,512]{1,0:T(8,128)(2,1)} %latent.1, bf16[64,512]{1,0:T(8,128)(2,1)} %bitcast.34, bf16[512,128]{1,0:T(8,128)(2,1)} %index.1), custom_call_target="tpu_custom_call" | custom-call | tf_op jit(solution)/shard_map/pallas_call | solution.py:411
  3.5 15.5 %all-to-all-start = ((bf16[32,16,384]{2,1,0:T(8,128)(2,1)}), bf16[32,16,384]{2,1,0:T(8,128)(2,1)S(1)}, u32[]{:S(2)}, u32[]{:S(2)}) async-start(bf16[32,16,384]{2,1,0:T(8,128)(2,1)} %bitcast.29), calls=%async_computation | async-start | bytes 786432 | tf_op jit(solution)/shard_map/all_to_all | solution.py:365
  19.0 0.9 dynamic-slice_reduce_fusion
  19.9 0.7 slice.64
  20.6 0.8 slice.65.own_index
  21.3 0.9 slice.63.own_latent
  22.3 0.1 iota_compare_fusion.2
  22.4 0.1 slice.62
  22.4 0.1 slice.66
  22.5 0.1 broadcast_in_dim.59
  22.6 0.1 reshape.162
  22.7 0.1 copy.49
  22.8 0.8 copy.42
  23.6 0.1 reshape.145
  23.8 0.2 copy.50
  24.0 0.4 copy.46
  24.4 1.8 %copy.41 = bf16[128,8,64]{2,1,0:T(8,128)(2,1)} copy(bf16[128,8,64]{0,2,1:T(8,128)(2,1)} %param.11) | data formatting | bytes 262144 | tf_op args[1]
  26.2 0.1 convert_bitcast_fusion
  26.4 0.1 pad.11.key_bias
  26.5 0.0 copy-done.2
  26.6 0.1 pad_maximum_fusion.2.own_rope
  26.6 1.0 fusion.7
  27.6 0.1 pad_maximum_fusion.1.rope
  27.8 0.6 select_reduce_fusion.1
  28.4 0.7 fusion.2
  29.0 18.2 %all-to-all-done.fetched = bf16[32,16,384]{2,1,0:T(8,128)(2,1)S(1)} async-done(((bf16[32,16,384]{2,1,0:T(8,128)(2,1)}), bf16[32,16,384]{2,1,0:T(8,128)(2,1)S(1)}, u32[]{:S(2)}, u32[]{:S(2)}) %all-to-all-start) | async-done | bytes 393248 | tf_op jit(solution)/shard_map/all_to_all | solution.py:365
  47.2 0.0 copy-done.3
  47.2 0.0 copy-done.1
  47.2 1.1 shard_map.104
  48.3 58.2 %all_to_all.25.arrived = bf16[16,352,384]{2,1,0:T(8,128)(2,1)} all-to-all(bf16[16,352,384]{2,1,0:T(8,128)(2,1)S(1)} %shard_map.104), channel_id=1, replica_groups=mesh['head'=16,'seq'=32] {'head'}, dimensions={0} | all-to-all | bytes 8650752 | tf_op jit(solution)/shard_map/all_to_all | solution.py:365
  106.5 0.0 copy-start.5
  106.5 0.0 copy-start.4
  106.5 0.3 copy.48.bias
  106.8 0.0 copy-start
  106.8 2.2 %copy-done = bf16[16,352,384]{2,1,0:T(8,128)(2,1)S(1)} copy-done((bf16[16,352,384]{2,1,0:T(8,128)(2,1)S(1)}, bf16[16,352,384]{2,1,0:T(8,128)(2,1)}, u32[]{:S(2)}) %copy-start) | copy-done | bytes 4325400
  109.0 12.1 %shard_map.105 = (bf16[512,128]{1,0:T(8,128)(2,1)S(1)}, bf16[16,16,128]{2,1,0:T(8,128)(2,1)S(1)}, bf16[16,128,128]{2,1,0:T(8,128)(2,1)S(1)}) custom-call(bf16[16,352,384]{2,1,0:T(8,128)(2,1)S(1)} %copy-done, f32[8,2048]{1,0:T(8,128)S(1)} %copy.48.bias, bf16[2048,128]{1,0:T(8,128)(2,1)S(1)} %pad.11.key_bias, bf16[128,512]{1,0:T(8,128)(2,1)S(1)} %slice.63.own_latent, ...), custom_call_target="tpu_custom_call" | custom-call | tf_op jit(solution)/shard_map/pallas_call | solution.py:477
  121.1 13.9 %all_to_all.26 = bf16[16,128,128]{2,1,0:T(8,128)(2,1)S(1)} all-to-all(bf16[16,128,128]{2,1,0:T(8,128)(2,1)S(1)} %get-tuple-element.76), channel_id=1, replica_groups=mesh['head'=16,'seq'=32] {'head'}, dimensions={0} | all-to-all | bytes 1048576 | tf_op jit(solution)/shard_map/all_to_all | solution.py:365
  135.0 0.0 copy-done.5
  135.0 0.1 convert_reduce_fusion
  135.1 0.6 gather_fusion
  135.7 0.1 select_convert_fusion
  135.8 17.7 %all_to_all.27 = bf16[32,8,128]{2,1,0:T(8,128)(2,1)S(1)} all-to-all(bf16[32,8,128]{2,1,0:T(8,128)(2,1)S(1)} %select_convert_fusion), channel_id=1, replica_groups=mesh['head'=16,'seq'=32] {'seq'}, dimensions={0} | all-to-all | bytes 131072 | tf_op jit(solution)/shard_map/all_to_all | solution.py:365
  153.5 0.0 copy-done.4
  153.5 0.2 multiply_reduce_fusion
  153.8 12.1 %all_to_all.28.final = bf16[16,80,128]{2,1,0:T(8,128)(2,1)S(1)} all-to-all(bf16[16,80,128]{2,1,0:T(8,128)(2,1)S(1)} %pad_maximum_fusion), channel_id=1, replica_groups=mesh['head'=16,'seq'=32] {'head'}, dimensions={0} | all-to-all | bytes 655360 | tf_op jit(solution)/shard_map/all_to_all | solution.py:365
  165.9 0.9 shard_map.106
  (22 shorter events, 0.2 us)
Async XLA Ops:
  0.6 25.9 %copy-start.2 = (s32[32,16]{0,1:T(8,128)S(1)}, s32[32,16]{0,1:T(8,128)}, u32[]{:S(2)}) copy-start(s32[32,16]{0,1:T(8,128)} %param.17) | copy-start | bytes 6148
  0.6 46.6 %copy-start.3 = (bf16[128,4,128]{2,1,0:T(4,128)(2,1)S(1)}, bf16[128,4,128]{2,1,0:T(4,128)(2,1)}, u32[]{:S(2)}) copy-start(bf16[128,4,128]{2,1,0:T(4,128)(2,1)} %param.14) | copy-start | bytes 393220
  0.7 46.5 %copy-start.1 = (bf16[128,8,512]{2,1,0:T(8,128)(2,1)S(1)}, bf16[128,8,512]{2,1,0:T(8,128)(2,1)}, u32[]{:S(2)}) copy-start(bf16[128,8,512]{2,1,0:T(8,128)(2,1)} %param.10) | copy-start | bytes 3145732
  3.5 43.7 %all-to-all-start = ((bf16[32,16,384]{2,1,0:T(8,128)(2,1)}), bf16[32,16,384]{2,1,0:T(8,128)(2,1)S(1)}, u32[]{:S(2)}, u32[]{:S(2)}) async-start(bf16[32,16,384]{2,1,0:T(8,128)(2,1)} %bitcast.29), calls=%async_computation | async-start | bytes 786432 | tf_op jit(solution)/shard_map/all_to_all | solution.py:365
  106.5 28.5 %copy-start.5 = (s32[32]{0:T(128)S(1)}, s32[32]{0:T(128)}, u32[]{:S(2)}) copy-start(s32[32]{0:T(128)} %select_reduce_fusion.1) | copy-start | bytes 388
  106.5 47.0 %copy-start.4 = (f32[32,4]{1,0:T(8,128)S(1)}, f32[32,4]{1,0:T(8,128)}, u32[]{:S(2)}) copy-start(f32[32,4]{1,0:T(8,128)} %fusion.2) | copy-start | bytes 1540
  106.8 2.2 %copy-start = (bf16[16,352,384]{2,1,0:T(8,128)(2,1)S(1)}, bf16[16,352,384]{2,1,0:T(8,128)(2,1)}, u32[]{:S(2)}) copy-start(bf16[16,352,384]{2,1,0:T(8,128)(2,1)} %all_to_all.25.arrived) | copy-start | bytes 12976132

commit v3 on v2

--- a/solution.py
+++ b/solution.py
@@ -35,7 +35,7 @@
 
 
 def first_kernel(
-    groups, sel_turned, latent, rope_turned, index, packed, wide, narrow, turned, rope, sems
+    groups, sel_turned, latent, rope_turned, index, packed, own_rope, wide, narrow, turned, rope, sems
 ):
     slots, destinations = sel_turned.shape
     local_blocks, rows, latent_width = wide.shape
@@ -82,56 +82,116 @@
                 axis=1,
             )
         )
+    own_rope[...] = rope[(local_blocks - 1) * block :, :]
     share = jnp.concatenate(parts, axis=0)
     packed[...] = dot(pick, share).astype(bf16)
 
 
-def second_kernel(local_blocks, sel, fetched, latent, rope, index, weight, outgoing):
-    destinations = outgoing.shape[0]
-    slots = sel.shape[0]
-    rows, lanes = fetched.shape[1:]
-    here = lax.axis_index("seq")
-    query_rows = latent.shape[0] // destinations
-    index_rows = index.shape[0] // destinations
-    rope_rows = rope.shape[0] // destinations
-    weight_rows = weight.shape[0] // destinations
-    first = (slots - 1) * rows
-    second = first + query_rows
+def place(side):
+    head = lax.axis_index("head")
+    core = lax.rem(lax.axis_index("seq"), 2)
+    x, y = lax.div(head, side), lax.rem(head, side)
+    return core, jnp.where(core == 0, y, x), jnp.where(core == 0, x, y)
+
+
+def head_at(side, core, u, v):
+    return jnp.where(core == 0, v * side + u, u * side + v)
+
+
+def query_kernel(
+    side, groups, sel_turned, latent, rope, index, weight, out0, out1, out2, out3, bias, key_bias
+):
+    outs = (out0, out1, out2, out3)
+    chunks = side * side
+    slots, destinations = sel_turned.shape
+    query_rows = latent.shape[0] // chunks
+    lanes = out0.shape[2]
+    index_rows = index.shape[0] // chunks
+    rope_rows = rope.shape[0] // chunks
+    weight_rows = weight.shape[0] // chunks
     tall = index_rows + weight_rows
     rest = query_rows - tall
+    core, u, _ = place(side)
+    for k in range(side):
+        out = outs[k]
+        for v in range(side):
+            chunk = head_at(side, core, lax.rem(u + k, side), v)
+
+            def at(count, size, begin=0):
+                return pl.ds(pl.multiple_of(chunk * count + begin, 16), size)
+
+            out[v, 0:query_rows, :] = latent[at(query_rows, query_rows), 0:lanes]
+            out[v, query_rows : query_rows + tall, 0:128] = latent[at(query_rows, tall), lanes:]
+            out[v, query_rows : query_rows + rest, 128:256] = latent[
+                at(query_rows, rest, tall), lanes:
+            ]
+            out[v, query_rows + rest : query_rows + tall, 128:256] = rope[
+                at(rope_rows, rope_rows), :
+            ]
+            out[v, query_rows : query_rows + index_rows, 256:384] = index[
+                at(index_rows, index_rows), :
+            ]
+            out[v, query_rows + index_rows : query_rows + tall, 256:384] = weight[
+                at(weight_rows, weight_rows), :
+            ]
+    tokens, total = bias.shape
+    rows = total // slots // groups
+    share_rows = (slots - 1) * rows
+    remote = groups * share_rows
+    here = lax.axis_index("seq")
+    head = lax.axis_index("head")
+    table = sel_turned[...].astype(f32)
+    pick = lax.broadcasted_iota(jnp.int32, (tokens, destinations), 1) == here
+    valid = (dot_last(pick.astype(f32), table) >= 0).astype(f32)
+    key = lax.broadcasted_iota(jnp.int32, (slots, total), 1)
+    slot = lax.div(lax.rem(key, share_rows), rows) + 1
+    mark = (slot == lax.broadcasted_iota(jnp.int32, (slots, total), 0)).astype(f32)
+    key = lax.broadcasted_iota(jnp.int32, (tokens, total), 1)
+    token = lax.broadcasted_iota(jnp.int32, (tokens, total), 0) + head * tokens
+    good = ((key < remote) & (dot(valid, mark) > 0)) | ((key >= remote) & (key - remote <= token))
+    masks = jnp.where(good, 0.0, -1e30)
+    bias[...] = masks
+    tall_masks = jnp.concatenate([masks, jnp.zeros((128 - tokens, total), f32)], axis=0)
+    key_bias[...] = tall_masks.T.astype(bf16)
+
+
+def stage_kernel(local_blocks, sel, fetched, in0, in1, in2, in3, outgoing):
+    parts = (in0, in1, in2, in3)
+    slots = sel.shape[0]
+    rows = fetched.shape[1]
+    height = in0.shape[1]
+    here = lax.axis_index("seq")
+    first = (slots - 1) * rows
     for j in range(1, slots):
-        source = lax.div(jnp.maximum(sel[j, here], 0), local_blocks)
-        piece = fetched[source]
-        for k in range(destinations):
-            outgoing[k, (j - 1) * rows : j * rows, :] = piece
-    for k in range(destinations):
-        at = k * query_rows
-        outgoing[k, first:second, :] = latent[at : at + query_rows, 0:lanes]
-        outgoing[k, second : second + tall, 0:128] = latent[at : at + tall, lanes:]
-        outgoing[k, second : second + rest, 128:256] = latent[
-            at + tall : at + query_rows, lanes:
-        ]
-        outgoing[k, second + rest : second + tall, 128:256] = rope[
-            k * rope_rows : (k + 1) * rope_rows, :
-        ]
-        outgoing[k, second : second + index_rows, 256:384] = index[
-            k * index_rows : (k + 1) * index_rows, :
-        ]
-        outgoing[k, second + index_rows : second + tall, 256:384] = weight[
-            k * weight_rows : (k + 1) * weight_rows, :
-        ]
+        piece = fetched[lax.div(jnp.maximum(sel[j, here], 0), local_blocks)]
+        for v in range(len(parts)):
+            outgoing[v, (j - 1) * rows : j * rows, :] = piece
+    for k in range(len(parts)):
+        for v in range(len(parts)):
+            at = first + k * height
+            outgoing[v, at : at + height, :] = parts[k][v]
+
+
+def spread_kernel(staged, outgoing):
+    side, height, _ = outgoing.shape
+    share = height // side
+    for v in range(side):
+        piece = staged[v, 0:share, :]
+        for u in range(side):
+            outgoing[u, v * share : (v + 1) * share, :] = piece
 
 
 def compute_kernel(
-    share_rows,
     loss_weight,
     index_scale,
-    arrived,
+    index_heads,
+    staged,
+    spread_shares,
     bias,
     key_bias,
-    own_latent,
     own_rope,
-    own_index,
+    latent,
+    index,
     grad_queries,
     grad_weights,
     shares,
@@ -145,88 +205,116 @@
     logit_rows,
     target_rows,
     grad_keys,
+    sems,
 ):
-    sources, _, lanes = arrived.shape
+    sources, share_rows, lanes = spread_shares.shape
+    step = staged.shape[0]
     groups = sources // 2
     tokens, total = bias.shape
-    block, latent_width = own_latent.shape
+    block = own_rope.shape[0]
+    latent_width = latent.shape[1]
     half_width = latent_width // 2
-    index_width = own_index.shape[1]
+    index_width = index.shape[1]
     query_rows = target_rows.shape[0]
     heads = query_rows // tokens
     index_rows = logit_rows.shape[0]
-    index_heads = index_rows // tokens
     remote = groups * share_rows
     tile = 2 * 128
     tiles = total // tile
-    step = 4
     score_rows = step * query_rows
-    index_step = step
-    chunk = index_step * index_rows
-    first = share_rows
-    second = share_rows + query_rows
-
-    low = arrived[0:groups, 0:share_rows, :]
-    high = arrived[groups:sources, 0:share_rows, :]
-    keys[0:remote, 0:half_width] = low[:, :, 0:half_width].reshape(remote, half_width)
-    index_k[0:remote, :] = low[:, :, half_width:lanes].reshape(remote, index_width)
-    keys[0:remote, half_width : latent_width + 128] = high.reshape(remote, lanes)
-    keys[remote:total, 0:latent_width] = own_latent[...]
+    chunk = step * index_rows
+    height = (staged.shape[1] - share_rows) // step
+    tall = height - query_rows
+    rest = query_rows - tall
+    core, own_u, _ = place(step)
+    own_rows = pl.ds(latent.shape[0] - block, block)
+    copies = (
+        pltpu.make_async_copy(
+            latent.at[own_rows], keys.at[pl.ds(remote, block), pl.ds(0, latent_width)], sems.at[0]
+        ),
+        pltpu.make_async_copy(index.at[own_rows], index_k.at[pl.ds(remote, block)], sems.at[1]),
+    )
+    for copy in copies:
+        copy.start()
+
+    for g in range(groups):
+        at = slice(g * share_rows, (g + 1) * share_rows)
+        x, y = g // step, g % step
+        low = jnp.where(core == 0, y * step + x, x * step + y)
+        x = x + step // 2
+        high = jnp.where(core == 0, y * step + x, x * step + y)
+        keys[at, 0:half_width] = spread_shares[low, :, 0:half_width]
+        index_k[at, :] = spread_shares[low, :, half_width:]
+        keys[at, half_width : latent_width + 128] = spread_shares[high]
     keys[remote:total, latent_width : latent_width + 128] = own_rope[...]
-    index_k[remote:total, :] = own_index[...]
     keys[:, latent_width + 128 :] = key_bias[...]
     target_rows[...] = jnp.zeros_like(target_rows)
     logit_rows[...] = jnp.zeros_like(logit_rows)
+    for copy in copies:
+        copy.wait()
 
     lane_low = lax.broadcasted_iota(jnp.int32, (query_rows // 2, 128), 1) < 64
     lane_low = lane_low.astype(f32)
-    keep_low = lane_low.astype(bf16)[None]
-    keep_high = (1.0 - lane_low).astype(bf16)[None]
-    tall = arrived.shape[1] - second
-    rest = query_rows - tall
+    keep_low = lane_low.astype(bf16)
+    keep_high = (1.0 - lane_low).astype(bf16)
 
     on_token = (
         lax.broadcasted_iota(jnp.int32, (query_rows, 128), 0) // heads
         == lax.broadcasted_iota(jnp.int32, (query_rows, 128), 1)
     ).astype(bf16)
-    on_token = jnp.broadcast_to(on_token[None], (step, query_rows, 128))
-
-    def weight_of(c):
-        pieces = arrived[
-            pl.ds(c * index_step, index_step), second + index_rows : second + tall, 256:384
-        ].astype(f32)
-        early = lax.broadcasted_iota(jnp.int32, pieces.shape, 2) < 3
-        return jnp.concatenate(
-            [
-                jnp.sum(jnp.where(early, pieces, 0.0), axis=-1, keepdims=True),
-                jnp.sum(jnp.where(early, 0.0, pieces), axis=-1, keepdims=True),
-            ],
-            axis=1,
-        )
+
+    def queries_of(v):
+        pieces = []
+        for k in range(step):
+            at = share_rows + k * height
+            below = at + query_rows
+            rope = staged[v, below + rest : below + tall, 128:256]
+            pieces.append(
+                jnp.concatenate(
+                    [
+                        staged[v, at:below, :],
+                        jnp.concatenate(
+                            [
+                                staged[v, below : below + tall, 0:128],
+                                staged[v, below : below + rest, 128:256],
+                            ],
+                            axis=0,
+                        ),
+                        jnp.concatenate([rope * keep_low, rope * keep_high], axis=0),
+                        on_token,
+                    ],
+                    axis=1,
+                )
+            )
+        return jnp.concatenate(pieces, axis=0)
+
+    def index_queries_of(v):
+        pieces = []
+        for k in range(step):
+            below = share_rows + k * height + query_rows
+            pieces.append(staged[v, below : below + index_rows, 256:384])
+        return jnp.concatenate(pieces, axis=0)
+
+    def weights_of(v):
+        columns = []
+        for k in range(step):
+            below = share_rows + k * height + query_rows
+            pieces = staged[v, below + index_rows : below + tall, 256:384].astype(f32)
+            early = lax.broadcasted_iota(jnp.int32, pieces.shape, 1) < 3
+            columns.append(jnp.sum(jnp.where(early, pieces, 0.0), axis=1, keepdims=True))
+            columns.append(jnp.sum(jnp.where(early, 0.0, pieces), axis=1, keepdims=True))
+        return jnp.concatenate(columns, axis=0).reshape(step, index_rows, 1)
+
+    def source_of(v, k):
+        return head_at(step, core, lax.rem(own_u + step - k, step), v)
 
     @pl.loop(0, sources // step)
     def _(c):
-        here = pl.ds(c * step, step)
         score_at = pl.ds(pl.multiple_of(c * score_rows, score_rows), score_rows)
         rows = pl.ds(pl.multiple_of(c * chunk, chunk), chunk)
-        rope = arrived[here, second + rest : second + tall, 128:256]
-        queries = jnp.concatenate(
-            [
-                arrived[here, first:second, :],
-                jnp.concatenate(
-                    [
-                        arrived[here, second : second + tall, 0:128],
-                        arrived[here, second : second + rest, 128:256],
-                    ],
-                    axis=1,
-                ),
-                jnp.concatenate([rope * keep_low, rope * keep_high], axis=1),
-                on_token,
-            ],
-            axis=-1,
-        ).reshape(score_rows, latent_width + 256)
-        index_q = arrived[here, second : second + index_rows, 256:384].reshape(chunk, index_width)
-        weights = weight_of(c)
+        queries = queries_of(c)
+        index_q = index_queries_of(c)
+        weights = weights_of(c)
         best = jnp.full((score_rows, 128), -3e38, f32)
         for k in range(tiles):
             at = slice(k * tile, (k + 1) * tile)
@@ -237,7 +325,7 @@
             active[rows, at] = act
             slope[rows, at] = rate
             logit_rows[:, at] += jnp.sum(
-                act.reshape(index_step, index_rows, tile) * weights, axis=0
+                act.reshape(step, index_rows, tile) * weights, axis=0
             )
         highest[score_at, :] = best
 
@@ -277,37 +365,37 @@
     ).astype(bf16)
     logit_rows[...] = dot(spread, grad_logits)
 
-    @pl.loop(0, sources // index_step)
+    @pl.loop(0, sources // step)
     def _(c):
         rows = pl.ds(pl.multiple_of(c * chunk, chunk), chunk)
-        weights = weight_of(c) * index_scale
+        weights = weights_of(c) * index_scale
         sums = jnp.zeros((chunk, 128), f32)
         for k in range(tiles):
             at = slice(k * tile, (k + 1) * tile)
             grad = logit_rows[:, at][None]
             product = (
-                active[rows, at].reshape(index_step, index_rows, tile) * grad
+                active[rows, at].reshape(step, index_rows, tile) * grad
             ).reshape(chunk, tile)
             sums = sums + (product[:, 0:128] + product[:, 128:256])
             grad_pre[rows, at] = (
-                (slope[rows, at].reshape(index_step, index_rows, tile) * (grad * weights))
+                (slope[rows, at].reshape(step, index_rows, tile) * (grad * weights))
                 .reshape(chunk, tile)
                 .astype(bf16)
             )
         turned = jnp.broadcast_to(jnp.sum(sums, axis=1, keepdims=True), (chunk, 128)).T
-        turned = turned[0:8]
-        turned_high = turned.astype(bf16)
-        turned_low = (turned - turned_high.astype(f32)).astype(bf16)
-        for i in range(index_step):
-            grad_weights[c * index_step + i] = jnp.concatenate([turned_high, turned_low], axis=0)
-
-    grad_queries[...] = dot(grad_pre[...], index_k[...]).astype(bf16)
-    turned = (
-        arrived[:, second : second + index_rows, 256:384]
-        .reshape(sources * index_rows, index_width)
-        .astype(f32)
-        .T.astype(bf16)
-    )
+        for k in range(step):
+            own = turned[0:8] if k == 0 else pltpu.roll(turned[0:8], 128 - k * index_rows, 1)
+            own_high = own.astype(bf16)
+            own_low = (own - own_high.astype(f32)).astype(bf16)
+            grad_weights[source_of(c, k)] = jnp.concatenate([own_high, own_low], axis=0)
+
+    result = dot(grad_pre[...], index_k[...]).astype(bf16)
+    for v in range(step):
+        for k in range(step):
+            at = (v * step + k) * index_rows
+            grad_queries[source_of(v, k)] = result[at : at + index_rows]
+    turned = jnp.concatenate([index_queries_of(v) for v in range(step)], axis=0)
+    turned = turned.astype(f32).T.astype(bf16)
     for k in range(tiles):
         at = slice(k * tile, (k + 1) * tile)
         grad_keys[at, :] = dot(turned, grad_pre[:, at]).T
@@ -341,12 +429,9 @@
         grad_queries[k * index_rows : (k + 1) * index_rows, :] = final[
             k, own_rows:second, :
         ].astype(f32)
-    together = 128 // index_rows
-    first_lane = lax.rem(lax.axis_index("head"), together) * index_rows
     row = lax.broadcasted_iota(jnp.int32, (block, width), 0)
     lane = lax.broadcasted_iota(jnp.int32, (block, width), 1)
-    spot = lane - first_lane
-    keep = (spot >= 0) & (spot < index_rows) & (lax.div(spot, index_heads) == row % tokens)
+    keep = (lane < index_rows) & (lax.div(lane, index_heads) == row % tokens)
     which = lax.broadcasted_iota(jnp.int32, (8, width), 0)
     head = lax.rem(lax.broadcasted_iota(jnp.int32, (8, width), 1), index_heads)
     fold = (which == head).astype(bf16)
@@ -361,13 +446,43 @@
     grad_weights[...] = result[0:index_heads]
 
 
-def exchange(array, axis):
-    return lax.all_to_all(array, axis, split_axis=0, concat_axis=0, tiled=True)
-
-
-def exchange_alone(array, axis, others):
+def exchange(array, axis, groups=None):
+    return lax.all_to_all(
+        array, axis, split_axis=0, concat_axis=0, tiled=True, axis_index_groups=groups
+    )
+
+
+def exchange_alone(array, axis, others, groups=None):
     array, others = lax.optimization_barrier((array, others))
-    return lax.optimization_barrier((exchange(array, axis), others))
+    return lax.optimization_barrier((exchange(array, axis, groups), others))
+
+
+def flat_index(side, seq_count, u, v, seq):
+    x, y = (v, u) if seq % 2 == 0 else (u, v)
+    return (x * side + y) * seq_count + seq
+
+
+def lines(side, seq_count, along_u):
+    return [
+        [
+            flat_index(side, seq_count, *((i, j) if along_u else (j, i)), seq)
+            for i in range(side)
+        ]
+        for seq in range(seq_count)
+        for j in range(side)
+    ]
+
+
+def shift_along_u(side, seq_count, k):
+    return [
+        (
+            flat_index(side, seq_count, u, v, seq),
+            flat_index(side, seq_count, (u + k) % side, v, seq),
+        )
+        for seq in range(seq_count)
+        for u in range(side)
+        for v in range(side)
+    ]
 
 
 def pad_lanes(array, width):
@@ -389,6 +504,7 @@
     index_scale = index_width ** (-0.5)
     loss_weight = float(slot_count * block)
     groups = head_count // 2
+    side = math.isqrt(head_count)
     rows = block // groups
     small = rows // 2
     tokens = block // head_count
@@ -408,11 +524,14 @@
     in_smem = pl.BlockSpec(memory_space=pltpu.SMEM)
     in_place = pl.BlockSpec(memory_space=pl.ANY)
 
-    packed = pl.pallas_call(
+    packed, own_rope = pl.pallas_call(
         functools.partial(first_kernel, groups),
-        out_shape=jax.ShapeDtypeStruct((seq_count * rows, lanes), bf16),
+        out_shape=(
+            jax.ShapeDtypeStruct((seq_count * rows, lanes), bf16),
+            jax.ShapeDtypeStruct((block, 2 * rope_width), bf16),
+        ),
         in_specs=[in_vmem] + [in_place] * 3,
-        out_specs=in_vmem,
+        out_specs=(in_vmem, in_vmem),
         scratch_shapes=[
             pltpu.VMEM((local_blocks, rows, latent_width), bf16),
             pltpu.VMEM((local_blocks, rows, index_width), bf16),
@@ -439,49 +558,55 @@
     pieces = jnp.concatenate([high, middle, low], axis=-1).astype(bf16)
     pieces = pad_lanes(jnp.concatenate([pieces[:, 0], pieces[:, 1]], axis=-1), 128)
     pieces = pieces.reshape(head_count * index_rows // 2, 128)
-    packed_rows = share_rows + query_rows + index_rows + index_rows // 2
-    own = slice((local_blocks - 1) * block, local_blocks * block)
-    own_rope = jnp.concatenate([rope_keys[own], rope_keys[own]], axis=-1)
+    height = query_rows + index_rows + index_rows // 2
     total = slot_count * block
-    token_at = head_index * tokens + jnp.arange(tokens)
-    remote_mask = jnp.broadcast_to(
-        slot_valid[None, 1:, None], (groups, remote_slots, rows)
-    ).reshape(-1)
-    key_mask = jnp.concatenate(
-        [
-            jnp.broadcast_to(remote_mask, (tokens, remote_mask.shape[0])),
-            jnp.arange(block)[None, :] <= token_at[:, None],
-        ],
-        axis=1,
-    )
-    bias = jnp.where(key_mask, 0.0, -1e30).astype(f32)
-    key_bias = pad_lanes(bias.T.astype(bf16), 128)
+    axes = ("head", "seq")
+    *parts, bias, key_bias = pl.pallas_call(
+        functools.partial(query_kernel, side, groups),
+        out_shape=tuple([jax.ShapeDtypeStruct((side, height, lanes), bf16)] * side)
+        + (
+            jax.ShapeDtypeStruct((tokens, total), f32),
+            jax.ShapeDtypeStruct((total, 128), bf16),
+        ),
+        in_specs=[in_vmem] * 5,
+        out_specs=tuple([in_vmem] * (side + 2)),
+        compiler_params=pltpu.CompilerParams(vmem_limit_bytes=24 * 1024 * 1024),
+    )(sel_blocks.T, latent_parts, rope_parts, index_parts, pieces)
+    for k in range(1, side):
+        parts[k] = lax.ppermute(parts[k], axes, shift_along_u(side, seq_count, k))
     outgoing = pl.pallas_call(
-        functools.partial(second_kernel, local_blocks),
-        out_shape=jax.ShapeDtypeStruct((head_count, packed_rows, lanes), bf16),
-        in_specs=[in_smem] + [in_vmem] * 5,
+        functools.partial(stage_kernel, local_blocks),
+        out_shape=jax.ShapeDtypeStruct((side, share_rows + side * height, lanes), bf16),
+        in_specs=[in_smem] + [in_vmem] * (side + 1),
         out_specs=in_vmem,
         compiler_params=pltpu.CompilerParams(vmem_limit_bytes=24 * 1024 * 1024),
-    )(sel_blocks.T, fetched, latent_parts, rope_parts, index_parts, pieces)
+    )(sel_blocks.T, fetched, *parts)
     found = (source[1:][None, :] == jnp.arange(seq_count)[:, None]) & slot_valid[1:][None, :]
     slot_of = jnp.sum(jnp.where(found, jnp.arange(1, slot_count)[None, :], 0), axis=1)
     owner = wanted[:, None] & (which[:, None] == jnp.arange(local_blocks)[None, :])
     owner = owner.astype(f32)
-    arrived, (bias, key_bias, own_latent, own_rope, own_index, slot_of, owner) = exchange_alone(
-        outgoing,
-        "head",
-        (bias, key_bias, latent_cache[own], own_rope, index_keys[own], slot_of, owner),
+    later = (bias, key_bias, own_rope, slot_of, owner)
+    staged, later = exchange_alone(outgoing, axes, later, lines(side, seq_count, False))
+    spread = pl.pallas_call(
+        spread_kernel,
+        out_shape=jax.ShapeDtypeStruct((side, side * share_rows, lanes), bf16),
+        in_specs=[in_vmem],
+        out_specs=in_vmem,
+        compiler_params=pltpu.CompilerParams(vmem_limit_bytes=16 * 1024 * 1024),
+    )(staged)
+    spread, (staged, bias, key_bias, own_rope, slot_of, owner) = exchange_alone(
+        spread, axes, (staged, *later), lines(side, seq_count, True)
     )
 
     all_rows = head_count * index_rows
     grad_queries, grad_weights, shares = pl.pallas_call(
-        functools.partial(compute_kernel, share_rows, loss_weight, index_scale),
+        functools.partial(compute_kernel, loss_weight, index_scale, index_heads),
         out_shape=(
-            jax.ShapeDtypeStruct((all_rows, index_width), bf16),
+            jax.ShapeDtypeStruct((head_count, index_rows, index_width), bf16),
             jax.ShapeDtypeStruct((head_count, 16, 128), bf16),
             jax.ShapeDtypeStruct((head_count, slot_count * small, index_width), bf16),
         ),
-        in_specs=[in_vmem] * 6,
+        in_specs=[in_vmem] * 5 + [in_place] * 2,
         out_specs=(in_vmem, in_vmem, in_vmem),
         scratch_shapes=[
             pltpu.VMEM((total, latent_width + 256), bf16),
@@ -494,9 +619,18 @@
             pltpu.VMEM((index_rows, total), f32),
             pltpu.VMEM((query_rows, total), f32),
             pltpu.VMEM((total, index_width), f32),
+            pltpu.SemaphoreType.DMA((2,)),
         ],
         compiler_params=pltpu.CompilerParams(vmem_limit_bytes=36 * 1024 * 1024),
-    )(arrived, bias, key_bias, own_latent, own_rope, own_index)
+    )(
+        staged,
+        spread.reshape(head_count, share_rows, lanes),
+        bias,
+        key_bias,
+        own_rope,
+        latent_cache,
+        index_keys,
+    )
 
     collected, (grad_queries, grad_weights, slot_of, owner) = exchange_alone(
         shares, "head", (grad_queries, grad_weights, slot_of, owner)
@@ -517,7 +651,7 @@
             jnp.broadcast_to(
                 owned.reshape(own_rows, index_width).astype(bf16), (head_count, own_rows, index_width)
             ),
-            grad_queries.reshape(head_count, index_rows, index_width),
+            grad_queries,
             grad_weights,
         ],
         axis=1,

time: 168 us -> 151 us (0.90)
  blocking collectives: 102 us -> 87.6 us
  starting transfers between devices: 15.5 us -> 27 us
  local copies, waits for them, and re-layouts: 11.3 us -> 3.19 us
  waiting for transfers between devices: 18.2 us -> 13.2 us
    all_to_all x4 -> x5, blocking collectives: 102 us -> 87.6 us  [exchange(): lax.all_to_all(array, axis, split_axis=0, concat_axis=0, tiled=True, axis...]
    ppermute x0 -> x3, starting transfers between devices: none -> 11.5 us  [body(): parts[k] = lax.ppermute(parts[k], axes, shift_along_u(side, seq_count, k))]
    all_to_all x1, waiting for transfers between devices: 18.2 us -> 7.89 us  [exchange(): lax.all_to_all(array, axis, split_axis=0, concat_axis=0, tiled=True, axis...]
    ppermute x0 -> x3, waiting for transfers between devices: none -> 5.29 us  [body(): parts[k] = lax.ppermute(parts[k], axes, shift_along_u(side, seq_count, k))]
    unnamed x16 -> x15, local copies, waits for them, and re-layouts: 5.14 us -> 2.1 us
    slice x4 -> x1, local copies, waits for them, and re-layouts: 2.47 us -> 0.08 us  [body(): slot_valid[1:][None, :]]
    pallas_call x3 -> x5, Pallas kernels: 15.9 us -> 16.7 us  [the longest x1 12.3 us: body(): pl.pallas_call(functools.partial(compute_kernel, loss_weight, index_scale...]
  transfers between devices with their start and end apart: 1 -> 4, of which waited for: 1 -> 3; matrix products, arithmetic and copies ran while one was open for 6% -> 2% of each run, Pallas kernels for 0% -> 0%
where the time goes in v3:
time: 151 us; the launch traced here: 150 us
  blocking collectives  87.6 us (58%)
  starting transfers between devices  27 us (18%)
  Pallas kernels  17.5 us (12%)
  waiting for transfers between devices  13.2 us (9%)
  local copies, waits for them, and re-layouts  3.19 us (2%)
    all_to_all x5, blocking collectives, exchange(): lax.all_to_all(array, axis, split_axis=0, concat_axis=0, tiled=True, axis...  87.6 us
    all_to_all x1, starting transfers between devices, exchange(): lax.all_to_all(array, axis, split_axis=0, concat_axis=0, tiled=True, axis...  15.5 us
    pallas_call x1, Pallas kernels, body(): pl.pallas_call(functools.partial(compute_kernel, loss_weight, index_scale...  12.3 us
    ppermute x3, starting transfers between devices, body(): parts[k] = lax.ppermute(parts[k], axes, shift_along_u(side, seq_count, k))  11.5 us
    all_to_all x1, waiting for transfers between devices, exchange(): lax.all_to_all(array, axis, split_axis=0, concat_axis=0, tiled=True, axis...  7.89 us
    ppermute x3, waiting for transfers between devices, body(): parts[k] = lax.ppermute(parts[k], axes, shift_along_u(side, seq_count, k))  5.29 us
  transfers between devices with their start and end apart: 4, of which 3 were waited for; matrix products, arithmetic and copies ran while one was open for 2% of the time, Pallas kernels for 0%

profile of v3, /device:TPU:6, one launch (start us, length us, event | category | flops | bytes accessed | tf_op | source)
XLA Modules:
  0.0 150.2 jit_solution(15525244444410657823)
XLA Ops:
  0.6 0.0 copy-start.3
  0.6 0.0 copy-start.4
  0.7 0.0 copy-start.1
  0.7 2.8 %shard_map.103 = (bf16[512,384]{1,0:T(8,128)(2,1)}, bf16[128,128]{1,0:T(8,128)(2,1)}) custom-call(s32[16,32]{1,0:T(8,128)} %bitcast.23, bf16[512,512]{1,0:T(8,128)(2,1)} %latent.3, bf16[64,512]{1,0:T(8,128)(2,1)} %bitcast.33, bf16[512,128]{1,0:T(8,128)(2,1)} %index.3), custom_call_target="tpu_custom_call" | custom-call | tf_op jit(solution)/shard_map/pallas_call | solution.py:527
  3.5 15.5 %all-to-all-start = ((bf16[32,16,384]{2,1,0:T(8,128)(2,1)}), bf16[32,16,384]{2,1,0:T(8,128)(2,1)S(1)}, u32[]{:S(2)}, u32[]{:S(2)}) async-start(bf16[32,16,384]{2,1,0:T(8,128)(2,1)} %bitcast.31), calls=%async_computation | async-start | bytes 786432 | tf_op jit(solution)/shard_map/all_to_all | solution.py:450
  19.0 0.8 copy.25
  19.8 0.1 reshape.137
  19.9 0.2 copy.29
  20.1 1.1 copy.24
  21.3 0.1 pad_maximum_fusion.1.rope
  21.4 0.0 copy-done.3
  21.4 0.0 copy-done.4
  21.4 0.0 copy-done.1
  21.4 0.5 shard_map.104
  21.9 3.5 %collective-permute-start = (bf16[4,112,384]{2,1,0:T(8,128)(2,1)S(1)}, bf16[4,112,384]{2,1,0:T(8,128)(2,1)S(1)}, u32[]{:S(2)}, u32[]{:S(2)}) collective-permute-start(bf16[4,112,384]{2,1,0:T(8,128)(2,1)S(1)} %get-tuple-element.77), channel_id=1, source_target_pairs={{0,32},{128,160},{256,288},{384,416},{32,64},{160,192},{288,320},{... | collective-permute-start | bytes 1032200 | tf_op jit(solution)/shard_map/ppermute | solution.py:576
  25.4 4.8 %collective-permute-start.1 = (bf16[4,112,384]{2,1,0:T(8,128)(2,1)S(1)}, bf16[4,112,384]{2,1,0:T(8,128)(2,1)S(1)}, u32[]{:S(2)}, u32[]{:S(2)}) collective-permute-start(bf16[4,112,384]{2,1,0:T(8,128)(2,1)S(1)} %get-tuple-element.78), channel_id=1, source_target_pairs={{0,64},{128,192},{256,320},{384,448},{32,96},{160,224},{288,352},{... | collective-permute-start | bytes 1032200 | tf_op jit(solution)/shard_map/ppermute | solution.py:576
  30.2 3.3 %collective-permute-start.2 = (bf16[4,112,384]{2,1,0:T(8,128)(2,1)S(1)}, bf16[4,112,384]{2,1,0:T(8,128)(2,1)S(1)}, u32[]{:S(2)}, u32[]{:S(2)}) collective-permute-start(bf16[4,112,384]{2,1,0:T(8,128)(2,1)S(1)} %get-tuple-element.79), channel_id=1, source_target_pairs={{0,96},{128,224},{256,352},{384,480},{32,0},{160,128},{288,256},{4... | collective-permute-start | bytes 1032200 | tf_op jit(solution)/shard_map/ppermute | solution.py:576
  33.4 0.2 dynamic-slice_reduce_fusion
  33.7 0.1 slice.52
  33.8 0.1 slice.51
  33.9 0.1 select_reduce_fusion.1
  34.0 0.1 fusion.2
  34.0 0.0 collective-permute-done.in1
  34.0 3.1 %collective-permute-done.1.in2 = bf16[4,112,384]{2,1,0:T(8,128)(2,1)S(1)} collective-permute-done((bf16[4,112,384]{2,1,0:T(8,128)(2,1)S(1)}, bf16[4,112,384]{2,1,0:T(8,128)(2,1)S(1)}, u32[]{:S(2)}, u32[]{:S(2)}) %collective-permute-start.1) | collective-permute-done | bytes 344096 | tf_op jit(solution)/shard_map/ppermute | solution.py:576
  37.2 2.2 %collective-permute-done.2.in3 = bf16[4,112,384]{2,1,0:T(8,128)(2,1)S(1)} collective-permute-done((bf16[4,112,384]{2,1,0:T(8,128)(2,1)S(1)}, bf16[4,112,384]{2,1,0:T(8,128)(2,1)S(1)}, u32[]{:S(2)}, u32[]{:S(2)}) %collective-permute-start.2) | collective-permute-done | bytes 344096 | tf_op jit(solution)/shard_map/ppermute | solution.py:576
  39.3 7.9 %all-to-all-done.fetched = bf16[32,16,384]{2,1,0:T(8,128)(2,1)S(1)} async-done(((bf16[32,16,384]{2,1,0:T(8,128)(2,1)}), bf16[32,16,384]{2,1,0:T(8,128)(2,1)S(1)}, u32[]{:S(2)}, u32[]{:S(2)}) %all-to-all-start) | async-done | bytes 393248 | tf_op jit(solution)/shard_map/all_to_all | solution.py:450
  47.2 0.9 shard_map.105
  48.1 19.1 %all_to_all.30.staged = bf16[4,688,384]{2,1,0:T(8,128)(2,1)S(1)} all-to-all(bf16[4,688,384]{2,1,0:T(8,128)(2,1)S(1)} %shard_map.105), channel_id=1, replica_groups={{0,128,256,384},{32,160,288,416},{64,192,320,448},{96,224,352,480},{1,3..., dimensions={0} | all-to-all | bytes 4227072 | tf_op jit(solution)/shard_map/all_to_all | solution.py:450
  67.2 0.3 shard_map.106
  67.4 0.0 copy-start
  67.4 0.0 copy-start.2
  67.5 0.0 copy-start.5
  67.5 25.5 %all_to_all.31 = bf16[4,960,384]{2,1,0:T(8,128)(2,1)S(1)} all-to-all(bf16[4,960,384]{2,1,0:T(8,128)(2,1)S(1)} %shard_map.106), channel_id=1, replica_groups={{0,32,64,96},{128,160,192,224},{256,288,320,352},{384,416,448,480},{1,1..., dimensions={0} | all-to-all | bytes 5898240 | tf_op jit(solution)/shard_map/all_to_all | solution.py:450
  92.9 0.0 copy-done
  92.9 0.0 copy-done.2
  92.9 0.0 copy-done.5
  93.0 12.3 %shard_map.107 = (bf16[16,32,128]{2,1,0:T(8,128)(2,1)S(1)}, bf16[16,16,128]{2,1,0:T(8,128)(2,1)S(1)}, bf16[16,128,128]{2,1,0:T(8,128)(2,1)S(1)}) custom-call(bf16[4,688,384]{2,1,0:T(8,128)(2,1)S(1)} %all_to_all.30.staged, bf16[16,240,384]{2,1,0:T(8,128)(2,1)S(1)} %bitcast.21, f32[8,2048]{1,0:T(8,128)S(1)} %get-tuple-element.104.bias, ...), custom_call_target="tpu_custom_call" | custom-call | tf_op jit(solution)/shard_map/pallas_call | solution.py:602
  105.2 13.0 %all_to_all.32 = bf16[16,128,128]{2,1,0:T(8,128)(2,1)S(1)} all-to-all(bf16[16,128,128]{2,1,0:T(8,128)(2,1)S(1)} %get-tuple-element.112), channel_id=1, replica_groups=mesh['head'=16,'seq'=32] {'head'}, dimensions={0} | all-to-all | bytes 1048576 | tf_op jit(solution)/shard_map/all_to_all | solution.py:450
  118.2 0.1 convert_reduce_fusion
  118.3 0.6 gather_fusion
  119.0 0.1 select_convert_fusion
  119.1 17.9 %all_to_all.33 = bf16[32,8,128]{2,1,0:T(8,128)(2,1)S(1)} all-to-all(bf16[32,8,128]{2,1,0:T(8,128)(2,1)S(1)} %select_convert_fusion), channel_id=1, replica_groups=mesh['head'=16,'seq'=32] {'seq'}, dimensions={0} | all-to-all | bytes 131072 | tf_op jit(solution)/shard_map/all_to_all | solution.py:450
  137.0 0.2 multiply_reduce_fusion
  137.3 12.1 %all_to_all.34.final = bf16[16,80,128]{2,1,0:T(8,128)(2,1)S(1)} all-to-all(bf16[16,80,128]{2,1,0:T(8,128)(2,1)S(1)} %pad_maximum_fusion), channel_id=1, replica_groups=mesh['head'=16,'seq'=32] {'head'}, dimensions={0} | all-to-all | bytes 655360 | tf_op jit(solution)/shard_map/all_to_all | solution.py:450
  149.4 0.9 shard_map.108
  (20 shorter events, 0.2 us)
Async XLA Ops:
  0.6 20.7 %copy-start.3 = (s32[32,16]{0,1:T(8,128)S(1)}, s32[32,16]{0,1:T(8,128)}, u32[]{:S(2)}) copy-start(s32[32,16]{0,1:T(8,128)} %param.17) | copy-start | bytes 6148
  0.6 20.7 %copy-start.4 = (bf16[128,4,128]{2,1,0:T(4,128)(2,1)S(1)}, bf16[128,4,128]{2,1,0:T(4,128)(2,1)}, u32[]{:S(2)}) copy-start(bf16[128,4,128]{2,1,0:T(4,128)(2,1)} %param.14) | copy-start | bytes 393220
  0.7 20.7 %copy-start.1 = (bf16[128,8,512]{2,1,0:T(8,128)(2,1)S(1)}, bf16[128,8,512]{2,1,0:T(8,128)(2,1)}, u32[]{:S(2)}) copy-start(bf16[128,8,512]{2,1,0:T(8,128)(2,1)} %param.10) | copy-start | bytes 3145732
  3.5 43.7 %all-to-all-start = ((bf16[32,16,384]{2,1,0:T(8,128)(2,1)}), bf16[32,16,384]{2,1,0:T(8,128)(2,1)S(1)}, u32[]{:S(2)}, u32[]{:S(2)}) async-start(bf16[32,16,384]{2,1,0:T(8,128)(2,1)} %bitcast.31), calls=%async_computation | async-start | bytes 786432 | tf_op jit(solution)/shard_map/all_to_all | solution.py:450
  21.9 12.2 %collective-permute-start = (bf16[4,112,384]{2,1,0:T(8,128)(2,1)S(1)}, bf16[4,112,384]{2,1,0:T(8,128)(2,1)S(1)}, u32[]{:S(2)}, u32[]{:S(2)}) collective-permute-start(bf16[4,112,384]{2,1,0:T(8,128)(2,1)S(1)} %get-tuple-element.77), channel_id=1, source_target_pairs={{0,32},{128,160},{256,288},{384,416},{32,64},{160,192},{288,320},{... | collective-permute-start | bytes 1032200 | tf_op jit(solution)/shard_map/ppermute | solution.py:576
  25.4 11.8 %collective-permute-start.1 = (bf16[4,112,384]{2,1,0:T(8,128)(2,1)S(1)}, bf16[4,112,384]{2,1,0:T(8,128)(2,1)S(1)}, u32[]{:S(2)}, u32[]{:S(2)}) collective-permute-start(bf16[4,112,384]{2,1,0:T(8,128)(2,1)S(1)} %get-tuple-element.78), channel_id=1, source_target_pairs={{0,64},{128,192},{256,320},{384,448},{32,96},{160,224},{288,352},{... | collective-permute-start | bytes 1032200 | tf_op jit(solution)/shard_map/ppermute | solution.py:576
  30.2 9.1 %collective-permute-start.2 = (bf16[4,112,384]{2,1,0:T(8,128)(2,1)S(1)}, bf16[4,112,384]{2,1,0:T(8,128)(2,1)S(1)}, u32[]{:S(2)}, u32[]{:S(2)}) collective-permute-start(bf16[4,112,384]{2,1,0:T(8,128)(2,1)S(1)} %get-tuple-element.79), channel_id=1, source_target_pairs={{0,96},{128,224},{256,352},{384,480},{32,0},{160,128},{288,256},{4... | collective-permute-start | bytes 1032200 | tf_op jit(solution)/shard_map/ppermute | solution.py:576
  67.4 25.5 %copy-start = (bf16[512,512]{1,0:T(8,128)(2,1)S(1)}, bf16[512,512]{1,0:T(8,128)(2,1)}, u32[]{:S(2)}) copy-start(bf16[512,512]{1,0:T(8,128)(2,1)} %latent.3) | copy-start | bytes 1572868
  67.4 25.5 %copy-start.2 = (bf16[512,128]{1,0:T(8,128)(2,1)S(1)}, bf16[512,128]{1,0:T(8,128)(2,1)}, u32[]{:S(2)}) copy-start(bf16[512,128]{1,0:T(8,128)(2,1)} %index.3) | copy-start | bytes 393220
  67.5 25.5 %copy-start.5 = (bf16[128,128]{1,0:T(8,128)(2,1)S(1)}, bf16[128,128]{1,0:T(8,128)(2,1)}, u32[]{:S(2)}) copy-start(bf16[128,128]{1,0:T(8,128)(2,1)} %get-tuple-element.106.own_rope) | copy-start | bytes 98308

commit v4 on v3

--- a/solution.py
+++ b/solution.py
@@ -35,7 +35,19 @@
 
 
 def first_kernel(
-    groups, sel_turned, latent, rope_turned, index, packed, own_rope, wide, narrow, turned, rope, sems
+    groups,
+    sel_turned,
+    latent,
+    rope_turned,
+    index,
+    packed,
+    own_rope,
+    wide,
+    narrow,
+    turned,
+    rope,
+    table,
+    sems,
 ):
     slots, destinations = sel_turned.shape
     local_blocks, rows, latent_width = wide.shape
@@ -44,7 +56,10 @@
     head = lax.axis_index("head")
     group = lax.rem(head, groups)
     is_low = head < groups
+    last = 1 + 2 * local_blocks
     copies = [pltpu.make_async_copy(rope_turned, turned, sems.at[0])]
+    table_copy = pltpu.make_async_copy(sel_turned, table, sems.at[last])
+    table_copy.start()
     spots = []
     for k in range(local_blocks):
         at = pl.ds(pl.multiple_of(k * block + group * rows, rows), rows)
@@ -57,7 +72,8 @@
     total = packed.shape[0]
     repeat = lax.broadcasted_iota(jnp.int32, (total, destinations), 0) // rows
     repeat = (repeat == lax.broadcasted_iota(jnp.int32, (total, destinations), 1)).astype(f32)
-    chosen = dot_last(repeat, sel_turned[...].astype(f32))
+    table_copy.wait()
+    chosen = dot_last(repeat, table[...].astype(f32))
     offset = chosen - (lax.axis_index("seq") * local_blocks).astype(f32)
     slot = lax.broadcasted_iota(jnp.int32, (total, slots), 1)
     inside = (chosen >= 0) & (offset >= 0) & (offset < local_blocks) & (slot > 0)
@@ -308,16 +324,37 @@
     def source_of(v, k):
         return head_at(step, core, lax.rem(own_u + step - k, step), v)
 
-    @pl.loop(0, sources // step)
-    def _(c):
-        score_at = pl.ds(pl.multiple_of(c * score_rows, score_rows), score_rows)
-        rows = pl.ds(pl.multiple_of(c * chunk, chunk), chunk)
+    tile_at = [slice(k * tile, (k + 1) * tile) for k in range(tiles)]
+
+    def soften(c, state, k):
+        score_at = slice(c * score_rows, (c + 1) * score_rows)
+        if k == 0:
+            state["top"] = jnp.max(state["best"], axis=1, keepdims=True)
+            state["sums"] = jnp.zeros((score_rows, 128), f32)
+        if k == tiles // 2:
+            weight = 1.0 / ((heads * sources) * jnp.sum(state["sums"], axis=1, keepdims=True))
+            state["weight"] = weight.reshape(step, query_rows, 1)
+        for i in range(2):
+            if k < tiles // 2:
+                at = tile_at[2 * k + i]
+                power = jnp.exp((scores[score_at, at] - state["top"]) * score_scale)
+                scores[score_at, at] = power
+                state["sums"] = state["sums"] + (power[:, 0:128] + power[:, 128:256])
+            else:
+                at = tile_at[2 * k - tiles + i]
+                power = scores[score_at, at].reshape(step, query_rows, tile)
+                target_rows[:, at] += jnp.sum(power * state["weight"], axis=0)
+
+    state = None
+    for c in range(sources // step):
+        score_at = slice(c * score_rows, (c + 1) * score_rows)
+        rows = slice(c * chunk, (c + 1) * chunk)
         queries = queries_of(c)
         index_q = index_queries_of(c)
         weights = weights_of(c)
         best = jnp.full((score_rows, 128), -3e38, f32)
         for k in range(tiles):
-            at = slice(k * tile, (k + 1) * tile)
+            at = tile_at[k]
             part = dot_last(queries, keys[at, :])
             scores[score_at, at] = part
             best = jnp.maximum(best, jnp.maximum(part[:, 0:128], part[:, 128:256]))
@@ -327,24 +364,11 @@
             logit_rows[:, at] += jnp.sum(
                 act.reshape(step, index_rows, tile) * weights, axis=0
             )
-        highest[score_at, :] = best
-
-    @pl.loop(0, sources // step)
-    def _(c):
-        score_at = pl.ds(pl.multiple_of(c * score_rows, score_rows), score_rows)
-        top = jnp.max(highest[score_at, :], axis=1, keepdims=True)
-        sums = jnp.zeros((score_rows, 128), f32)
-        for k in range(tiles):
-            at = slice(k * tile, (k + 1) * tile)
-            power = jnp.exp((scores[score_at, at] - top) * score_scale)
-            scores[score_at, at] = power
-            sums = sums + (power[:, 0:128] + power[:, 128:256])
-        weight = 1.0 / ((heads * sources) * jnp.sum(sums, axis=1, keepdims=True))
-        weight = weight.reshape(step, query_rows, 1)
-        for k in range(tiles):
-            at = slice(k * tile, (k + 1) * tile)
-            power = scores[score_at, at].reshape(step, query_rows, tile)
-            target_rows[:, at] += jnp.sum(power * weight, axis=0)
+            if state is not None:
+                soften(c - 1, state, k)
+        state = {"best": best}
+    for k in range(tiles):
+        soften(sources // step - 1, state, k)
 
     def gather(count):
         return (
@@ -365,9 +389,8 @@
     ).astype(bf16)
     logit_rows[...] = dot(spread, grad_logits)
 
-    @pl.loop(0, sources // step)
-    def _(c):
-        rows = pl.ds(pl.multiple_of(c * chunk, chunk), chunk)
+    for c in range(sources // step):
+        rows = slice(c * chunk, (c + 1) * chunk)
         weights = weights_of(c) * index_scale
         sums = jnp.zeros((chunk, 128), f32)
         for k in range(tiles):
@@ -530,14 +553,15 @@
             jax.ShapeDtypeStruct((seq_count * rows, lanes), bf16),
             jax.ShapeDtypeStruct((block, 2 * rope_width), bf16),
         ),
-        in_specs=[in_vmem] + [in_place] * 3,
+        in_specs=[in_place] * 4,
         out_specs=(in_vmem, in_vmem),
         scratch_shapes=[
             pltpu.VMEM((local_blocks, rows, latent_width), bf16),
             pltpu.VMEM((local_blocks, rows, index_width), bf16),
             pltpu.VMEM((rope_width, local_blocks * block), bf16),
             pltpu.VMEM((local_blocks * block, 2 * rope_width), bf16),
-            pltpu.SemaphoreType.DMA((1 + 2 * local_blocks,)),
+            pltpu.VMEM((slot_count, seq_count), jnp.int32),
+            pltpu.SemaphoreType.DMA((2 + 2 * local_blocks,)),
         ],
         compiler_params=pltpu.CompilerParams(vmem_limit_bytes=60 * 1024 * 1024),
     )(sel_blocks.T, latent_cache, rope_keys.T, index_keys)

time: 151 us -> 147 us (0.974)
  Pallas kernels: 17.5 us -> 13.9 us
    pallas_call x1, Pallas kernels: 12.3 us -> 9.19 us  [body(): pl.pallas_call(functools.partial(compute_kernel, loss_weight, index_scale...]
where the time goes in v4:
time: 147 us
  blocking collectives  87.6 us (60%)
  starting transfers between devices  27 us (18%)
  Pallas kernels  13.9 us (9%)
  waiting for transfers between devices  13.2 us (9%)
  local copies, waits for them, and re-layouts  3.19 us (2%)
    all_to_all x5, blocking collectives, exchange(): lax.all_to_all(array, axis, split_axis=0, concat_axis=0, tiled=True, axis...  87.6 us
    all_to_all x1, starting transfers between devices, exchange(): lax.all_to_all(array, axis, split_axis=0, concat_axis=0, tiled=True, axis...  15.5 us
    ppermute x3, starting transfers between devices, body(): parts[k] = lax.ppermute(parts[k], axes, shift_along_u(side, seq_count, k))  11.5 us
    pallas_call x1, Pallas kernels, body(): pl.pallas_call(functools.partial(compute_kernel, loss_weight, index_scale...  9.19 us
    all_to_all x1, waiting for transfers between devices, exchange(): lax.all_to_all(array, axis, split_axis=0, concat_axis=0, tiled=True, axis...  7.89 us
    ppermute x3, waiting for transfers between devices, body(): parts[k] = lax.ppermute(parts[k], axes, shift_along_u(side, seq_count, k))  5.28 us
  transfers between devices with their start and end apart: 4, of which 3 were waited for; matrix products, arithmetic and copies ran while one was open for 2% of the time, Pallas kernels for 0%

profile of v4, /device:TPU:6, one launch (start us, length us, event | category | flops | bytes accessed | tf_op | source)
XLA Modules:
  0.0 146.6 jit_solution(3214161901750620487)
XLA Ops:
  0.6 0.0 copy-start.3
  0.6 0.0 copy-start.4
  0.7 0.0 copy-start.1
  0.7 2.2 %shard_map.103 = (bf16[512,384]{1,0:T(8,128)(2,1)}, bf16[128,128]{1,0:T(8,128)(2,1)}) custom-call(s32[16,32]{1,0:T(8,128)} %bitcast.23, bf16[512,512]{1,0:T(8,128)(2,1)} %latent.3, bf16[64,512]{1,0:T(8,128)(2,1)} %bitcast.33, bf16[512,128]{1,0:T(8,128)(2,1)} %index.3), custom_call_target="tpu_custom_call" | custom-call | tf_op jit(solution)/shard_map/pallas_call | solution.py:550
  2.9 15.5 %all-to-all-start = ((bf16[32,16,384]{2,1,0:T(8,128)(2,1)}), bf16[32,16,384]{2,1,0:T(8,128)(2,1)S(1)}, u32[]{:S(2)}, u32[]{:S(2)}) async-start(bf16[32,16,384]{2,1,0:T(8,128)(2,1)} %bitcast.31), calls=%async_computation | async-start | bytes 786432 | tf_op jit(solution)/shard_map/all_to_all | solution.py:473
  18.4 0.8 copy.25
  19.2 0.1 reshape.137
  19.4 0.2 copy.29
  19.6 1.1 copy.24
  20.7 0.1 pad_maximum_fusion.1.rope
  20.8 0.0 copy-done.3
  20.8 0.0 copy-done.4
  20.8 0.0 copy-done.1
  20.8 0.5 shard_map.104
  21.3 3.5 %collective-permute-start = (bf16[4,112,384]{2,1,0:T(8,128)(2,1)S(1)}, bf16[4,112,384]{2,1,0:T(8,128)(2,1)S(1)}, u32[]{:S(2)}, u32[]{:S(2)}) collective-permute-start(bf16[4,112,384]{2,1,0:T(8,128)(2,1)S(1)} %get-tuple-element.77), channel_id=1, source_target_pairs={{0,32},{128,160},{256,288},{384,416},{32,64},{160,192},{288,320},{... | collective-permute-start | bytes 1032200 | tf_op jit(solution)/shard_map/ppermute | solution.py:600
  24.8 4.8 %collective-permute-start.1 = (bf16[4,112,384]{2,1,0:T(8,128)(2,1)S(1)}, bf16[4,112,384]{2,1,0:T(8,128)(2,1)S(1)}, u32[]{:S(2)}, u32[]{:S(2)}) collective-permute-start(bf16[4,112,384]{2,1,0:T(8,128)(2,1)S(1)} %get-tuple-element.78), channel_id=1, source_target_pairs={{0,64},{128,192},{256,320},{384,448},{32,96},{160,224},{288,352},{... | collective-permute-start | bytes 1032200 | tf_op jit(solution)/shard_map/ppermute | solution.py:600
  29.6 3.3 %collective-permute-start.2 = (bf16[4,112,384]{2,1,0:T(8,128)(2,1)S(1)}, bf16[4,112,384]{2,1,0:T(8,128)(2,1)S(1)}, u32[]{:S(2)}, u32[]{:S(2)}) collective-permute-start(bf16[4,112,384]{2,1,0:T(8,128)(2,1)S(1)} %get-tuple-element.79), channel_id=1, source_target_pairs={{0,96},{128,224},{256,352},{384,480},{32,0},{160,128},{288,256},{4... | collective-permute-start | bytes 1032200 | tf_op jit(solution)/shard_map/ppermute | solution.py:600
  32.9 0.2 dynamic-slice_reduce_fusion
  33.2 0.1 slice.52
  33.2 0.1 slice.51
  33.3 0.1 select_reduce_fusion.1
  33.4 0.1 fusion.2
  33.5 0.0 collective-permute-done.in1
  33.5 3.1 %collective-permute-done.1.in2 = bf16[4,112,384]{2,1,0:T(8,128)(2,1)S(1)} collective-permute-done((bf16[4,112,384]{2,1,0:T(8,128)(2,1)S(1)}, bf16[4,112,384]{2,1,0:T(8,128)(2,1)S(1)}, u32[]{:S(2)}, u32[]{:S(2)}) %collective-permute-start.1) | collective-permute-done | bytes 344096 | tf_op jit(solution)/shard_map/ppermute | solution.py:600
  36.6 2.2 %collective-permute-done.2.in3 = bf16[4,112,384]{2,1,0:T(8,128)(2,1)S(1)} collective-permute-done((bf16[4,112,384]{2,1,0:T(8,128)(2,1)S(1)}, bf16[4,112,384]{2,1,0:T(8,128)(2,1)S(1)}, u32[]{:S(2)}, u32[]{:S(2)}) %collective-permute-start.2) | collective-permute-done | bytes 344096 | tf_op jit(solution)/shard_map/ppermute | solution.py:600
  38.8 7.9 %all-to-all-done.fetched = bf16[32,16,384]{2,1,0:T(8,128)(2,1)S(1)} async-done(((bf16[32,16,384]{2,1,0:T(8,128)(2,1)}), bf16[32,16,384]{2,1,0:T(8,128)(2,1)S(1)}, u32[]{:S(2)}, u32[]{:S(2)}) %all-to-all-start) | async-done | bytes 393248 | tf_op jit(solution)/shard_map/all_to_all | solution.py:473
  46.7 0.9 shard_map.105
  47.5 19.1 %all_to_all.30.staged = bf16[4,688,384]{2,1,0:T(8,128)(2,1)S(1)} all-to-all(bf16[4,688,384]{2,1,0:T(8,128)(2,1)S(1)} %shard_map.105), channel_id=1, replica_groups={{0,128,256,384},{32,160,288,416},{64,192,320,448},{96,224,352,480},{1,3..., dimensions={0} | all-to-all | bytes 4227072 | tf_op jit(solution)/shard_map/all_to_all | solution.py:473
  66.6 0.3 shard_map.106
  66.9 0.0 copy-start
  66.9 0.0 copy-start.2
  66.9 0.0 copy-start.5
  66.9 25.5 %all_to_all.31 = bf16[4,960,384]{2,1,0:T(8,128)(2,1)S(1)} all-to-all(bf16[4,960,384]{2,1,0:T(8,128)(2,1)S(1)} %shard_map.106), channel_id=1, replica_groups={{0,32,64,96},{128,160,192,224},{256,288,320,352},{384,416,448,480},{1,1..., dimensions={0} | all-to-all | bytes 5898240 | tf_op jit(solution)/shard_map/all_to_all | solution.py:473
  92.4 0.0 copy-done
  92.4 0.0 copy-done.2
  92.4 0.0 copy-done.5
  92.4 9.2 %shard_map.107 = (bf16[16,32,128]{2,1,0:T(8,128)(2,1)S(1)}, bf16[16,16,128]{2,1,0:T(8,128)(2,1)S(1)}, bf16[16,128,128]{2,1,0:T(8,128)(2,1)S(1)}) custom-call(bf16[4,688,384]{2,1,0:T(8,128)(2,1)S(1)} %all_to_all.30.staged, bf16[16,240,384]{2,1,0:T(8,128)(2,1)S(1)} %bitcast.21, f32[8,2048]{1,0:T(8,128)S(1)} %get-tuple-element.104.bias, ...), custom_call_target="tpu_custom_call" | custom-call | tf_op jit(solution)/shard_map/pallas_call | solution.py:626
  101.6 13.0 %all_to_all.32 = bf16[16,128,128]{2,1,0:T(8,128)(2,1)S(1)} all-to-all(bf16[16,128,128]{2,1,0:T(8,128)(2,1)S(1)} %get-tuple-element.112), channel_id=1, replica_groups=mesh['head'=16,'seq'=32] {'head'}, dimensions={0} | all-to-all | bytes 1048576 | tf_op jit(solution)/shard_map/all_to_all | solution.py:473
  114.6 0.1 convert_reduce_fusion
  114.7 0.6 gather_fusion
  115.3 0.1 select_convert_fusion
  115.4 17.9 %all_to_all.33 = bf16[32,8,128]{2,1,0:T(8,128)(2,1)S(1)} all-to-all(bf16[32,8,128]{2,1,0:T(8,128)(2,1)S(1)} %select_convert_fusion), channel_id=1, replica_groups=mesh['head'=16,'seq'=32] {'seq'}, dimensions={0} | all-to-all | bytes 131072 | tf_op jit(solution)/shard_map/all_to_all | solution.py:473
  133.3 0.2 multiply_reduce_fusion
  133.6 12.1 %all_to_all.34.final = bf16[16,80,128]{2,1,0:T(8,128)(2,1)S(1)} all-to-all(bf16[16,80,128]{2,1,0:T(8,128)(2,1)S(1)} %pad_maximum_fusion), channel_id=1, replica_groups=mesh['head'=16,'seq'=32] {'head'}, dimensions={0} | all-to-all | bytes 655360 | tf_op jit(solution)/shard_map/all_to_all | solution.py:473
  145.7 0.9 shard_map.108
  (20 shorter events, 0.2 us)
Async XLA Ops:
  0.6 20.2 %copy-start.3 = (s32[32,16]{0,1:T(8,128)S(1)}, s32[32,16]{0,1:T(8,128)}, u32[]{:S(2)}) copy-start(s32[32,16]{0,1:T(8,128)} %param.17) | copy-start | bytes 6148
  0.6 20.2 %copy-start.4 = (bf16[128,4,128]{2,1,0:T(4,128)(2,1)S(1)}, bf16[128,4,128]{2,1,0:T(4,128)(2,1)}, u32[]{:S(2)}) copy-start(bf16[128,4,128]{2,1,0:T(4,128)(2,1)} %param.14) | copy-start | bytes 393220
  0.7 20.2 %copy-start.1 = (bf16[128,8,512]{2,1,0:T(8,128)(2,1)S(1)}, bf16[128,8,512]{2,1,0:T(8,128)(2,1)}, u32[]{:S(2)}) copy-start(bf16[128,8,512]{2,1,0:T(8,128)(2,1)} %param.10) | copy-start | bytes 3145732
  2.9 43.7 %all-to-all-start = ((bf16[32,16,384]{2,1,0:T(8,128)(2,1)}), bf16[32,16,384]{2,1,0:T(8,128)(2,1)S(1)}, u32[]{:S(2)}, u32[]{:S(2)}) async-start(bf16[32,16,384]{2,1,0:T(8,128)(2,1)} %bitcast.31), calls=%async_computation | async-start | bytes 786432 | tf_op jit(solution)/shard_map/all_to_all | solution.py:473
  21.3 12.2 %collective-permute-start = (bf16[4,112,384]{2,1,0:T(8,128)(2,1)S(1)}, bf16[4,112,384]{2,1,0:T(8,128)(2,1)S(1)}, u32[]{:S(2)}, u32[]{:S(2)}) collective-permute-start(bf16[4,112,384]{2,1,0:T(8,128)(2,1)S(1)} %get-tuple-element.77), channel_id=1, source_target_pairs={{0,32},{128,160},{256,288},{384,416},{32,64},{160,192},{288,320},{... | collective-permute-start | bytes 1032200 | tf_op jit(solution)/shard_map/ppermute | solution.py:600
  24.8 11.8 %collective-permute-start.1 = (bf16[4,112,384]{2,1,0:T(8,128)(2,1)S(1)}, bf16[4,112,384]{2,1,0:T(8,128)(2,1)S(1)}, u32[]{:S(2)}, u32[]{:S(2)}) collective-permute-start(bf16[4,112,384]{2,1,0:T(8,128)(2,1)S(1)} %get-tuple-element.78), channel_id=1, source_target_pairs={{0,64},{128,192},{256,320},{384,448},{32,96},{160,224},{288,352},{... | collective-permute-start | bytes 1032200 | tf_op jit(solution)/shard_map/ppermute | solution.py:600
  29.6 9.1 %collective-permute-start.2 = (bf16[4,112,384]{2,1,0:T(8,128)(2,1)S(1)}, bf16[4,112,384]{2,1,0:T(8,128)(2,1)S(1)}, u32[]{:S(2)}, u32[]{:S(2)}) collective-permute-start(bf16[4,112,384]{2,1,0:T(8,128)(2,1)S(1)} %get-tuple-element.79), channel_id=1, source_target_pairs={{0,96},{128,224},{256,352},{384,480},{32,0},{160,128},{288,256},{4... | collective-permute-start | bytes 1032200 | tf_op jit(solution)/shard_map/ppermute | solution.py:600
  66.9 25.5 %copy-start = (bf16[512,512]{1,0:T(8,128)(2,1)S(1)}, bf16[512,512]{1,0:T(8,128)(2,1)}, u32[]{:S(2)}) copy-start(bf16[512,512]{1,0:T(8,128)(2,1)} %latent.3) | copy-start | bytes 1572868
  66.9 25.5 %copy-start.2 = (bf16[512,128]{1,0:T(8,128)(2,1)S(1)}, bf16[512,128]{1,0:T(8,128)(2,1)}, u32[]{:S(2)}) copy-start(bf16[512,128]{1,0:T(8,128)(2,1)} %index.3) | copy-start | bytes 393220
  66.9 25.5 %copy-start.5 = (bf16[128,128]{1,0:T(8,128)(2,1)S(1)}, bf16[128,128]{1,0:T(8,128)(2,1)}, u32[]{:S(2)}) copy-start(bf16[128,128]{1,0:T(8,128)(2,1)} %get-tuple-element.106.own_rope) | copy-start | bytes 98308

commit v5 on v4

--- a/solution.py
+++ b/solution.py
@@ -50,22 +50,29 @@
     sems,
 ):
     slots, destinations = sel_turned.shape
-    local_blocks, rows, latent_width = wide.shape
+    variants, local_blocks, rows, latent_width = wide.shape
     block = latent.shape[0] // local_blocks
     half_width = latent_width // 2
+    side = groups // 2
     head = lax.axis_index("head")
-    group = lax.rem(head, groups)
-    is_low = head < groups
-    last = 1 + 2 * local_blocks
+    x, y = lax.div(head, side), lax.rem(head, side)
+    spots = []
+    lows = []
+    count = variants * local_blocks
     copies = [pltpu.make_async_copy(rope_turned, turned, sems.at[0])]
-    table_copy = pltpu.make_async_copy(sel_turned, table, sems.at[last])
+    table_copy = pltpu.make_async_copy(sel_turned, table, sems.at[1])
     table_copy.start()
-    spots = []
-    for k in range(local_blocks):
-        at = pl.ds(pl.multiple_of(k * block + group * rows, rows), rows)
-        spots.append(at)
-        copies.append(pltpu.make_async_copy(latent.at[at], wide.at[k], sems.at[1 + 2 * k]))
-        copies.append(pltpu.make_async_copy(index.at[at], narrow.at[k], sems.at[2 + 2 * k]))
+    for i, (u, v) in enumerate(((y, x), (x, y))):
+        group = lax.rem(v, 2) * side + u
+        lows.append(v < side // 2)
+        for k in range(local_blocks):
+            at = pl.ds(pl.multiple_of(k * block + group * rows, rows), rows)
+            n = i * local_blocks + k
+            spots.append(at)
+            copies.append(pltpu.make_async_copy(latent.at[at], wide.at[i, k], sems.at[2 + n]))
+            copies.append(
+                pltpu.make_async_copy(index.at[at], narrow.at[i, k], sems.at[2 + count + n])
+            )
     for copy in copies:
         copy.start()
 
@@ -78,26 +85,28 @@
     slot = lax.broadcasted_iota(jnp.int32, (total, slots), 1)
     inside = (chosen >= 0) & (offset >= 0) & (offset < local_blocks) & (slot > 0)
     which = jnp.sum(jnp.where(inside, offset, 0.0), axis=1, keepdims=True)
-    width = local_blocks * rows
-    row = lax.broadcasted_iota(jnp.int32, (total, width), 0) % rows
+    width = variants * local_blocks * rows
+    row = lax.broadcasted_iota(jnp.int32, (total, width), 0)
+    start = (row // rows) % variants * (local_blocks * rows) + row % rows
     column = lax.broadcasted_iota(jnp.int32, (total, width), 1)
-    pick = (column.astype(f32) == which * rows + row.astype(f32)).astype(bf16)
+    pick = (column.astype(f32) == which * rows + start.astype(f32)).astype(bf16)
 
     for copy in copies:
         copy.wait()
     rope_rows = turned[...].astype(f32)
     rope[...] = jnp.concatenate([rope_rows, rope_rows], axis=0).T.astype(bf16)
     parts = []
-    for k in range(local_blocks):
-        parts.append(
-            jnp.concatenate(
-                [
-                    jnp.where(is_low, wide[k, :, 0:half_width], wide[k, :, half_width:]),
-                    jnp.where(is_low, narrow[k], rope[spots[k], :]),
-                ],
-                axis=1,
+    for i in range(variants):
+        for k in range(local_blocks):
+            parts.append(
+                jnp.concatenate(
+                    [
+                        jnp.where(lows[i], wide[i, k, :, 0:half_width], wide[i, k, :, half_width:]),
+                        jnp.where(lows[i], narrow[i, k], rope[spots[i * local_blocks + k], :]),
+                    ],
+                    axis=1,
+                )
             )
-        )
     own_rope[...] = rope[(local_blocks - 1) * block :, :]
     share = jnp.concatenate(parts, axis=0)
     packed[...] = dot(pick, share).astype(bf16)
@@ -188,13 +197,24 @@
             outgoing[v, at : at + height, :] = parts[k][v]
 
 
-def spread_kernel(staged, outgoing):
-    side, height, _ = outgoing.shape
-    share = height // side
-    for v in range(side):
-        piece = staged[v, 0:share, :]
-        for u in range(side):
-            outgoing[u, v * share : (v + 1) * share, :] = piece
+def spread_kernel(share, staged, outgoing):
+    side = outgoing.shape[0]
+    lane_low = (lax.broadcasted_iota(jnp.int32, (share, 128), 1) < 64).astype(f32)
+    third, fourth = staged[2, 0:share, :], staged[3, 0:share, :]
+    rope = third[:, 256:384] * lane_low.astype(bf16) + fourth[:, 256:384] * (
+        1.0 - lane_low
+    ).astype(bf16)
+    long = share * 2 // 3
+    rest = share - long
+    for u in range(side):
+        outgoing[u, 0:share, :] = staged[0, 0:share, :]
+        outgoing[u, share : 2 * share, :] = staged[1, 0:share, :]
+        outgoing[u, 2 * share : 3 * share, 0:256] = third[:, 0:256]
+        outgoing[u, 2 * share : 3 * share, 256:384] = rope
+        at = 3 * share
+        outgoing[u, at : at + long, 0:256] = fourth[0:long, 0:256]
+        outgoing[u, at : at + rest, 256:384] = fourth[long:, 0:128]
+        outgoing[u, at + rest : at + long, 256:384] = fourth[long:, 128:256]
 
 
 def compute_kernel(
@@ -223,8 +243,8 @@
     grad_keys,
     sems,
 ):
-    sources, share_rows, lanes = spread_shares.shape
     step = staged.shape[0]
+    sources = step * step
     groups = sources // 2
     tokens, total = bias.shape
     block = own_rope.shape[0]
@@ -234,7 +254,8 @@
     query_rows = target_rows.shape[0]
     heads = query_rows // tokens
     index_rows = logit_rows.shape[0]
-    remote = groups * share_rows
+    remote = total - block
+    share_rows = remote // groups
     tile = 2 * 128
     tiles = total // tile
     score_rows = step * query_rows
@@ -253,15 +274,36 @@
     for copy in copies:
         copy.start()
 
-    for g in range(groups):
-        at = slice(g * share_rows, (g + 1) * share_rows)
-        x, y = g // step, g % step
-        low = jnp.where(core == 0, y * step + x, x * step + y)
-        x = x + step // 2
-        high = jnp.where(core == 0, y * step + x, x * step + y)
-        keys[at, 0:half_width] = spread_shares[low, :, 0:half_width]
-        index_k[at, :] = spread_shares[low, :, half_width:]
-        keys[at, half_width : latent_width + 128] = spread_shares[high]
+    long = share_rows * 2 // 3
+    short = share_rows - long
+    last = 3 * share_rows
+    under = lax.broadcasted_iota(jnp.int32, (share_rows, 128), 1) < 64
+    middle_lanes = slice(half_width, latent_width)
+    rope_lanes = slice(latent_width, latent_width + 128)
+    for u in range(step):
+        for i in range(2):
+            g = i * step + u
+            at = slice(g * share_rows, (g + 1) * share_rows)
+            low = slice(i * share_rows, (i + 1) * share_rows)
+            keys[at, 0:half_width] = spread_shares[u, low, 0:half_width]
+            index_k[at, :] = spread_shares[u, low, half_width:]
+        one = slice(u * share_rows, (u + 1) * share_rows)
+        two = slice((step + u) * share_rows, (step + u + 1) * share_rows)
+        keys[one, middle_lanes] = spread_shares[u, 2 * share_rows : last, 0:half_width]
+        top = slice((step + u) * share_rows, (step + u) * share_rows + long)
+        low = slice((step + u) * share_rows + long, (step + u + 1) * share_rows)
+        keys[top, middle_lanes] = spread_shares[u, last : last + long, 0:half_width]
+        keys[low, middle_lanes] = jnp.concatenate(
+            [
+                spread_shares[u, last : last + short, half_width:],
+                spread_shares[u, last + short : last + long, half_width:],
+            ],
+            axis=1,
+        )
+        rope = spread_shares[u, 2 * share_rows : last, half_width:].astype(f32)
+        swapped = pltpu.roll(rope, 64, 1)
+        keys[one, rope_lanes] = jnp.where(under, rope, swapped).astype(bf16)
+        keys[two, rope_lanes] = jnp.where(under, swapped, rope).astype(bf16)
     keys[remote:total, latent_width : latent_width + 128] = own_rope[...]
     keys[:, latent_width + 128 :] = key_bias[...]
     target_rows[...] = jnp.zeros_like(target_rows)
@@ -556,12 +598,12 @@
         in_specs=[in_place] * 4,
         out_specs=(in_vmem, in_vmem),
         scratch_shapes=[
-            pltpu.VMEM((local_blocks, rows, latent_width), bf16),
-            pltpu.VMEM((local_blocks, rows, index_width), bf16),
+            pltpu.VMEM((2, local_blocks, rows, latent_width), bf16),
+            pltpu.VMEM((2, local_blocks, rows, index_width), bf16),
             pltpu.VMEM((rope_width, local_blocks * block), bf16),
             pltpu.VMEM((local_blocks * block, 2 * rope_width), bf16),
             pltpu.VMEM((slot_count, seq_count), jnp.int32),
-            pltpu.SemaphoreType.DMA((2 + 2 * local_blocks,)),
+            pltpu.SemaphoreType.DMA((2 + 4 * local_blocks,)),
         ],
         compiler_params=pltpu.CompilerParams(vmem_limit_bytes=60 * 1024 * 1024),
     )(sel_blocks.T, latent_cache, rope_keys.T, index_keys)
@@ -612,8 +654,8 @@
     later = (bias, key_bias, own_rope, slot_of, owner)
     staged, later = exchange_alone(outgoing, axes, later, lines(side, seq_count, False))
     spread = pl.pallas_call(
-        spread_kernel,
-        out_shape=jax.ShapeDtypeStruct((side, side * share_rows, lanes), bf16),
+        functools.partial(spread_kernel, share_rows),
+        out_shape=jax.ShapeDtypeStruct((side, share_rows * 11 // 3, lanes), bf16),
         in_specs=[in_vmem],
         out_specs=in_vmem,
         compiler_params=pltpu.CompilerParams(vmem_limit_bytes=16 * 1024 * 1024),
@@ -648,7 +690,7 @@
         compiler_params=pltpu.CompilerParams(vmem_limit_bytes=36 * 1024 * 1024),
     )(
         staged,
-        spread.reshape(head_count, share_rows, lanes),
+        spread,
         bias,
         key_bias,
         own_rope,

time: 147 us -> 146 us (level)
  no operation moved by 1% of the time
where the time goes in v5:
time: 146 us; the launch traced here: 145 us
  blocking collectives  86.2 us (59%)
  starting transfers between devices  27 us (18%)
  Pallas kernels  14 us (10%)
  waiting for transfers between devices  13.2 us (9%)
  local copies, waits for them, and re-layouts  3.19 us (2%)
    all_to_all x5, blocking collectives, exchange(): lax.all_to_all(array, axis, split_axis=0, concat_axis=0, tiled=True, axis...  86.2 us
    all_to_all x1, starting transfers between devices, exchange(): lax.all_to_all(array, axis, split_axis=0, concat_axis=0, tiled=True, axis...  15.5 us
    ppermute x3, starting transfers between devices, body(): parts[k] = lax.ppermute(parts[k], axes, shift_along_u(side, seq_count, k))  11.6 us
    pallas_call x1, Pallas kernels, body(): pl.pallas_call(functools.partial(compute_kernel, loss_weight, index_scale...  9.26 us
    all_to_all x1, waiting for transfers between devices, exchange(): lax.all_to_all(array, axis, split_axis=0, concat_axis=0, tiled=True, axis...  7.89 us
    ppermute x3, waiting for transfers between devices, body(): parts[k] = lax.ppermute(parts[k], axes, shift_along_u(side, seq_count, k))  5.28 us
  transfers between devices with their start and end apart: 4, of which 3 were waited for; matrix products, arithmetic and copies ran while one was open for 2% of the time, Pallas kernels for 0%

profile of v5, /device:TPU:6, one launch (start us, length us, event | category | flops | bytes accessed | tf_op | source)
XLA Modules:
  0.0 145.4 jit_solution(6564289745150400391)
XLA Ops:
  0.6 0.0 copy-start.3
  0.6 0.0 copy-start.4
  0.7 0.0 copy-start.1
  0.7 2.4 %shard_map.103 = (bf16[512,384]{1,0:T(8,128)(2,1)}, bf16[128,128]{1,0:T(8,128)(2,1)}) custom-call(s32[16,32]{1,0:T(8,128)} %bitcast.21, bf16[512,512]{1,0:T(8,128)(2,1)} %latent.3, bf16[64,512]{1,0:T(8,128)(2,1)} %bitcast.31, bf16[512,128]{1,0:T(8,128)(2,1)} %index.3), custom_call_target="tpu_custom_call" | custom-call | tf_op jit(solution)/shard_map/pallas_call | solution.py:592
  3.0 15.5 %all-to-all-start = ((bf16[32,16,384]{2,1,0:T(8,128)(2,1)}), bf16[32,16,384]{2,1,0:T(8,128)(2,1)S(1)}, u32[]{:S(2)}, u32[]{:S(2)}) async-start(bf16[32,16,384]{2,1,0:T(8,128)(2,1)} %bitcast.29), calls=%async_computation | async-start | bytes 786432 | tf_op jit(solution)/shard_map/all_to_all | solution.py:515
  18.5 0.8 copy.25
  19.3 0.1 reshape.134
  19.5 0.2 copy.29
  19.7 1.1 copy.24
  20.8 0.1 pad_maximum_fusion.1.rope
  20.9 0.0 copy-done.3
  20.9 0.0 copy-done.4
  20.9 0.0 copy-done.1
  21.0 0.5 shard_map.104
  21.4 3.5 %collective-permute-start = (bf16[4,112,384]{2,1,0:T(8,128)(2,1)S(1)}, bf16[4,112,384]{2,1,0:T(8,128)(2,1)S(1)}, u32[]{:S(2)}, u32[]{:S(2)}) collective-permute-start(bf16[4,112,384]{2,1,0:T(8,128)(2,1)S(1)} %get-tuple-element.77), channel_id=1, source_target_pairs={{0,32},{128,160},{256,288},{384,416},{32,64},{160,192},{288,320},{... | collective-permute-start | bytes 1032200 | tf_op jit(solution)/shard_map/ppermute | solution.py:642
  24.9 4.8 %collective-permute-start.1 = (bf16[4,112,384]{2,1,0:T(8,128)(2,1)S(1)}, bf16[4,112,384]{2,1,0:T(8,128)(2,1)S(1)}, u32[]{:S(2)}, u32[]{:S(2)}) collective-permute-start(bf16[4,112,384]{2,1,0:T(8,128)(2,1)S(1)} %get-tuple-element.78), channel_id=1, source_target_pairs={{0,64},{128,192},{256,320},{384,448},{32,96},{160,224},{288,352},{... | collective-permute-start | bytes 1032200 | tf_op jit(solution)/shard_map/ppermute | solution.py:642
  29.7 3.3 %collective-permute-start.2 = (bf16[4,112,384]{2,1,0:T(8,128)(2,1)S(1)}, bf16[4,112,384]{2,1,0:T(8,128)(2,1)S(1)}, u32[]{:S(2)}, u32[]{:S(2)}) collective-permute-start(bf16[4,112,384]{2,1,0:T(8,128)(2,1)S(1)} %get-tuple-element.79), channel_id=1, source_target_pairs={{0,96},{128,224},{256,352},{384,480},{32,0},{160,128},{288,256},{4... | collective-permute-start | bytes 1032200 | tf_op jit(solution)/shard_map/ppermute | solution.py:642
  33.0 0.2 dynamic-slice_reduce_fusion
  33.3 0.1 slice.52
  33.3 0.1 slice.51
  33.4 0.1 select_reduce_fusion.1
  33.5 0.1 fusion.2
  33.6 0.0 collective-permute-done.in1
  33.6 3.1 %collective-permute-done.1.in2 = bf16[4,112,384]{2,1,0:T(8,128)(2,1)S(1)} collective-permute-done((bf16[4,112,384]{2,1,0:T(8,128)(2,1)S(1)}, bf16[4,112,384]{2,1,0:T(8,128)(2,1)S(1)}, u32[]{:S(2)}, u32[]{:S(2)}) %collective-permute-start.1) | collective-permute-done | bytes 344096 | tf_op jit(solution)/shard_map/ppermute | solution.py:642
  36.7 2.2 %collective-permute-done.2.in3 = bf16[4,112,384]{2,1,0:T(8,128)(2,1)S(1)} collective-permute-done((bf16[4,112,384]{2,1,0:T(8,128)(2,1)S(1)}, bf16[4,112,384]{2,1,0:T(8,128)(2,1)S(1)}, u32[]{:S(2)}, u32[]{:S(2)}) %collective-permute-start.2) | collective-permute-done | bytes 344096 | tf_op jit(solution)/shard_map/ppermute | solution.py:642
  38.9 7.9 %all-to-all-done.fetched = bf16[32,16,384]{2,1,0:T(8,128)(2,1)S(1)} async-done(((bf16[32,16,384]{2,1,0:T(8,128)(2,1)}), bf16[32,16,384]{2,1,0:T(8,128)(2,1)S(1)}, u32[]{:S(2)}, u32[]{:S(2)}) %all-to-all-start) | async-done | bytes 393248 | tf_op jit(solution)/shard_map/all_to_all | solution.py:515
  46.8 0.9 shard_map.105
  47.6 19.1 %all_to_all.30.staged = bf16[4,688,384]{2,1,0:T(8,128)(2,1)S(1)} all-to-all(bf16[4,688,384]{2,1,0:T(8,128)(2,1)S(1)} %shard_map.105), channel_id=1, replica_groups={{0,128,256,384},{32,160,288,416},{64,192,320,448},{96,224,352,480},{1,3..., dimensions={0} | all-to-all | bytes 4227072 | tf_op jit(solution)/shard_map/all_to_all | solution.py:515
  66.7 0.2 shard_map.106
  67.0 0.0 copy-start
  67.0 0.0 copy-start.2
  67.0 0.0 copy-start.5
  67.0 24.2 %all_to_all.31.spread_shares = bf16[4,880,384]{2,1,0:T(8,128)(2,1)S(1)} all-to-all(bf16[4,880,384]{2,1,0:T(8,128)(2,1)S(1)} %shard_map.106), channel_id=1, replica_groups={{0,32,64,96},{128,160,192,224},{256,288,320,352},{384,416,448,480},{1,1..., dimensions={0} | all-to-all | bytes 5406720 | tf_op jit(solution)/shard_map/all_to_all | solution.py:515
  91.1 0.0 copy-done
  91.2 0.0 copy-done.2
  91.2 0.0 copy-done.5
  91.2 9.3 %shard_map.107 = (bf16[16,32,128]{2,1,0:T(8,128)(2,1)S(1)}, bf16[16,16,128]{2,1,0:T(8,128)(2,1)S(1)}, bf16[16,128,128]{2,1,0:T(8,128)(2,1)S(1)}) custom-call(bf16[4,688,384]{2,1,0:T(8,128)(2,1)S(1)} %all_to_all.30.staged, bf16[4,880,384]{2,1,0:T(8,128)(2,1)S(1)} %all_to_all.31.spread_shares, f32[8,2048]{1,0:T(8,128)S(1)} %get-tuple-element.104.bias, ...), custom_call_target="tpu_custom_call" | custom-call | tf_op jit(solution)/shard_map/pallas_call | solution.py:668
  100.4 13.0 %all_to_all.32 = bf16[16,128,128]{2,1,0:T(8,128)(2,1)S(1)} all-to-all(bf16[16,128,128]{2,1,0:T(8,128)(2,1)S(1)} %get-tuple-element.112), channel_id=1, replica_groups=mesh['head'=16,'seq'=32] {'head'}, dimensions={0} | all-to-all | bytes 1048576 | tf_op jit(solution)/shard_map/all_to_all | solution.py:515
  113.4 0.1 convert_reduce_fusion
  113.5 0.6 gather_fusion
  114.1 0.1 select_convert_fusion
  114.3 17.9 %all_to_all.33 = bf16[32,8,128]{2,1,0:T(8,128)(2,1)S(1)} all-to-all(bf16[32,8,128]{2,1,0:T(8,128)(2,1)S(1)} %select_convert_fusion), channel_id=1, replica_groups=mesh['head'=16,'seq'=32] {'seq'}, dimensions={0} | all-to-all | bytes 131072 | tf_op jit(solution)/shard_map/all_to_all | solution.py:515
  132.2 0.2 multiply_reduce_fusion
  132.5 12.1 %all_to_all.34.final = bf16[16,80,128]{2,1,0:T(8,128)(2,1)S(1)} all-to-all(bf16[16,80,128]{2,1,0:T(8,128)(2,1)S(1)} %pad_maximum_fusion), channel_id=1, replica_groups=mesh['head'=16,'seq'=32] {'head'}, dimensions={0} | all-to-all | bytes 655360 | tf_op jit(solution)/shard_map/all_to_all | solution.py:515
  144.6 0.9 shard_map.108
  (20 shorter events, 0.2 us)
Async XLA Ops:
  0.6 20.3 %copy-start.3 = (s32[32,16]{0,1:T(8,128)S(1)}, s32[32,16]{0,1:T(8,128)}, u32[]{:S(2)}) copy-start(s32[32,16]{0,1:T(8,128)} %param.17) | copy-start | bytes 6148
  0.6 20.3 %copy-start.4 = (bf16[128,4,128]{2,1,0:T(4,128)(2,1)S(1)}, bf16[128,4,128]{2,1,0:T(4,128)(2,1)}, u32[]{:S(2)}) copy-start(bf16[128,4,128]{2,1,0:T(4,128)(2,1)} %param.14) | copy-start | bytes 393220
  0.7 20.3 %copy-start.1 = (bf16[128,8,512]{2,1,0:T(8,128)(2,1)S(1)}, bf16[128,8,512]{2,1,0:T(8,128)(2,1)}, u32[]{:S(2)}) copy-start(bf16[128,8,512]{2,1,0:T(8,128)(2,1)} %param.10) | copy-start | bytes 3145732
  3.0 43.7 %all-to-all-start = ((bf16[32,16,384]{2,1,0:T(8,128)(2,1)}), bf16[32,16,384]{2,1,0:T(8,128)(2,1)S(1)}, u32[]{:S(2)}, u32[]{:S(2)}) async-start(bf16[32,16,384]{2,1,0:T(8,128)(2,1)} %bitcast.29), calls=%async_computation | async-start | bytes 786432 | tf_op jit(solution)/shard_map/all_to_all | solution.py:515
  21.4 12.2 %collective-permute-start = (bf16[4,112,384]{2,1,0:T(8,128)(2,1)S(1)}, bf16[4,112,384]{2,1,0:T(8,128)(2,1)S(1)}, u32[]{:S(2)}, u32[]{:S(2)}) collective-permute-start(bf16[4,112,384]{2,1,0:T(8,128)(2,1)S(1)} %get-tuple-element.77), channel_id=1, source_target_pairs={{0,32},{128,160},{256,288},{384,416},{32,64},{160,192},{288,320},{... | collective-permute-start | bytes 1032200 | tf_op jit(solution)/shard_map/ppermute | solution.py:642
  24.9 11.8 %collective-permute-start.1 = (bf16[4,112,384]{2,1,0:T(8,128)(2,1)S(1)}, bf16[4,112,384]{2,1,0:T(8,128)(2,1)S(1)}, u32[]{:S(2)}, u32[]{:S(2)}) collective-permute-start(bf16[4,112,384]{2,1,0:T(8,128)(2,1)S(1)} %get-tuple-element.78), channel_id=1, source_target_pairs={{0,64},{128,192},{256,320},{384,448},{32,96},{160,224},{288,352},{... | collective-permute-start | bytes 1032200 | tf_op jit(solution)/shard_map/ppermute | solution.py:642
  29.7 9.1 %collective-permute-start.2 = (bf16[4,112,384]{2,1,0:T(8,128)(2,1)S(1)}, bf16[4,112,384]{2,1,0:T(8,128)(2,1)S(1)}, u32[]{:S(2)}, u32[]{:S(2)}) collective-permute-start(bf16[4,112,384]{2,1,0:T(8,128)(2,1)S(1)} %get-tuple-element.79), channel_id=1, source_target_pairs={{0,96},{128,224},{256,352},{384,480},{32,0},{160,128},{288,256},{4... | collective-permute-start | bytes 1032200 | tf_op jit(solution)/shard_map/ppermute | solution.py:642
  67.0 24.2 %copy-start = (bf16[512,512]{1,0:T(8,128)(2,1)S(1)}, bf16[512,512]{1,0:T(8,128)(2,1)}, u32[]{:S(2)}) copy-start(bf16[512,512]{1,0:T(8,128)(2,1)} %latent.3) | copy-start | bytes 1572868
  67.0 24.2 %copy-start.2 = (bf16[512,128]{1,0:T(8,128)(2,1)S(1)}, bf16[512,128]{1,0:T(8,128)(2,1)}, u32[]{:S(2)}) copy-start(bf16[512,128]{1,0:T(8,128)(2,1)} %index.3) | copy-start | bytes 393220
  67.0 24.2 %copy-start.5 = (bf16[128,128]{1,0:T(8,128)(2,1)S(1)}, bf16[128,128]{1,0:T(8,128)(2,1)}, u32[]{:S(2)}) copy-start(bf16[128,128]{1,0:T(8,128)(2,1)} %get-tuple-element.106.own_rope) | copy-start | bytes 98308

commit v6 on v5

--- a/solution.py
+++ b/solution.py
@@ -51,28 +51,25 @@
 ):
     slots, destinations = sel_turned.shape
     variants, local_blocks, rows, latent_width = wide.shape
-    block = latent.shape[0] // local_blocks
+    block = latent.shape[1]
     half_width = latent_width // 2
     side = groups // 2
     head = lax.axis_index("head")
     x, y = lax.div(head, side), lax.rem(head, side)
-    spots = []
+    firsts = []
     lows = []
-    count = variants * local_blocks
     copies = [pltpu.make_async_copy(rope_turned, turned, sems.at[0])]
     table_copy = pltpu.make_async_copy(sel_turned, table, sems.at[1])
     table_copy.start()
     for i, (u, v) in enumerate(((y, x), (x, y))):
-        group = lax.rem(v, 2) * side + u
+        first = pl.multiple_of((lax.rem(v, 2) * side + u) * rows, rows)
+        at = pl.ds(first, rows)
+        firsts.append(first)
         lows.append(v < side // 2)
-        for k in range(local_blocks):
-            at = pl.ds(pl.multiple_of(k * block + group * rows, rows), rows)
-            n = i * local_blocks + k
-            spots.append(at)
-            copies.append(pltpu.make_async_copy(latent.at[at], wide.at[i, k], sems.at[2 + n]))
-            copies.append(
-                pltpu.make_async_copy(index.at[at], narrow.at[i, k], sems.at[2 + count + n])
-            )
+        copies.append(pltpu.make_async_copy(latent.at[:, at], wide.at[i], sems.at[2 + i]))
+        copies.append(
+            pltpu.make_async_copy(index.at[:, at], narrow.at[i], sems.at[2 + variants + i])
+        )
     for copy in copies:
         copy.start()
 
@@ -102,7 +99,11 @@
                 jnp.concatenate(
                     [
                         jnp.where(lows[i], wide[i, k, :, 0:half_width], wide[i, k, :, half_width:]),
-                        jnp.where(lows[i], narrow[i, k], rope[spots[i * local_blocks + k], :]),
+                        jnp.where(
+                            lows[i],
+                            narrow[i, k],
+                            rope[pl.ds(pl.multiple_of(k * block + firsts[i], rows), rows), :],
+                        ),
                     ],
                     axis=1,
                 )
@@ -280,30 +281,31 @@
     under = lax.broadcasted_iota(jnp.int32, (share_rows, 128), 1) < 64
     middle_lanes = slice(half_width, latent_width)
     rope_lanes = slice(latent_width, latent_width + 128)
-    for u in range(step):
-        for i in range(2):
-            g = i * step + u
-            at = slice(g * share_rows, (g + 1) * share_rows)
-            low = slice(i * share_rows, (i + 1) * share_rows)
-            keys[at, 0:half_width] = spread_shares[u, low, 0:half_width]
-            index_k[at, :] = spread_shares[u, low, half_width:]
-        one = slice(u * share_rows, (u + 1) * share_rows)
-        two = slice((step + u) * share_rows, (step + u + 1) * share_rows)
-        keys[one, middle_lanes] = spread_shares[u, 2 * share_rows : last, 0:half_width]
-        top = slice((step + u) * share_rows, (step + u) * share_rows + long)
-        low = slice((step + u) * share_rows + long, (step + u + 1) * share_rows)
-        keys[top, middle_lanes] = spread_shares[u, last : last + long, 0:half_width]
-        keys[low, middle_lanes] = jnp.concatenate(
-            [
-                spread_shares[u, last : last + short, half_width:],
-                spread_shares[u, last + short : last + long, half_width:],
-            ],
-            axis=1,
-        )
+
+    def gather_keys(g):
+        i, u = g // step, g % step
+        at = slice(g * share_rows, (g + 1) * share_rows)
+        low = slice(i * share_rows, (i + 1) * share_rows)
+        keys[at, 0:half_width] = spread_shares[u, low, 0:half_width]
+        index_k[at, :] = spread_shares[u, low, half_width:]
         rope = spread_shares[u, 2 * share_rows : last, half_width:].astype(f32)
         swapped = pltpu.roll(rope, 64, 1)
-        keys[one, rope_lanes] = jnp.where(under, rope, swapped).astype(bf16)
-        keys[two, rope_lanes] = jnp.where(under, swapped, rope).astype(bf16)
+        if i == 0:
+            keys[at, middle_lanes] = spread_shares[u, 2 * share_rows : last, 0:half_width]
+            keys[at, rope_lanes] = jnp.where(under, rope, swapped).astype(bf16)
+        else:
+            top = slice(g * share_rows, g * share_rows + long)
+            end = slice(g * share_rows + long, (g + 1) * share_rows)
+            keys[top, middle_lanes] = spread_shares[u, last : last + long, 0:half_width]
+            keys[end, middle_lanes] = jnp.concatenate(
+                [
+                    spread_shares[u, last : last + short, half_width:],
+                    spread_shares[u, last + short : last + long, half_width:],
+                ],
+                axis=1,
+            )
+            keys[at, rope_lanes] = jnp.where(under, swapped, rope).astype(bf16)
+
     keys[remote:total, latent_width : latent_width + 128] = own_rope[...]
     keys[:, latent_width + 128 :] = key_bias[...]
     target_rows[...] = jnp.zeros_like(target_rows)
@@ -388,6 +390,7 @@
                 target_rows[:, at] += jnp.sum(power * state["weight"], axis=0)
 
     state = None
+    ready = 0
     for c in range(sources // step):
         score_at = slice(c * score_rows, (c + 1) * score_rows)
         rows = slice(c * chunk, (c + 1) * chunk)
@@ -397,6 +400,9 @@
         best = jnp.full((score_rows, 128), -3e38, f32)
         for k in range(tiles):
             at = tile_at[k]
+            while c == 0 and ready < min((k + 1) * tile, remote):
+                gather_keys(ready // share_rows)
+                ready += share_rows
             part = dot_last(queries, keys[at, :])
             scores[score_at, at] = part
             best = jnp.maximum(best, jnp.maximum(part[:, 0:128], part[:, 128:256]))
@@ -474,6 +480,28 @@
         both_keys = jnp.concatenate([own, rest_keys], axis=0)
         for i in range(2):
             shares[i * groups + g] = both_keys[:, i].reshape(block, index_width).astype(bf16)
+
+
+def route_kernel(local_blocks, sel_turned, collected, outgoing, own_sum):
+    slots, owners = sel_turned.shape
+    total, width = outgoing.shape[0], collected.shape[1]
+    small = total // owners
+    summed = collected[0].astype(f32)
+    for k in range(1, collected.shape[0]):
+        summed = summed + collected[k].astype(f32)
+    own_sum[...] = summed[0:small]
+    here = lax.axis_index("seq")
+    pick = (lax.broadcasted_iota(jnp.int32, (total, owners), 1) == here).astype(f32)
+    blocks = dot_last(pick, sel_turned[...].astype(f32))
+    slot = lax.broadcasted_iota(jnp.int32, (slots, width), 1) // small
+    mark = (slot == lax.broadcasted_iota(jnp.int32, (slots, width), 0)).astype(f32)
+    block = dot(blocks, mark)
+    row = lax.broadcasted_iota(jnp.int32, (total, width), 0)
+    column = lax.broadcasted_iota(jnp.int32, (total, width), 1)
+    first = (row // small * local_blocks).astype(f32)
+    chosen = (block >= first) & (block < first + local_blocks)
+    chosen = chosen & (column >= small) & (column % small == row % small)
+    outgoing[...] = dot(chosen.astype(bf16), summed.astype(bf16)).astype(bf16)
 
 
 def last_kernel(groups, index_heads, final, grad_queries, grad_weights, grad_keys):
@@ -582,9 +610,6 @@
     inside = (later >= 0) & (offsets >= 0) & (offsets < local_blocks)
     wanted = jnp.any(inside, axis=1)
     which = jnp.sum(jnp.where(inside, offsets, 0), axis=1)
-    sel_row = lax.dynamic_index_in_dim(sel_blocks, seq_index, 0, keepdims=False)
-    slot_valid = sel_row >= 0
-    source = jnp.where(slot_valid, sel_row // local_blocks, 0)
     in_vmem = pl.BlockSpec(memory_space=pltpu.VMEM)
     in_smem = pl.BlockSpec(memory_space=pltpu.SMEM)
     in_place = pl.BlockSpec(memory_space=pl.ANY)
@@ -603,10 +628,15 @@
             pltpu.VMEM((rope_width, local_blocks * block), bf16),
             pltpu.VMEM((local_blocks * block, 2 * rope_width), bf16),
             pltpu.VMEM((slot_count, seq_count), jnp.int32),
-            pltpu.SemaphoreType.DMA((2 + 4 * local_blocks,)),
+            pltpu.SemaphoreType.DMA((6,)),
         ],
         compiler_params=pltpu.CompilerParams(vmem_limit_bytes=60 * 1024 * 1024),
-    )(sel_blocks.T, latent_cache, rope_keys.T, index_keys)
+    )(
+        sel_blocks.T,
+        latent_cache.reshape(local_blocks, block, latent_width),
+        rope_keys.T,
+        index_keys.reshape(local_blocks, block, index_width),
+    )
     fetched = exchange(packed.reshape(seq_count, rows, lanes), "seq")
 
     share_rows = remote_slots * rows
@@ -647,11 +677,9 @@
         out_specs=in_vmem,
         compiler_params=pltpu.CompilerParams(vmem_limit_bytes=24 * 1024 * 1024),
     )(sel_blocks.T, fetched, *parts)
-    found = (source[1:][None, :] == jnp.arange(seq_count)[:, None]) & slot_valid[1:][None, :]
-    slot_of = jnp.sum(jnp.where(found, jnp.arange(1, slot_count)[None, :], 0), axis=1)
     owner = wanted[:, None] & (which[:, None] == jnp.arange(local_blocks)[None, :])
     owner = owner.astype(f32)
-    later = (bias, key_bias, own_rope, slot_of, owner)
+    later = (bias, key_bias, own_rope, owner)
     staged, later = exchange_alone(outgoing, axes, later, lines(side, seq_count, False))
     spread = pl.pallas_call(
         functools.partial(spread_kernel, share_rows),
@@ -660,7 +688,7 @@
         out_specs=in_vmem,
         compiler_params=pltpu.CompilerParams(vmem_limit_bytes=16 * 1024 * 1024),
     )(staged)
-    spread, (staged, bias, key_bias, own_rope, slot_of, owner) = exchange_alone(
+    spread, (staged, bias, key_bias, own_rope, owner) = exchange_alone(
         spread, axes, (staged, *later), lines(side, seq_count, True)
     )
 
@@ -698,13 +726,21 @@
         index_keys,
     )
 
-    collected, (grad_queries, grad_weights, slot_of, owner) = exchange_alone(
-        shares, "head", (grad_queries, grad_weights, slot_of, owner)
-    )
-    summed = jnp.sum(collected.astype(f32), axis=0).reshape(slot_count, small, index_width)
-    own_sum = summed[0]
+    collected, (grad_queries, grad_weights, owner) = exchange_alone(
+        shares, "head", (grad_queries, grad_weights, owner)
+    )
+    routed, own_sum = pl.pallas_call(
+        functools.partial(route_kernel, local_blocks),
+        out_shape=(
+            jax.ShapeDtypeStruct((seq_count * small, index_width), bf16),
+            jax.ShapeDtypeStruct((small, index_width), f32),
+        ),
+        in_specs=[in_vmem, in_vmem],
+        out_specs=(in_vmem, in_vmem),
+        compiler_params=pltpu.CompilerParams(vmem_limit_bytes=16 * 1024 * 1024),
+    )(sel_blocks.T, collected)
     returned, (own_sum, grad_queries, grad_weights, owner) = exchange_alone(
-        jnp.take(summed, slot_of, axis=0).astype(bf16),
+        routed.reshape(seq_count, small, index_width),
         "seq",
         (own_sum, grad_queries, grad_weights, owner),
     )

time: 146 us -> 146 us (level)
  no operation moved by 1% of the time
where the time goes in v6:
time: 146 us; the launch traced here: 145 us
  blocking collectives  86.2 us (59%)
  starting transfers between devices  27 us (18%)
  Pallas kernels  14.1 us (10%)
  waiting for transfers between devices  13.6 us (9%)
  local copies, waits for them, and re-layouts  2.25 us (2%)
    all_to_all x5, blocking collectives, exchange(): lax.all_to_all(array, axis, split_axis=0, concat_axis=0, tiled=True, axis...  86.2 us
    all_to_all x1, starting transfers between devices, exchange(): lax.all_to_all(array, axis, split_axis=0, concat_axis=0, tiled=True, axis...  15.5 us
    ppermute x3, starting transfers between devices, body(): parts[k] = lax.ppermute(parts[k], axes, shift_along_u(side, seq_count, k))  11.5 us
    pallas_call x1, Pallas kernels, body(): pl.pallas_call(functools.partial(compute_kernel, loss_weight, index_scale...  9.07 us
    all_to_all x1, waiting for transfers between devices, exchange(): lax.all_to_all(array, axis, split_axis=0, concat_axis=0, tiled=True, axis...  7.89 us
    ppermute x3, waiting for transfers between devices, body(): parts[k] = lax.ppermute(parts[k], axes, shift_along_u(side, seq_count, k))  5.74 us
  transfers between devices with their start and end apart: 4, of which 3 were waited for; matrix products, arithmetic and copies ran while one was open for 2% of the time, Pallas kernels for 0%

profile of v6, /device:TPU:6, one launch (start us, length us, event | category | flops | bytes accessed | tf_op | source)
XLA Modules:
  0.0 144.6 jit_solution(16453743475173149487)
XLA Ops:
  0.6 0.0 copy-start.3
  0.6 0.0 copy-start.4
  0.7 0.0 copy-start.1
  0.7 2.2 %shard_map.103 = (bf16[512,384]{1,0:T(8,128)(2,1)}, bf16[128,128]{1,0:T(8,128)(2,1)}) custom-call(s32[16,32]{1,0:T(8,128)} %bitcast.25, bf16[4,128,512]{2,1,0:T(8,128)(2,1)} %bitcast.22, bf16[64,512]{1,0:T(8,128)(2,1)} %bitcast.36, bf16[4,128,128]{2,1,0:T(8,128)(2,1)} %bitcast.24), custom_call_target="tpu_custom_call" | custom-call | tf_op jit(solution)/shard_map/pallas_call | solution.py:617
  2.9 15.5 %all-to-all-start = ((bf16[32,16,384]{2,1,0:T(8,128)(2,1)}), bf16[32,16,384]{2,1,0:T(8,128)(2,1)S(1)}, u32[]{:S(2)}, u32[]{:S(2)}) async-start(bf16[32,16,384]{2,1,0:T(8,128)(2,1)} %bitcast.35), calls=%async_computation | async-start | bytes 786432 | tf_op jit(solution)/shard_map/all_to_all | solution.py:543
  18.4 0.8 copy.25
  19.2 0.1 reshape.129
  19.3 0.2 copy.29
  19.5 1.1 copy.24
  20.7 0.1 pad_maximum_fusion.1.rope
  20.8 0.0 copy-done.3
  20.8 0.0 copy-done.4
  20.8 0.0 copy-done.1
  20.8 0.5 shard_map.104
  21.3 3.5 %collective-permute-start = (bf16[4,112,384]{2,1,0:T(8,128)(2,1)S(1)}, bf16[4,112,384]{2,1,0:T(8,128)(2,1)S(1)}, u32[]{:S(2)}, u32[]{:S(2)}) collective-permute-start(bf16[4,112,384]{2,1,0:T(8,128)(2,1)S(1)} %get-tuple-element.73), channel_id=1, source_target_pairs={{0,32},{128,160},{256,288},{384,416},{32,64},{160,192},{288,320},{... | collective-permute-start | bytes 1032200 | tf_op jit(solution)/shard_map/ppermute | solution.py:672
  24.8 4.8 %collective-permute-start.1 = (bf16[4,112,384]{2,1,0:T(8,128)(2,1)S(1)}, bf16[4,112,384]{2,1,0:T(8,128)(2,1)S(1)}, u32[]{:S(2)}, u32[]{:S(2)}) collective-permute-start(bf16[4,112,384]{2,1,0:T(8,128)(2,1)S(1)} %get-tuple-element.74), channel_id=1, source_target_pairs={{0,64},{128,192},{256,320},{384,448},{32,96},{160,224},{288,352},{... | collective-permute-start | bytes 1032200 | tf_op jit(solution)/shard_map/ppermute | solution.py:672
  29.6 3.3 %collective-permute-start.2 = (bf16[4,112,384]{2,1,0:T(8,128)(2,1)S(1)}, bf16[4,112,384]{2,1,0:T(8,128)(2,1)S(1)}, u32[]{:S(2)}, u32[]{:S(2)}) collective-permute-start(bf16[4,112,384]{2,1,0:T(8,128)(2,1)S(1)} %get-tuple-element.75), channel_id=1, source_target_pairs={{0,96},{128,224},{256,352},{384,480},{32,0},{160,128},{288,256},{4... | collective-permute-start | bytes 1032200 | tf_op jit(solution)/shard_map/ppermute | solution.py:672
  32.9 0.1 fusion.2
  33.0 0.0 collective-permute-done.in1
  33.0 3.6 %collective-permute-done.1.in2 = bf16[4,112,384]{2,1,0:T(8,128)(2,1)S(1)} collective-permute-done((bf16[4,112,384]{2,1,0:T(8,128)(2,1)S(1)}, bf16[4,112,384]{2,1,0:T(8,128)(2,1)S(1)}, u32[]{:S(2)}, u32[]{:S(2)}) %collective-permute-start.1) | collective-permute-done | bytes 344096 | tf_op jit(solution)/shard_map/ppermute | solution.py:672
  36.6 2.2 %collective-permute-done.2.in3 = bf16[4,112,384]{2,1,0:T(8,128)(2,1)S(1)} collective-permute-done((bf16[4,112,384]{2,1,0:T(8,128)(2,1)S(1)}, bf16[4,112,384]{2,1,0:T(8,128)(2,1)S(1)}, u32[]{:S(2)}, u32[]{:S(2)}) %collective-permute-start.2) | collective-permute-done | bytes 344096 | tf_op jit(solution)/shard_map/ppermute | solution.py:672
  38.7 7.9 %all-to-all-done.fetched = bf16[32,16,384]{2,1,0:T(8,128)(2,1)S(1)} async-done(((bf16[32,16,384]{2,1,0:T(8,128)(2,1)}), bf16[32,16,384]{2,1,0:T(8,128)(2,1)S(1)}, u32[]{:S(2)}, u32[]{:S(2)}) %all-to-all-start) | async-done | bytes 393248 | tf_op jit(solution)/shard_map/all_to_all | solution.py:543
  46.6 0.9 shard_map.105
  47.5 19.1 %all_to_all.30.staged = bf16[4,688,384]{2,1,0:T(8,128)(2,1)S(1)} all-to-all(bf16[4,688,384]{2,1,0:T(8,128)(2,1)S(1)} %shard_map.105), channel_id=1, replica_groups={{0,128,256,384},{32,160,288,416},{64,192,320,448},{96,224,352,480},{1,3..., dimensions={0} | all-to-all | bytes 4227072 | tf_op jit(solution)/shard_map/all_to_all | solution.py:543
  66.6 0.2 shard_map.106
  66.8 0.0 copy-start
  66.8 0.0 copy-start.2
  66.8 0.0 copy-start.5
  66.8 24.2 %all_to_all.31.spread_shares = bf16[4,880,384]{2,1,0:T(8,128)(2,1)S(1)} all-to-all(bf16[4,880,384]{2,1,0:T(8,128)(2,1)S(1)} %shard_map.106), channel_id=1, replica_groups={{0,32,64,96},{128,160,192,224},{256,288,320,352},{384,416,448,480},{1,1..., dimensions={0} | all-to-all | bytes 5406720 | tf_op jit(solution)/shard_map/all_to_all | solution.py:543
  91.0 0.0 copy-done
  91.0 0.0 copy-done.2
  91.0 0.0 copy-done.5
  91.0 9.1 %shard_map.107 = (bf16[16,32,128]{2,1,0:T(8,128)(2,1)S(1)}, bf16[16,16,128]{2,1,0:T(8,128)(2,1)S(1)}, bf16[16,128,128]{2,1,0:T(8,128)(2,1)S(1)}) custom-call(bf16[4,688,384]{2,1,0:T(8,128)(2,1)S(1)} %all_to_all.30.staged, bf16[4,880,384]{2,1,0:T(8,128)(2,1)S(1)} %all_to_all.31.spread_shares, f32[8,2048]{1,0:T(8,128)S(1)} %get-tuple-element.97.bias, ...), custom_call_target="tpu_custom_call" | custom-call | tf_op jit(solution)/shard_map/pallas_call | solution.py:696
  100.1 13.0 %all_to_all.32.collected = bf16[16,128,128]{2,1,0:T(8,128)(2,1)S(1)} all-to-all(bf16[16,128,128]{2,1,0:T(8,128)(2,1)S(1)} %get-tuple-element.104), channel_id=1, replica_groups=mesh['head'=16,'seq'=32] {'head'}, dimensions={0} | all-to-all | bytes 1048576 | tf_op jit(solution)/shard_map/all_to_all | solution.py:543
  113.1 0.4 shard_map.108
  113.5 17.9 %all_to_all.33 = bf16[32,8,128]{2,1,0:T(8,128)(2,1)S(1)} all-to-all(bf16[32,8,128]{2,1,0:T(8,128)(2,1)S(1)} %bitcast.31), channel_id=1, replica_groups=mesh['head'=16,'seq'=32] {'seq'}, dimensions={0} | all-to-all | bytes 131072 | tf_op jit(solution)/shard_map/all_to_all | solution.py:543
  131.4 0.2 multiply_reduce_fusion
  131.7 12.1 %all_to_all.34.final = bf16[16,80,128]{2,1,0:T(8,128)(2,1)S(1)} all-to-all(bf16[16,80,128]{2,1,0:T(8,128)(2,1)S(1)} %pad_maximum_fusion), channel_id=1, replica_groups=mesh['head'=16,'seq'=32] {'head'}, dimensions={0} | all-to-all | bytes 655360 | tf_op jit(solution)/shard_map/all_to_all | solution.py:543
  143.8 0.9 shard_map.109
  (13 shorter events, 0.2 us)
Async XLA Ops:
  0.6 20.1 %copy-start.3 = (s32[32,16]{0,1:T(8,128)S(1)}, s32[32,16]{0,1:T(8,128)}, u32[]{:S(2)}) copy-start(s32[32,16]{0,1:T(8,128)} %param.17) | copy-start | bytes 6148
  0.6 20.1 %copy-start.4 = (bf16[128,4,128]{2,1,0:T(4,128)(2,1)S(1)}, bf16[128,4,128]{2,1,0:T(4,128)(2,1)}, u32[]{:S(2)}) copy-start(bf16[128,4,128]{2,1,0:T(4,128)(2,1)} %param.14) | copy-start | bytes 393220
  0.7 20.1 %copy-start.1 = (bf16[128,8,512]{2,1,0:T(8,128)(2,1)S(1)}, bf16[128,8,512]{2,1,0:T(8,128)(2,1)}, u32[]{:S(2)}) copy-start(bf16[128,8,512]{2,1,0:T(8,128)(2,1)} %param.10) | copy-start | bytes 3145732
  2.9 43.7 %all-to-all-start = ((bf16[32,16,384]{2,1,0:T(8,128)(2,1)}), bf16[32,16,384]{2,1,0:T(8,128)(2,1)S(1)}, u32[]{:S(2)}, u32[]{:S(2)}) async-start(bf16[32,16,384]{2,1,0:T(8,128)(2,1)} %bitcast.35), calls=%async_computation | async-start | bytes 786432 | tf_op jit(solution)/shard_map/all_to_all | solution.py:543
  21.3 11.7 %collective-permute-start = (bf16[4,112,384]{2,1,0:T(8,128)(2,1)S(1)}, bf16[4,112,384]{2,1,0:T(8,128)(2,1)S(1)}, u32[]{:S(2)}, u32[]{:S(2)}) collective-permute-start(bf16[4,112,384]{2,1,0:T(8,128)(2,1)S(1)} %get-tuple-element.73), channel_id=1, source_target_pairs={{0,32},{128,160},{256,288},{384,416},{32,64},{160,192},{288,320},{... | collective-permute-start | bytes 1032200 | tf_op jit(solution)/shard_map/ppermute | solution.py:672
  24.8 11.8 %collective-permute-start.1 = (bf16[4,112,384]{2,1,0:T(8,128)(2,1)S(1)}, bf16[4,112,384]{2,1,0:T(8,128)(2,1)S(1)}, u32[]{:S(2)}, u32[]{:S(2)}) collective-permute-start(bf16[4,112,384]{2,1,0:T(8,128)(2,1)S(1)} %get-tuple-element.74), channel_id=1, source_target_pairs={{0,64},{128,192},{256,320},{384,448},{32,96},{160,224},{288,352},{... | collective-permute-start | bytes 1032200 | tf_op jit(solution)/shard_map/ppermute | solution.py:672
  29.6 9.1 %collective-permute-start.2 = (bf16[4,112,384]{2,1,0:T(8,128)(2,1)S(1)}, bf16[4,112,384]{2,1,0:T(8,128)(2,1)S(1)}, u32[]{:S(2)}, u32[]{:S(2)}) collective-permute-start(bf16[4,112,384]{2,1,0:T(8,128)(2,1)S(1)} %get-tuple-element.75), channel_id=1, source_target_pairs={{0,96},{128,224},{256,352},{384,480},{32,0},{160,128},{288,256},{4... | collective-permute-start | bytes 1032200 | tf_op jit(solution)/shard_map/ppermute | solution.py:672
  66.8 24.2 %copy-start = (bf16[512,512]{1,0:T(8,128)(2,1)S(1)}, bf16[512,512]{1,0:T(8,128)(2,1)}, u32[]{:S(2)}) copy-start(bf16[512,512]{1,0:T(8,128)(2,1)} %latent.1) | copy-start | bytes 1572868
  66.8 24.2 %copy-start.2 = (bf16[512,128]{1,0:T(8,128)(2,1)S(1)}, bf16[512,128]{1,0:T(8,128)(2,1)}, u32[]{:S(2)}) copy-start(bf16[512,128]{1,0:T(8,128)(2,1)} %index.1) | copy-start | bytes 393220
  66.8 24.2 %copy-start.5 = (bf16[128,128]{1,0:T(8,128)(2,1)S(1)}, bf16[128,128]{1,0:T(8,128)(2,1)}, u32[]{:S(2)}) copy-start(bf16[128,128]{1,0:T(8,128)(2,1)} %get-tuple-element.99.own_rope) | copy-start | bytes 98308

commit v7 on v6

--- a/solution.py
+++ b/solution.py
@@ -41,11 +41,9 @@
     rope_turned,
     index,
     packed,
-    own_rope,
     wide,
     narrow,
     turned,
-    rope,
     table,
     sems,
 ):
@@ -88,10 +86,15 @@
     column = lax.broadcasted_iota(jnp.int32, (total, width), 1)
     pick = (column.astype(f32) == which * rows + start.astype(f32)).astype(bf16)
 
+    tokens = rope_turned.shape[1]
+    row = lax.broadcasted_iota(jnp.int32, (width, tokens), 0)
+    spot = (row // rows) % local_blocks * block + row % rows
+    spot = spot + jnp.where(row < local_blocks * rows, firsts[0], firsts[1])
+    spot = (spot == lax.broadcasted_iota(jnp.int32, (width, tokens), 1)).astype(bf16)
+
     for copy in copies:
         copy.wait()
-    rope_rows = turned[...].astype(f32)
-    rope[...] = jnp.concatenate([rope_rows, rope_rows], axis=0).T.astype(bf16)
+    rope = dot_last(spot, jnp.concatenate([turned[...], turned[...]], axis=0)).astype(bf16)
     parts = []
     for i in range(variants):
         for k in range(local_blocks):
@@ -102,13 +105,12 @@
                         jnp.where(
                             lows[i],
                             narrow[i, k],
-                            rope[pl.ds(pl.multiple_of(k * block + firsts[i], rows), rows), :],
+                            rope[(i * local_blocks + k) * rows : (i * local_blocks + k + 1) * rows],
                         ),
                     ],
                     axis=1,
                 )
             )
-    own_rope[...] = rope[(local_blocks - 1) * block :, :]
     share = jnp.concatenate(parts, axis=0)
     packed[...] = dot(pick, share).astype(bf16)
 
@@ -614,19 +616,15 @@
     in_smem = pl.BlockSpec(memory_space=pltpu.SMEM)
     in_place = pl.BlockSpec(memory_space=pl.ANY)
 
-    packed, own_rope = pl.pallas_call(
+    packed = pl.pallas_call(
         functools.partial(first_kernel, groups),
-        out_shape=(
-            jax.ShapeDtypeStruct((seq_count * rows, lanes), bf16),
-            jax.ShapeDtypeStruct((block, 2 * rope_width), bf16),
-        ),
+        out_shape=jax.ShapeDtypeStruct((seq_count * rows, lanes), bf16),
         in_specs=[in_place] * 4,
-        out_specs=(in_vmem, in_vmem),
+        out_specs=in_vmem,
         scratch_shapes=[
             pltpu.VMEM((2, local_blocks, rows, latent_width), bf16),
             pltpu.VMEM((2, local_blocks, rows, index_width), bf16),
             pltpu.VMEM((rope_width, local_blocks * block), bf16),
-            pltpu.VMEM((local_blocks * block, 2 * rope_width), bf16),
             pltpu.VMEM((slot_count, seq_count), jnp.int32),
             pltpu.SemaphoreType.DMA((6,)),
         ],
@@ -655,6 +653,8 @@
     pieces = pad_lanes(jnp.concatenate([pieces[:, 0], pieces[:, 1]], axis=-1), 128)
     pieces = pieces.reshape(head_count * index_rows // 2, 128)
     height = query_rows + index_rows + index_rows // 2
+    own_rope = rope_keys[(local_blocks - 1) * block :]
+    own_rope = jnp.concatenate([own_rope, own_rope], axis=-1)
     total = slot_count * block
     axes = ("head", "seq")
     *parts, bias, key_bias = pl.pallas_call(

time: 146 us -> 146 us (level)
  no operation moved by 1% of the time
where the time goes in v7:
time: 146 us; the launch traced here: 145 us
  blocking collectives  86.2 us (59%)
  starting transfers between devices  27 us (18%)
  Pallas kernels  14.1 us (10%)
  waiting for transfers between devices  12.7 us (9%)
  local copies, waits for them, and re-layouts  3.08 us (2%)
    all_to_all x5, blocking collectives, exchange(): lax.all_to_all(array, axis, split_axis=0, concat_axis=0, tiled=True, axis...  86.2 us
    all_to_all x1, starting transfers between devices, exchange(): lax.all_to_all(array, axis, split_axis=0, concat_axis=0, tiled=True, axis...  15.5 us
    ppermute x3, starting transfers between devices, body(): parts[k] = lax.ppermute(parts[k], axes, shift_along_u(side, seq_count, k))  11.5 us
    pallas_call x1, Pallas kernels, body(): pl.pallas_call(functools.partial(compute_kernel, loss_weight, index_scale...  9.05 us
    all_to_all x1, waiting for transfers between devices, exchange(): lax.all_to_all(array, axis, split_axis=0, concat_axis=0, tiled=True, axis...  7.89 us
    ppermute x3, waiting for transfers between devices, body(): parts[k] = lax.ppermute(parts[k], axes, shift_along_u(side, seq_count, k))  4.81 us
  transfers between devices with their start and end apart: 4, of which 3 were waited for; matrix products, arithmetic and copies ran while one was open for 2% of the time, Pallas kernels for 0%

profile of v7, /device:TPU:6, one launch (start us, length us, event | category | flops | bytes accessed | tf_op | source)
XLA Modules:
  0.0 144.7 jit_solution(16013728932732344087)
XLA Ops:
  0.6 0.0 copy-start.3
  0.6 0.0 copy-start.4
  0.7 0.0 copy-start.1
  0.7 2.3 %shard_map.103 = bf16[512,384]{1,0:T(8,128)(2,1)} custom-call(s32[16,32]{1,0:T(8,128)} %bitcast.25, bf16[4,128,512]{2,1,0:T(8,128)(2,1)} %bitcast.22, bf16[64,512]{1,0:T(8,128)(2,1)} %bitcast.36, bf16[4,128,128]{2,1,0:T(8,128)(2,1)} %bitcast.24), custom_call_target="tpu_custom_call" | custom-call | tf_op jit(solution)/shard_map/pallas_call | solution.py:619
  3.0 15.5 %all-to-all-start = ((bf16[32,16,384]{2,1,0:T(8,128)(2,1)}), bf16[32,16,384]{2,1,0:T(8,128)(2,1)S(1)}, u32[]{:S(2)}, u32[]{:S(2)}) async-start(bf16[32,16,384]{2,1,0:T(8,128)(2,1)} %bitcast.32), calls=%async_computation | async-start | bytes 786432 | tf_op jit(solution)/shard_map/all_to_all | solution.py:545
  18.5 0.8 copy.30
  19.2 0.1 reshape.129
  19.4 0.2 copy.36
  19.6 1.1 copy.29
  20.7 0.1 pad_maximum_fusion.1.rope
  20.9 0.0 copy-done.3
  20.9 0.0 copy-done.4
  20.9 0.0 copy-done.1
  20.9 0.5 shard_map.104
  21.3 3.5 %collective-permute-start = (bf16[4,112,384]{2,1,0:T(8,128)(2,1)S(1)}, bf16[4,112,384]{2,1,0:T(8,128)(2,1)S(1)}, u32[]{:S(2)}, u32[]{:S(2)}) collective-permute-start(bf16[4,112,384]{2,1,0:T(8,128)(2,1)S(1)} %get-tuple-element.70), channel_id=1, source_target_pairs={{0,32},{128,160},{256,288},{384,416},{32,64},{160,192},{288,320},{... | collective-permute-start | bytes 1032200 | tf_op jit(solution)/shard_map/ppermute | solution.py:672
  24.8 4.8 %collective-permute-start.1 = (bf16[4,112,384]{2,1,0:T(8,128)(2,1)S(1)}, bf16[4,112,384]{2,1,0:T(8,128)(2,1)S(1)}, u32[]{:S(2)}, u32[]{:S(2)}) collective-permute-start(bf16[4,112,384]{2,1,0:T(8,128)(2,1)S(1)} %get-tuple-element.71), channel_id=1, source_target_pairs={{0,64},{128,192},{256,320},{384,448},{32,96},{160,224},{288,352},{... | collective-permute-start | bytes 1032200 | tf_op jit(solution)/shard_map/ppermute | solution.py:672
  29.7 3.3 %collective-permute-start.2 = (bf16[4,112,384]{2,1,0:T(8,128)(2,1)S(1)}, bf16[4,112,384]{2,1,0:T(8,128)(2,1)S(1)}, u32[]{:S(2)}, u32[]{:S(2)}) collective-permute-start(bf16[4,112,384]{2,1,0:T(8,128)(2,1)S(1)} %get-tuple-element.72), channel_id=1, source_target_pairs={{0,96},{128,224},{256,352},{384,480},{32,0},{160,128},{288,256},{4... | collective-permute-start | bytes 1032200 | tf_op jit(solution)/shard_map/ppermute | solution.py:672
  33.0 0.7 slice.44
  33.7 0.1 copy.35
  33.8 0.1 pad_maximum_fusion.2.own_rope
  33.9 0.1 fusion.2
  34.0 0.0 collective-permute-done.in1
  34.0 2.6 %collective-permute-done.1.in2 = bf16[4,112,384]{2,1,0:T(8,128)(2,1)S(1)} collective-permute-done((bf16[4,112,384]{2,1,0:T(8,128)(2,1)S(1)}, bf16[4,112,384]{2,1,0:T(8,128)(2,1)S(1)}, u32[]{:S(2)}, u32[]{:S(2)}) %collective-permute-start.1) | collective-permute-done | bytes 344096 | tf_op jit(solution)/shard_map/ppermute | solution.py:672
  36.6 2.2 %collective-permute-done.2.in3 = bf16[4,112,384]{2,1,0:T(8,128)(2,1)S(1)} collective-permute-done((bf16[4,112,384]{2,1,0:T(8,128)(2,1)S(1)}, bf16[4,112,384]{2,1,0:T(8,128)(2,1)S(1)}, u32[]{:S(2)}, u32[]{:S(2)}) %collective-permute-start.2) | collective-permute-done | bytes 344096 | tf_op jit(solution)/shard_map/ppermute | solution.py:672
  38.8 7.9 %all-to-all-done.fetched = bf16[32,16,384]{2,1,0:T(8,128)(2,1)S(1)} async-done(((bf16[32,16,384]{2,1,0:T(8,128)(2,1)}), bf16[32,16,384]{2,1,0:T(8,128)(2,1)S(1)}, u32[]{:S(2)}, u32[]{:S(2)}) %all-to-all-start) | async-done | bytes 393248 | tf_op jit(solution)/shard_map/all_to_all | solution.py:545
  46.7 0.9 shard_map.105
  47.6 19.1 %all_to_all.30.staged = bf16[4,688,384]{2,1,0:T(8,128)(2,1)S(1)} all-to-all(bf16[4,688,384]{2,1,0:T(8,128)(2,1)S(1)} %shard_map.105), channel_id=1, replica_groups={{0,128,256,384},{32,160,288,416},{64,192,320,448},{96,224,352,480},{1,3..., dimensions={0} | all-to-all | bytes 4227072 | tf_op jit(solution)/shard_map/all_to_all | solution.py:545
  66.6 0.2 shard_map.106
  66.9 0.0 copy-start
  66.9 0.0 copy-start.2
  66.9 24.2 %all_to_all.31.spread_shares = bf16[4,880,384]{2,1,0:T(8,128)(2,1)S(1)} all-to-all(bf16[4,880,384]{2,1,0:T(8,128)(2,1)S(1)} %shard_map.106), channel_id=1, replica_groups={{0,32,64,96},{128,160,192,224},{256,288,320,352},{384,416,448,480},{1,1..., dimensions={0} | all-to-all | bytes 5406720 | tf_op jit(solution)/shard_map/all_to_all | solution.py:545
  91.1 0.0 copy-done
  91.1 0.0 copy-done.2
  91.1 9.1 %shard_map.107 = (bf16[16,32,128]{2,1,0:T(8,128)(2,1)S(1)}, bf16[16,16,128]{2,1,0:T(8,128)(2,1)S(1)}, bf16[16,128,128]{2,1,0:T(8,128)(2,1)S(1)}) custom-call(bf16[4,688,384]{2,1,0:T(8,128)(2,1)S(1)} %all_to_all.30.staged, bf16[4,880,384]{2,1,0:T(8,128)(2,1)S(1)} %all_to_all.31.spread_shares, f32[8,2048]{1,0:T(8,128)S(1)} %get-tuple-element.93.bias, ...), custom_call_target="tpu_custom_call" | custom-call | tf_op jit(solution)/shard_map/pallas_call | solution.py:696
  100.1 13.0 %all_to_all.32.collected = bf16[16,128,128]{2,1,0:T(8,128)(2,1)S(1)} all-to-all(bf16[16,128,128]{2,1,0:T(8,128)(2,1)S(1)} %get-tuple-element.100), channel_id=1, replica_groups=mesh['head'=16,'seq'=32] {'head'}, dimensions={0} | all-to-all | bytes 1048576 | tf_op jit(solution)/shard_map/all_to_all | solution.py:545
  113.1 0.4 shard_map.108
  113.5 17.9 %all_to_all.33 = bf16[32,8,128]{2,1,0:T(8,128)(2,1)S(1)} all-to-all(bf16[32,8,128]{2,1,0:T(8,128)(2,1)S(1)} %bitcast.31), channel_id=1, replica_groups=mesh['head'=16,'seq'=32] {'seq'}, dimensions={0} | all-to-all | bytes 131072 | tf_op jit(solution)/shard_map/all_to_all | solution.py:545
  131.4 0.2 multiply_reduce_fusion
  131.7 12.1 %all_to_all.34.final = bf16[16,80,128]{2,1,0:T(8,128)(2,1)S(1)} all-to-all(bf16[16,80,128]{2,1,0:T(8,128)(2,1)S(1)} %pad_maximum_fusion), channel_id=1, replica_groups=mesh['head'=16,'seq'=32] {'head'}, dimensions={0} | all-to-all | bytes 655360 | tf_op jit(solution)/shard_map/all_to_all | solution.py:545
  143.8 0.9 shard_map.109
  (13 shorter events, 0.2 us)
Async XLA Ops:
  0.6 20.2 %copy-start.3 = (s32[32,16]{0,1:T(8,128)S(1)}, s32[32,16]{0,1:T(8,128)}, u32[]{:S(2)}) copy-start(s32[32,16]{0,1:T(8,128)} %param.17) | copy-start | bytes 6148
  0.6 20.2 %copy-start.4 = (bf16[128,4,128]{2,1,0:T(4,128)(2,1)S(1)}, bf16[128,4,128]{2,1,0:T(4,128)(2,1)}, u32[]{:S(2)}) copy-start(bf16[128,4,128]{2,1,0:T(4,128)(2,1)} %param.14) | copy-start | bytes 393220
  0.7 20.2 %copy-start.1 = (bf16[128,8,512]{2,1,0:T(8,128)(2,1)S(1)}, bf16[128,8,512]{2,1,0:T(8,128)(2,1)}, u32[]{:S(2)}) copy-start(bf16[128,8,512]{2,1,0:T(8,128)(2,1)} %param.10) | copy-start | bytes 3145732
  3.0 43.7 %all-to-all-start = ((bf16[32,16,384]{2,1,0:T(8,128)(2,1)}), bf16[32,16,384]{2,1,0:T(8,128)(2,1)S(1)}, u32[]{:S(2)}, u32[]{:S(2)}) async-start(bf16[32,16,384]{2,1,0:T(8,128)(2,1)} %bitcast.32), calls=%async_computation | async-start | bytes 786432 | tf_op jit(solution)/shard_map/all_to_all | solution.py:545
  21.3 12.6 %collective-permute-start = (bf16[4,112,384]{2,1,0:T(8,128)(2,1)S(1)}, bf16[4,112,384]{2,1,0:T(8,128)(2,1)S(1)}, u32[]{:S(2)}, u32[]{:S(2)}) collective-permute-start(bf16[4,112,384]{2,1,0:T(8,128)(2,1)S(1)} %get-tuple-element.70), channel_id=1, source_target_pairs={{0,32},{128,160},{256,288},{384,416},{32,64},{160,192},{288,320},{... | collective-permute-start | bytes 1032200 | tf_op jit(solution)/shard_map/ppermute | solution.py:672
  24.8 11.8 %collective-permute-start.1 = (bf16[4,112,384]{2,1,0:T(8,128)(2,1)S(1)}, bf16[4,112,384]{2,1,0:T(8,128)(2,1)S(1)}, u32[]{:S(2)}, u32[]{:S(2)}) collective-permute-start(bf16[4,112,384]{2,1,0:T(8,128)(2,1)S(1)} %get-tuple-element.71), channel_id=1, source_target_pairs={{0,64},{128,192},{256,320},{384,448},{32,96},{160,224},{288,352},{... | collective-permute-start | bytes 1032200 | tf_op jit(solution)/shard_map/ppermute | solution.py:672
  29.7 9.1 %collective-permute-start.2 = (bf16[4,112,384]{2,1,0:T(8,128)(2,1)S(1)}, bf16[4,112,384]{2,1,0:T(8,128)(2,1)S(1)}, u32[]{:S(2)}, u32[]{:S(2)}) collective-permute-start(bf16[4,112,384]{2,1,0:T(8,128)(2,1)S(1)} %get-tuple-element.72), channel_id=1, source_target_pairs={{0,96},{128,224},{256,352},{384,480},{32,0},{160,128},{288,256},{4... | collective-permute-start | bytes 1032200 | tf_op jit(solution)/shard_map/ppermute | solution.py:672
  66.9 24.2 %copy-start = (bf16[512,512]{1,0:T(8,128)(2,1)S(1)}, bf16[512,512]{1,0:T(8,128)(2,1)}, u32[]{:S(2)}) copy-start(bf16[512,512]{1,0:T(8,128)(2,1)} %latent.1) | copy-start | bytes 1572868
  66.9 24.2 %copy-start.2 = (bf16[512,128]{1,0:T(8,128)(2,1)S(1)}, bf16[512,128]{1,0:T(8,128)(2,1)}, u32[]{:S(2)}) copy-start(bf16[512,128]{1,0:T(8,128)(2,1)} %index.1) | copy-start | bytes 393220
